TPU v7x, 256 devices: a whole 4x4x8 slice. The times are simulated.
256 devices in a mesh: gx: 16 (over z, core), gy: 4 (over x), gz: 4 (over y).
Axes of the slice: x: 4, y: 4, z: 8, core: 2. Of those that a mesh axis runs over, the one named last changes fastest.
Arguments:
- displacement: float32 [3, 64, 32, 2048], P(None, 'gz', 'gy', 'gx'), may hold values from -4 to 4
- direction: float32 [3, 64, 32, 2048], P(None, 'gz', 'gy', 'gx'), may hold values from -6 to 6
- modulus: float32 [64, 32, 2048], P('gz', 'gy', 'gx'), may hold values from 0.5 to 5
- external: float32 [3, 64, 32, 2048], P(None, 'gz', 'gy', 'gx'), may hold values from -6 to 6
- stiffness: float32 [81, 81], replicated, as said below
- master_record: float32 [27, 524288], P(None, ('gx', 'gy', 'gz')), may hold values from -1 to 1
- pair_face: int32 [262144], P(('gx', 'gy', 'gz')), may hold values from 0 to 188
- pair_owner: int32 [262144, 1], P(('gx', 'gy', 'gz')), may hold values from 0 to 63; in each aligned block of 1024 rows (0 to 1023, 1024 to 2047, ...) at most 32 rows name the same one
- pair_row: int32 [262144], P(('gx', 'gy', 'gz')), may hold values from 0 to 2047
- pair_count: int32 [256], P(('gx', 'gy', 'gz')), may hold values from 1 to 1024, 104857 in all
Outputs:
- residual: float32 [3, 64, 32, 2048], P(None, 'gz', 'gy', 'gx')
- tangent: float32 [3, 64, 32, 2048], P(None, 'gz', 'gy', 'gx')
Inputs may be any that keep to these rules, and one draw needn't show every extreme that they name: `pair_owner`: among the pair slots of one device, at most 32 name the same owner, a bound that the slots of some device reach. `pair_count`: the busiest device has all 1024 slots live; the counts sum to 104857. `stiffness`: symmetric with a dominant positive diagonal.
All inputs are finite; a program needn't handle non-finite values.
Results may differ from a plain program's by a relative error of at most 0.00011.
Values sent between devices are 32-bit elements; how exact they have to be, the bound alone decides.
No kernel may reach another device: no remote copies, remote signals or barrier semaphores. Data moves between devices by JAX's collectives and lax.ppermute only.
A program may use at most 128 MiB of HBM per device.

v0:
```python
import jax
import jax.numpy as jnp
import numpy as np
from jax import lax
from jax.sharding import PartitionSpec as P

BETA_CUBIC = 0.1
PENALTY = 4.0
SMOOTHING = 0.5
HIGHEST = lax.Precision.HIGHEST


def padded_2(cells, sides, width):
    for axis, dim in sides:
        count = lax.axis_size(axis)
        ends = count - 1
        head = lax.slice_in_dim(cells, 0, width, axis=dim)
        tail = lax.slice_in_dim(cells, cells.shape[dim] - width, cells.shape[dim], axis=dim)
        cells = jnp.concatenate(
            [
                lax.ppermute(tail, axis, [(i, (i + 1) % count) for i in range(ends)]),
                cells,
                lax.ppermute(head, axis, [((i + 1) % count, i) for i in range(ends)]),
            ],
            axis=dim,
        )
    return cells


def face_tables():
    points = np.array([-np.sqrt(0.6), 0.0, np.sqrt(0.6)])
    gauss_w = np.array([5.0, 8.0, 5.0]) / 9.0
    line_shape = np.stack(
        [points * (points - 1.0) / 2.0, 1.0 - points * points, points * (points + 1.0) / 2.0],
        axis=1,
    )
    table = (line_shape[:, None, :, None] * line_shape[None, :, None, :]).reshape(9, 9)
    weights = np.outer(gauss_w, gauss_w).reshape(9) * 0.25
    return (jnp.asarray(table, jnp.float32), jnp.asarray(table * weights[:, None], jnp.float32))


def integrate(slave_u, slave_v, record):
    table, weighted = face_tables()
    slots = slave_u.shape[-1]
    u_points = jnp.einsum("qa,acs->qcs", table, slave_u.reshape(9, 3, slots), precision=HIGHEST)
    v_points = jnp.einsum("qa,acs->qcs", table, slave_v.reshape(9, 3, slots), precision=HIGHEST)
    m_points = jnp.einsum("qa,kas->kqs", table, record.reshape(3, 9, slots), precision=HIGHEST)
    gap_value = (
        m_points[0] + m_points[1] * u_points[:, 0] + m_points[2] * u_points[:, 1] + u_points[:, 2]
    )
    scaled = -gap_value / SMOOTHING
    pressure = PENALTY * SMOOTHING * jax.nn.softplus(scaled)
    slope = PENALTY * jax.nn.sigmoid(scaled)
    normal_dot = m_points[1] * v_points[:, 0] + m_points[2] * v_points[:, 1] + v_points[:, 2]
    normal = jnp.stack([m_points[1], m_points[2], jnp.ones_like(m_points[1])], axis=1)
    res_part = -jnp.einsum("qa,qcs->acs", weighted, pressure[:, None] * normal, precision=HIGHEST)
    tan_part = jnp.einsum(
        "qa,qcs->acs", weighted, (slope * normal_dot)[:, None] * normal, precision=HIGHEST
    )
    return (res_part.reshape(27, slots), tan_part.reshape(27, slots))


def weave(first, middle, last, axis):
    count = first.shape[axis]
    lower = [(0, 0)] * first.ndim
    upper = [(0, 0)] * first.ndim
    lower[axis] = (0, 1)
    upper[axis] = (1, 0)
    even = jnp.pad(first, lower) + jnp.pad(last, upper)
    woven = jnp.stack([lax.slice_in_dim(even, 0, count, axis=axis), middle], axis=axis + 1)
    shape = list(first.shape)
    shape[axis] = 2 * count
    woven = woven.reshape(shape)
    return jnp.concatenate([woven, lax.slice_in_dim(even, count, count + 1, axis=axis)], axis=axis)


def element_block(nodes, stiffness, valid):
    za = (nodes.shape[1] - 1) // 2
    yb = (nodes.shape[2] - 1) // 2
    xc = (nodes.shape[3] - 1) // 2
    elems = za * yb * xc
    pieces = []
    for r in range(3):
        for q in range(3):
            for p in range(3):
                pieces.append(
                    nodes[:, r : r + 2 * za : 2, q : q + 2 * yb : 2, p : p + 2 * xc : 2].reshape(
                        7, elems
                    )
                )
    gathered = jnp.stack(pieces, axis=0)
    disp_dofs = gathered[:, 0:3].reshape(81, elems)
    dir_dofs = gathered[:, 3:6].reshape(81, elems)
    coeff = jnp.mean(gathered[:, 6], axis=0) * valid
    both = jnp.dot(stiffness, jnp.concatenate([disp_dofs, dir_dofs], axis=1), precision=HIGHEST)
    force = coeff * (both[:, :elems] + BETA_CUBIC * disp_dofs**3)
    image = coeff * (both[:, elems:] + 3.0 * BETA_CUBIC * disp_dofs * disp_dofs * dir_dofs)
    result = jnp.concatenate(
        [force.reshape(27, 3, elems), image.reshape(27, 3, elems)], axis=1
    ).reshape(3, 3, 3, 6, za, yb, xc)
    along = weave(result[:, :, 0], result[:, :, 1], result[:, :, 2], 5)
    across = weave(along[:, 0], along[:, 1], along[:, 2], 3)
    return weave(across[0], across[1], across[2], 1)


def edge_mask(elems, axis_name_index, axis_size):
    position = jnp.arange(elems + 1, dtype=jnp.int32)
    outside = (position == 0) & (axis_name_index == 0) | (position == elems) & (
        axis_name_index == axis_size - 1
    )
    return jnp.where(outside, 0.0, 1.0).astype(jnp.float32)


def local(
    displacement,
    direction,
    modulus,
    external,
    stiffness,
    master_record,
    pair_face,
    pair_owner,
    pair_row,
    pair_count,
):
    stacked = jnp.concatenate([displacement, direction, modulus[None]], axis=0)
    depth = displacement.shape[1]
    across = displacement.shape[2]
    along_x = displacement.shape[3]
    padded = padded_2(stacked, (("gz", 1), ("gy", 2), ("gx", 3)), 2)
    nodes = padded[:, : depth + 3, : across + 3, : along_x + 3]
    mask_z = edge_mask(depth // 2, lax.axis_index("gz"), lax.axis_size("gz"))
    mask_y = edge_mask(across // 2, lax.axis_index("gy"), lax.axis_size("gy"))
    mask_x = edge_mask(along_x // 2, lax.axis_index("gx"), lax.axis_size("gx"))
    valid = (mask_z[:, None, None] * mask_y[None, :, None] * mask_x[None, None, :]).reshape(-1)
    inner = element_block(nodes, stiffness, valid)[
        :, 2 : 2 + depth, 2 : 2 + across, 2 : 2 + along_x
    ]
    owners = lax.axis_size(("gx", "gy"))
    pairs = pair_face.shape[0]
    capacity = 2 * pairs // owners
    slot_ids = jnp.arange(pairs, dtype=jnp.int32)
    live = slot_ids < pair_count[0]
    target = pair_owner[:, 0]
    hits = (
        (target[None, :] == jnp.arange(owners, dtype=jnp.int32)[:, None]) & live[None, :]
    ).astype(jnp.int32)
    within = jnp.sum(hits * (jnp.cumsum(hits, axis=1) - 1), axis=0)
    flat_slot = jnp.where(live, target * capacity + within, owners * capacity)
    pick_slot = jnp.minimum(flat_slot, owners * capacity - 1)
    request = (
        jnp.full((owners * capacity + 1,), -1, jnp.int32)
        .at[flat_slot]
        .set(pair_row)[: owners * capacity]
        .reshape(owners, 1, capacity)
    )
    face_rows = across // 2 - 1
    face_cols = along_x // 2 - 1
    faces = face_rows * face_cols
    plane = stacked[:6, 0]
    patches = jnp.stack(
        [
            plane[:, b : b + 2 * face_rows : 2, a : a + 2 * face_cols : 2].reshape(6, faces)
            for b in range(3)
            for a in range(3)
        ],
        axis=0,
    )
    patch_table = jnp.concatenate(
        [patches[:, :3].reshape(27, faces), patches[:, 3:].reshape(27, faces)], axis=0
    )
    block_size = min(pairs, 512)
    block_count = pairs // block_size
    face_blocks = pair_face.reshape(block_count, block_size)
    face_ids = jnp.arange(faces, dtype=jnp.int32)

    def pick_faces(ids):
        selector = (face_ids[:, None] == ids[None, :]).astype(jnp.float32)
        return jnp.dot(patch_table, selector, precision=HIGHEST)

    kinematics = lax.map(pick_faces, face_blocks).transpose(1, 0, 2).reshape(54, pairs)
    surface_u = kinematics[:27]
    surface_v = kinematics[27:]
    ids = lax.all_to_all(request, ("gx", "gy"), split_axis=0, concat_axis=0, tiled=True)
    width_k = ids.shape[2]
    flat_ids = ids.reshape(-1)
    found = jnp.take(master_record, jnp.maximum(flat_ids, 0), axis=1)
    found = jnp.where(flat_ids[None, :] >= 0, found, 0.0)
    found, flat_ids, width_k = (found, flat_ids, width_k)
    reply = found.reshape(27, owners, width_k).transpose(1, 0, 2)
    replies = lax.all_to_all(reply, ("gx", "gy"), split_axis=0, concat_axis=0, tiled=True)
    paired = replies.transpose(1, 0, 2).reshape(27, owners * capacity)[:, pick_slot]
    res_part, tan_part = integrate(surface_u, surface_v, paired)
    contact = jnp.concatenate([res_part, tan_part], axis=0)
    contact = jnp.where(live[None, :], contact, 0.0)
    contact_blocks = contact.reshape(54, block_count, block_size).transpose(1, 0, 2)

    def add_faces(carry, pieces):
        ids, values = pieces
        selector = (ids[:, None] == face_ids[None, :]).astype(jnp.float32)
        return (carry + jnp.dot(values, selector, precision=HIGHEST), None)

    face_sums, _ = lax.scan(
        add_faces, jnp.zeros((54, faces), jnp.float32), (face_blocks, contact_blocks)
    )
    face_sums = (
        face_sums.reshape(2, 9, 3, faces)
        .transpose(1, 0, 2, 3)
        .reshape(3, 3, 6, face_rows, face_cols)
    )
    along = weave(face_sums[:, 0], face_sums[:, 1], face_sums[:, 2], 3)
    surface_plane = weave(along[0], along[1], along[2], 1)
    surface = jnp.pad(surface_plane[:, None], ((0, 0), (0, depth - 1), (0, 1), (0, 1)))
    total = inner + surface
    return (total[:3] - external, total[3:])


def solution(mesh):
    placed = (
        P(None, "gz", "gy", "gx"),
        P(None, "gz", "gy", "gx"),
        P("gz", "gy", "gx"),
        P(None, "gz", "gy", "gx"),
        P(),
        P(None, ("gx", "gy", "gz")),
        P(("gx", "gy", "gz")),
        P(("gx", "gy", "gz"), None),
        P(("gx", "gy", "gz")),
        P(("gx", "gy", "gz")),
    )
    return jax.shard_map(
        local,
        mesh=mesh,
        in_specs=placed,
        out_specs=(P(None, "gz", "gy", "gx"), P(None, "gz", "gy", "gx")),
        check_vma=False,
    )
```

profile of v0, /device:TPU:8, one launch (start us, length us, event | category | flops | bytes accessed | tf_op | source)
XLA Modules:
  0.0 627.2 jit_solution(3410735551760649066)
XLA Ops:
  3.7 4.1 collective-permute-start.1
  7.8 1.9 collective-permute-start
  11.1 18.0 %reduce-window.6 = s32[64,8,128]{2,1,0:T(8,128)S(1)} reduce-window(s32[64,8,128]{2,1,0:T(8,128)S(1)} %fusion.31, s32[]{:T(128)} %constant.41.clone.1), window={size=1x1x128 pad=0_0x0_0x127_0}, to_apply=%region_1.2 | reduce-window | flops 8323072 | bytes 524292 | tf_op jit(solution)/shard_map/reduce-window
  29.7 4.5 scatter_custom_fusion
  34.9 11.8 %all-to-all-start = ((s32[64,1,32]{2,1,0:T(1,128)}), s32[64,1,32]{2,1,0:T(1,128)S(1)}, u32[]{:S(2)}, u32[]{:S(2)}) async-start(s32[64,1,32]{2,1,0:T(1,128)} %bitcast.20), calls=%async_computation | async-start | bytes 65536 | tf_op jit(solution)/shard_map/all_to_all | solution.py:184
  46.7 2.2 pad_maximum_fusion.3
  59.3 4.6 collective-permute-start.2
  64.5 6.4 %gather_fusion = f32[2048,27]{1,0:T(8,128)S(1)} fusion(f32[27,2048]{0,1:T(8,128)S(1)} %copy.266, s32[2048]{0:T(1024)} %broadcast_clamp_fusion), kind=kCustom, calls=%fused_computation | custom fusion | bytes 450560 | tf_op jit(solution)/shard_map/jit(_take)/gather | solution.py:187
  74.9 3.5 collective-permute-start.4
  79.8 1.9 reshape.313
  81.7 10.9 %all-to-all-start.1 = ((f32[64,1,864]{2,1,0:T(1,128)}), f32[64,1,864]{2,1,0:T(1,128)}, u32[]{:S(2)}, u32[]{:S(2)}) async-start(f32[64,1,864]{2,1,0:T(1,128)} %reshape.313), calls=%async_computation.1 | async-start | bytes 458752 | tf_op jit(solution)/shard_map/all_to_all | solution.py:191
  93.6 1.9 copy.220
  95.6 2.2 pad_maximum_fusion.4
  97.8 16.7 %slice.290 = f32[7,9,5,65]{3,0,2,1:T(8,128)} slice(f32[7,19,11,131]{3,0,2,1:T(8,128)S(1)} %pad_maximum_fusion.4), slice={[0:7:1], [0:18:2], [0:10:2], [0:130:2]} | slice | bytes 163800 | tf_op jit(solution)/shard_map/slice | solution.py:87
  114.5 16.7 %slice.291 = f32[7,9,5,65]{3,0,2,1:T(8,128)} slice(f32[7,19,11,131]{3,0,2,1:T(8,128)S(1)} %pad_maximum_fusion.4), slice={[0:7:1], [0:18:2], [0:10:2], [1:131:2]} | slice | bytes 163800 | tf_op jit(solution)/shard_map/slice | solution.py:87
  131.2 16.7 %slice.292 = f32[7,9,5,65]{3,0,2,1:T(8,128)} slice(f32[7,19,11,131]{3,0,2,1:T(8,128)S(1)} %pad_maximum_fusion.4), slice={[0:7:1], [0:18:2], [0:10:2], [2:131:2]} | slice | bytes 163800 | tf_op jit(solution)/shard_map/slice | solution.py:87
  147.9 16.7 %slice.293 = f32[7,9,5,65]{3,0,2,1:T(8,128)} slice(f32[7,19,11,131]{3,0,2,1:T(8,128)S(1)} %pad_maximum_fusion.4), slice={[0:7:1], [0:18:2], [1:11:2], [0:130:2]} | slice | bytes 163800 | tf_op jit(solution)/shard_map/slice | solution.py:87
  164.6 16.7 %slice.294 = f32[7,9,5,65]{3,0,2,1:T(8,128)} slice(f32[7,19,11,131]{3,0,2,1:T(8,128)S(1)} %pad_maximum_fusion.4), slice={[0:7:1], [0:18:2], [1:11:2], [1:131:2]} | slice | bytes 163800 | tf_op jit(solution)/shard_map/slice | solution.py:87
  181.3 16.7 %slice.295 = f32[7,9,5,65]{3,0,2,1:T(8,128)} slice(f32[7,19,11,131]{3,0,2,1:T(8,128)S(1)} %pad_maximum_fusion.4), slice={[0:7:1], [0:18:2], [1:11:2], [2:131:2]} | slice | bytes 163800 | tf_op jit(solution)/shard_map/slice | solution.py:87
  198.0 16.7 %slice.296 = f32[7,9,5,65]{3,0,2,1:T(8,128)} slice(f32[7,19,11,131]{3,0,2,1:T(8,128)S(1)} %pad_maximum_fusion.4), slice={[0:7:1], [0:18:2], [2:11:2], [0:130:2]} | slice | bytes 163800 | tf_op jit(solution)/shard_map/slice | solution.py:87
  214.7 16.7 %slice.297 = f32[7,9,5,65]{3,0,2,1:T(8,128)} slice(f32[7,19,11,131]{3,0,2,1:T(8,128)S(1)} %pad_maximum_fusion.4), slice={[0:7:1], [0:18:2], [2:11:2], [1:131:2]} | slice | bytes 163800 | tf_op jit(solution)/shard_map/slice | solution.py:87
  231.4 16.7 %slice.298 = f32[7,9,5,65]{3,0,2,1:T(8,128)} slice(f32[7,19,11,131]{3,0,2,1:T(8,128)S(1)} %pad_maximum_fusion.4), slice={[0:7:1], [0:18:2], [2:11:2], [2:131:2]} | slice | bytes 163800 | tf_op jit(solution)/shard_map/slice | solution.py:87
  248.1 16.7 %slice.299 = f32[7,9,5,65]{3,0,2,1:T(8,128)} slice(f32[7,19,11,131]{3,0,2,1:T(8,128)S(1)} %pad_maximum_fusion.4), slice={[0:7:1], [1:19:2], [0:10:2], [0:130:2]} | slice | bytes 163800 | tf_op jit(solution)/shard_map/slice | solution.py:87
  264.8 16.7 %slice.300 = f32[7,9,5,65]{3,0,2,1:T(8,128)} slice(f32[7,19,11,131]{3,0,2,1:T(8,128)S(1)} %pad_maximum_fusion.4), slice={[0:7:1], [1:19:2], [0:10:2], [1:131:2]} | slice | bytes 163800 | tf_op jit(solution)/shard_map/slice | solution.py:87
  281.5 16.7 %slice.301 = f32[7,9,5,65]{3,0,2,1:T(8,128)} slice(f32[7,19,11,131]{3,0,2,1:T(8,128)S(1)} %pad_maximum_fusion.4), slice={[0:7:1], [1:19:2], [0:10:2], [2:131:2]} | slice | bytes 163800 | tf_op jit(solution)/shard_map/slice | solution.py:87
  298.2 16.7 %slice.302 = f32[7,9,5,65]{3,0,2,1:T(8,128)} slice(f32[7,19,11,131]{3,0,2,1:T(8,128)S(1)} %pad_maximum_fusion.4), slice={[0:7:1], [1:19:2], [1:11:2], [0:130:2]} | slice | bytes 163800 | tf_op jit(solution)/shard_map/slice | solution.py:87
  314.9 16.7 %slice.303 = f32[7,9,5,65]{3,0,2,1:T(8,128)} slice(f32[7,19,11,131]{3,0,2,1:T(8,128)S(1)} %pad_maximum_fusion.4), slice={[0:7:1], [1:19:2], [1:11:2], [1:131:2]} | slice | bytes 163800 | tf_op jit(solution)/shard_map/slice | solution.py:87
  331.6 16.7 %slice.304 = f32[7,9,5,65]{3,0,2,1:T(8,128)} slice(f32[7,19,11,131]{3,0,2,1:T(8,128)S(1)} %pad_maximum_fusion.4), slice={[0:7:1], [1:19:2], [1:11:2], [2:131:2]} | slice | bytes 163800 | tf_op jit(solution)/shard_map/slice | solution.py:87
  348.4 16.7 %slice.305 = f32[7,9,5,65]{3,0,2,1:T(8,128)} slice(f32[7,19,11,131]{3,0,2,1:T(8,128)S(1)} %pad_maximum_fusion.4), slice={[0:7:1], [1:19:2], [2:11:2], [0:130:2]} | slice | bytes 163800 | tf_op jit(solution)/shard_map/slice | solution.py:87
  365.0 16.7 %slice.306 = f32[7,9,5,65]{3,0,2,1:T(8,128)} slice(f32[7,19,11,131]{3,0,2,1:T(8,128)S(1)} %pad_maximum_fusion.4), slice={[0:7:1], [1:19:2], [2:11:2], [1:131:2]} | slice | bytes 163800 | tf_op jit(solution)/shard_map/slice | solution.py:87
  381.8 16.7 %slice.307 = f32[7,9,5,65]{3,0,2,1:T(8,128)} slice(f32[7,19,11,131]{3,0,2,1:T(8,128)S(1)} %pad_maximum_fusion.4), slice={[0:7:1], [1:19:2], [2:11:2], [2:131:2]} | slice | bytes 163800 | tf_op jit(solution)/shard_map/slice | solution.py:87
  398.5 6.6 %slice.308 = f32[7,9,5,65]{3,0,2,1:T(8,128)S(1)} slice(f32[7,19,11,131]{3,0,2,1:T(8,128)S(1)} %pad_maximum_fusion.4), slice={[0:7:1], [2:19:2], [0:10:2], [0:130:2]} | slice | bytes 163800 | tf_op jit(solution)/shard_map/slice | solution.py:87
  405.1 6.6 %slice.309 = f32[7,9,5,65]{3,0,2,1:T(8,128)S(1)} slice(f32[7,19,11,131]{3,0,2,1:T(8,128)S(1)} %pad_maximum_fusion.4), slice={[0:7:1], [2:19:2], [0:10:2], [1:131:2]} | slice | bytes 163800 | tf_op jit(solution)/shard_map/slice | solution.py:87
  411.7 6.6 %slice.310 = f32[7,9,5,65]{3,0,2,1:T(8,128)S(1)} slice(f32[7,19,11,131]{3,0,2,1:T(8,128)S(1)} %pad_maximum_fusion.4), slice={[0:7:1], [2:19:2], [0:10:2], [2:131:2]} | slice | bytes 163800 | tf_op jit(solution)/shard_map/slice | solution.py:87
  418.4 6.6 %slice.311 = f32[7,9,5,65]{3,0,2,1:T(8,128)S(1)} slice(f32[7,19,11,131]{3,0,2,1:T(8,128)S(1)} %pad_maximum_fusion.4), slice={[0:7:1], [2:19:2], [1:11:2], [0:130:2]} | slice | bytes 163800 | tf_op jit(solution)/shard_map/slice | solution.py:87
  425.0 6.6 %slice.312 = f32[7,9,5,65]{3,0,2,1:T(8,128)S(1)} slice(f32[7,19,11,131]{3,0,2,1:T(8,128)S(1)} %pad_maximum_fusion.4), slice={[0:7:1], [2:19:2], [1:11:2], [1:131:2]} | slice | bytes 163800 | tf_op jit(solution)/shard_map/slice | solution.py:87
  431.6 6.6 %slice.313 = f32[7,9,5,65]{3,0,2,1:T(8,128)S(1)} slice(f32[7,19,11,131]{3,0,2,1:T(8,128)S(1)} %pad_maximum_fusion.4), slice={[0:7:1], [2:19:2], [1:11:2], [2:131:2]} | slice | bytes 163800 | tf_op jit(solution)/shard_map/slice | solution.py:87
  438.3 7.2 %slice.314 = f32[7,9,5,65]{3,0,2,1:T(8,128)S(1)} slice(f32[7,19,11,131]{3,0,2,1:T(8,128)S(1)} %pad_maximum_fusion.4), slice={[0:7:1], [2:19:2], [2:11:2], [0:130:2]} | slice | bytes 163800 | tf_op jit(solution)/shard_map/slice | solution.py:87
  445.5 7.2 %slice.315 = f32[7,9,5,65]{3,0,2,1:T(8,128)S(1)} slice(f32[7,19,11,131]{3,0,2,1:T(8,128)S(1)} %pad_maximum_fusion.4), slice={[0:7:1], [2:19:2], [2:11:2], [1:131:2]} | slice | bytes 163800 | tf_op jit(solution)/shard_map/slice | solution.py:87
  452.7 7.2 %slice.316 = f32[7,9,5,65]{3,0,2,1:T(8,128)S(1)} slice(f32[7,19,11,131]{3,0,2,1:T(8,128)S(1)} %pad_maximum_fusion.4), slice={[0:7:1], [2:19:2], [2:11:2], [2:131:2]} | slice | bytes 163800 | tf_op jit(solution)/shard_map/slice | solution.py:87
  492.8 1.5 constant_dynamic-update-slice_fusion.5
  494.3 1.5 constant_dynamic-update-slice_fusion.4
  498.4 4.1 fusion.63
  502.5 2.1 slice_reduce_fusion
  504.6 2.0 reshape.267
  507.1 2.1 convolution_bitcast_fusion.1
  509.2 1.8 fusion.23
  510.9 2.0 concatenate.54
  512.9 1.8 constant_dynamic-update-slice_fusion.28
  514.8 2.0 concatenate.55
  516.8 1.8 constant_dynamic-update-slice_fusion.27
  518.6 4.6 slice_bitcast_fusion.2
  524.3 1.9 add_bitcast_fusion
  526.2 1.7 copy.252
  527.9 4.6 pad_maximum_fusion.2
  532.5 21.3 %copy.251 = f32[3,3,6,9,5,65,2]{3,6,5,4,2,1,0:T(2,128)} copy(f32[3,3,6,9,5,65,2]{5,4,3,2,1,0,6:T(8,128)} %pad_maximum_fusion.2) | data formatting | bytes 2527200 | tf_op jit(solution)/shard_map/stack | solution.py:70
  553.8 22.2 %reshape.268 = f32[3,3,6,9,5,130]{3,5,4,2,1,0:T(8,128)} reshape(f32[3,3,6,9,5,65,2]{3,6,5,4,2,1,0:T(2,128)} %copy.251) | data formatting | bytes 2527200 | tf_op jit(solution)/shard_map/reshape | solution.py:73
  576.0 7.4 %fusion.13 = (f32[3,6,9,5,1,131]{2,5,3,1,0,4:T(8,128)S(1)}, f32[3,6,9,5,131]{2,4,3,1,0:T(8,128)S(1)}, f32[3,6,9,5,131]{2,4,3,1,0:T(8,128)S(1)}) fusion(f32[3,3,6,9,5,1]{3,5,4,2,1,0:T(1,128)S(1)} %copy.252, f32[3,3,6,9,5,130]{3,5,4,2,1,0:T(8,128)} %reshape.268), kind=kLoop, calls=%fused_computation.31 | loop fusion | flops 318330 | bytes 2546640 | tf_op jit(solution)/shard_map/stack;squeeze | solution.py:70
  583.4 3.4 fusion.8
  587.9 8.4 %pad_maximum_fusion = f32[3,6,9,5,2,131]{2,5,3,1,0,4:T(8,128)} fusion(f32[3,6,9,5,1,131]{2,5,3,1,0,4:T(8,128)S(1)} %get-tuple-element.135, f32[3,6,9,5,1,131]{2,5,3,1,0,4:T(8,128)} %fusion.8), kind=kLoop, calls=%fused_computation.20 | loop fusion | flops 212220 | bytes 1697760 | tf_op jit(solution)/shard_map/stack | solution.py:70
  596.3 10.8 %copy.255 = f32[3,6,9,5,2,131]{5,1,4,3,2,0:T(8,128)S(1)} copy(f32[3,6,9,5,2,131]{2,5,3,1,0,4:T(8,128)} %pad_maximum_fusion) | data formatting | bytes 1697760 | tf_op jit(solution)/shard_map/stack | solution.py:70
  607.1 1.6 copy.256
  612.4 2.2 reduce.2
  615.8 2.8 gather_fusion.1
  (319 shorter events, 74.1 us)
Async XLA Ops:
  0.6 506.4 %copy-start = (f32[81,81]{1,0:T(8,128)S(1)}, f32[81,81]{1,0:T(8,128)}, u32[]{:S(2)}) copy-start(f32[81,81]{1,0:T(8,128)} %param.20) | copy-start | bytes 78736
  0.6 46.0 %copy-start.3 = (f32[16,8,128]{2,1,0:T(8,128)S(1)}, f32[16,8,128]{2,1,0:T(8,128)}, u32[]{:S(2)}) copy-start(f32[16,8,128]{2,1,0:T(8,128)} %param.18) | copy-start | bytes 196612
  0.7 28.9 %copy-start.41 = (s32[1024,1]{0,1:T(1,128)S(1)}, s32[1024,1]{0,1:T(1,128)}, u32[]{:S(2)}) copy-start(s32[1024,1]{0,1:T(1,128)} %param.23) | copy-start | bytes 12292
  2.8 46.1 %copy-start.4 = (f32[3,16,8,128]{3,2,1,0:T(8,128)S(1)}, f32[3,16,8,128]{3,2,1,0:T(8,128)}, u32[]{:S(2)}) copy-start(f32[3,16,8,128]{3,2,1,0:T(8,128)} %param.17) | copy-start | bytes 589828
  2.9 46.0 %copy-start.5 = (f32[3,16,8,128]{3,2,1,0:T(8,128)S(1)}, f32[3,16,8,128]{3,2,1,0:T(8,128)}, u32[]{:S(2)}) copy-start(f32[3,16,8,128]{3,2,1,0:T(8,128)} %param.16) | copy-start | bytes 589828
  3.7 54.2 %collective-permute-start.1 = (f32[7,2,8,128]{3,0,2,1:T(8,128)S(1)}, f32[7,2,8,128]{3,0,2,1:T(8,128)S(1)}, u32[]{:S(2)}, u32[]{:S(2)}) collective-permute-start(f32[7,2,8,128]{3,0,2,1:T(8,128)S(1)} %get-tuple-element.153), channel_id=1, source_target_pairs={{1,0},{2,1},{3,2},{5,4},{6,5},{7,6},{9,8},{10,9},{11,10},{13,12},{... | collective-permute-start | bytes 172040 | tf_op jit(solution)/shard_map/ppermute | solution.py:23
  7.8 50.1 %collective-permute-start = (f32[7,2,8,128]{3,0,2,1:T(8,128)S(1)}, f32[7,2,8,128]{3,0,2,1:T(8,128)S(1)}, u32[]{:S(2)}, u32[]{:S(2)}) collective-permute-start(f32[7,2,8,128]{3,0,2,1:T(8,128)S(1)} %get-tuple-element.152), channel_id=1, source_target_pairs={{0,1},{1,2},{2,3},{4,5},{5,6},{6,7},{8,9},{9,10},{10,11},{12,13},{... | collective-permute-start | bytes 172040 | tf_op jit(solution)/shard_map/ppermute | solution.py:21
  11.1 40.4 %copy-start.44 = (s32[1024]{0:T(1024)S(1)}, s32[1024]{0:T(1024)}, u32[]{:S(2)}) copy-start(s32[1024]{0:T(1024)} %param.22) | copy-start | bytes 12292
  34.9 21.9 %all-to-all-start = ((s32[64,1,32]{2,1,0:T(1,128)}), s32[64,1,32]{2,1,0:T(1,128)S(1)}, u32[]{:S(2)}, u32[]{:S(2)}) async-start(s32[64,1,32]{2,1,0:T(1,128)} %bitcast.20), calls=%async_computation | async-start | bytes 65536 | tf_op jit(solution)/shard_map/all_to_all | solution.py:184
  48.9 4.6 copy-start.39
  48.9 7.6 %copy-start.37 = (f32[27,2048]{1,0:T(8,128)S(1)}, f32[27,2048]{1,0:T(8,128)}, u32[]{:S(2)}) copy-start(f32[27,2048]{1,0:T(8,128)} %param.21) | copy-start | bytes 663556
  58.0 12.9 %collective-permute-start.3 = (f32[7,20,2,128]{3,0,2,1:T(8,128)S(1)}, f32[7,20,2,128]{3,0,2,1:T(8,128)S(1)}, u32[]{:S(2)}, u32[]{:S(2)}) collective-permute-start(f32[7,20,2,128]{3,0,2,1:T(8,128)S(1)} %get-tuple-element.151), channel_id=1, source_target_pairs={{4,0},{8,4},{12,8},{5,1},{9,5},{13,9},{6,2},{10,6},{14,10},{7,3},{... | collective-permute-start | bytes 430088 | tf_op jit(solution)/shard_map/ppermute | solution.py:23
  59.3 11.6 %collective-permute-start.2 = (f32[7,20,2,128]{3,0,2,1:T(8,128)S(1)}, f32[7,20,2,128]{3,0,2,1:T(8,128)S(1)}, u32[]{:S(2)}, u32[]{:S(2)}) collective-permute-start(f32[7,20,2,128]{3,0,2,1:T(8,128)S(1)} %get-tuple-element.150), channel_id=1, source_target_pairs={{0,4},{4,8},{8,12},{1,5},{5,9},{9,13},{2,6},{6,10},{10,14},{3,7},{... | collective-permute-start | bytes 430088 | tf_op jit(solution)/shard_map/ppermute | solution.py:21
  72.9 19.8 %collective-permute-start.5 = (f32[7,20,12,2]{1,0,3,2:T(8,128)}, f32[7,20,12,2]{1,0,3,2:T(8,128)S(1)}, u32[]{:S(2)}, u32[]{:S(2)}) collective-permute-start(f32[7,20,12,2]{1,0,3,2:T(8,128)} %copy.219), channel_id=1, source_target_pairs={{16,0},{32,16},{48,32},{64,48},{80,64},{96,80},{112,96},{128,112},... | collective-permute-start | bytes 40328 | tf_op jit(solution)/shard_map/ppermute | solution.py:23
  74.9 18.7 %collective-permute-start.4 = (f32[7,20,12,2]{1,0,3,2:T(8,128)S(1)}, f32[7,20,12,2]{1,0,3,2:T(8,128)S(1)}, u32[]{:S(2)}, u32[]{:S(2)}) collective-permute-start(f32[7,20,12,2]{1,0,3,2:T(8,128)S(1)} %copy.218), channel_id=1, source_target_pairs={{0,16},{16,32},{32,48},{48,64},{64,80},{80,96},{96,112},{112,128},... | collective-permute-start | bytes 40328 | tf_op jit(solution)/shard_map/ppermute | solution.py:21
  81.7 530.1 %all-to-all-start.1 = ((f32[64,1,864]{2,1,0:T(1,128)}), f32[64,1,864]{2,1,0:T(1,128)}, u32[]{:S(2)}, u32[]{:S(2)}) async-start(f32[64,1,864]{2,1,0:T(1,128)} %reshape.313), calls=%async_computation.1 | async-start | bytes 458752 | tf_op jit(solution)/shard_map/all_to_all | solution.py:191
  459.9 4.1 copy-start.20
  460.0 4.9 copy-start.19
  460.0 5.7 copy-start.18
  460.0 6.5 %copy-start.17 = (f32[7,9,5,65]{3,0,2,1:T(8,128)S(1)}, f32[7,9,5,65]{3,0,2,1:T(8,128)}, u32[]{:S(2)}) copy-start(f32[7,9,5,65]{3,0,2,1:T(8,128)} %slice.296) | copy-start | bytes 245704
  461.2 6.2 copy-start.16
  462.8 5.3 copy-start.15
  463.9 5.0 copy-start.14
  464.1 5.7 copy-start.13
  464.9 5.7 copy-start.12
  465.7 5.0 copy-start.11
  466.6 4.4 copy-start.10
  467.4 3.7 copy-start.9
  468.2 3.1 copy-start.8
  469.0 2.5 copy-start.7
  469.8 1.9 copy-start.6
  474.9 6.2 copy-start.21
  475.0 6.8 %copy-start.22 = (f32[1,7,2925]{2,1,0:T(8,128)S(1)}, f32[1,7,2925]{2,1,0:T(8,128)}, u32[]{:S(2)}) copy-start(f32[1,7,2925]{2,1,0:T(8,128)} %stack_reshape.112) | copy-start | bytes 245704
  475.0 7.4 %copy-start.23 = (f32[1,7,2925]{2,1,0:T(8,128)S(1)}, f32[1,7,2925]{2,1,0:T(8,128)}, u32[]{:S(2)}) copy-start(f32[1,7,2925]{2,1,0:T(8,128)} %stack_reshape.113) | copy-start | bytes 245704
  475.7 7.3 %copy-start.24 = (f32[1,7,2925]{2,1,0:T(8,128)S(1)}, f32[1,7,2925]{2,1,0:T(8,128)}, u32[]{:S(2)}) copy-start(f32[1,7,2925]{2,1,0:T(8,128)} %stack_reshape.114) | copy-start | bytes 245704
  475.7 8.0 %copy-start.25 = (f32[1,7,2925]{2,1,0:T(8,128)S(1)}, f32[1,7,2925]{2,1,0:T(8,128)}, u32[]{:S(2)}) copy-start(f32[1,7,2925]{2,1,0:T(8,128)} %stack_reshape.115) | copy-start | bytes 245704
  475.8 8.6 %copy-start.26 = (f32[1,7,2925]{2,1,0:T(8,128)S(1)}, f32[1,7,2925]{2,1,0:T(8,128)}, u32[]{:S(2)}) copy-start(f32[1,7,2925]{2,1,0:T(8,128)} %stack_reshape.116) | copy-start | bytes 245704
  475.8 9.2 %copy-start.27 = (f32[1,7,2925]{2,1,0:T(8,128)S(1)}, f32[1,7,2925]{2,1,0:T(8,128)}, u32[]{:S(2)}) copy-start(f32[1,7,2925]{2,1,0:T(8,128)} %stack_reshape.117) | copy-start | bytes 245704
  475.8 9.8 %copy-start.28 = (f32[1,7,2925]{2,1,0:T(8,128)S(1)}, f32[1,7,2925]{2,1,0:T(8,128)}, u32[]{:S(2)}) copy-start(f32[1,7,2925]{2,1,0:T(8,128)} %stack_reshape.118) | copy-start | bytes 245704
  477.4 12.7 %copy-start.29 = (f32[1,7,2925]{2,1,0:T(8,128)S(1)}, f32[1,7,2925]{2,1,0:T(8,128)}, u32[]{:S(2)}) copy-start(f32[1,7,2925]{2,1,0:T(8,128)} %stack_reshape.125) | copy-start | bytes 245704
  477.4 13.4 %copy-start.30 = (f32[1,7,2925]{2,1,0:T(8,128)S(1)}, f32[1,7,2925]{2,1,0:T(8,128)}, u32[]{:S(2)}) copy-start(f32[1,7,2925]{2,1,0:T(8,128)} %stack_reshape.126) | copy-start | bytes 245704
  478.2 13.3 %copy-start.31 = (f32[1,7,2925]{2,1,0:T(8,128)S(1)}, f32[1,7,2925]{2,1,0:T(8,128)}, u32[]{:S(2)}) copy-start(f32[1,7,2925]{2,1,0:T(8,128)} %stack_reshape.127) | copy-start | bytes 245704
  478.2 13.9 %copy-start.32 = (f32[1,7,2925]{2,1,0:T(8,128)S(1)}, f32[1,7,2925]{2,1,0:T(8,128)}, u32[]{:S(2)}) copy-start(f32[1,7,2925]{2,1,0:T(8,128)} %stack_reshape.128) | copy-start | bytes 245704
  479.0 16.8 %copy-start.33 = (f32[1,7,2925]{2,1,0:T(8,128)S(1)}, f32[1,7,2925]{2,1,0:T(8,128)}, u32[]{:S(2)}) copy-start(f32[1,7,2925]{2,1,0:T(8,128)} %stack_reshape.131) | copy-start | bytes 245704
  479.1 17.4 %copy-start.34 = (f32[1,7,2925]{2,1,0:T(8,128)S(1)}, f32[1,7,2925]{2,1,0:T(8,128)}, u32[]{:S(2)}) copy-start(f32[1,7,2925]{2,1,0:T(8,128)} %stack_reshape.132) | copy-start | bytes 245704
  479.8 17.3 %copy-start.35 = (f32[1,7,2925]{2,1,0:T(8,128)S(1)}, f32[1,7,2925]{2,1,0:T(8,128)}, u32[]{:S(2)}) copy-start(f32[1,7,2925]{2,1,0:T(8,128)} %stack_reshape.133) | copy-start | bytes 245704
  479.8 17.9 %copy-start.36 = (f32[1,7,2925]{2,1,0:T(8,128)S(1)}, f32[1,7,2925]{2,1,0:T(8,128)}, u32[]{:S(2)}) copy-start(f32[1,7,2925]{2,1,0:T(8,128)} %stack_reshape.134) | copy-start | bytes 245704
  596.3 10.8 %copy-start.2 = (f32[3,6,9,1,131]{2,4,3,1,0:T(8,128)S(1)}, f32[3,6,9,1,131]{2,4,3,1,0:T(8,128)}, u32[]{:S(2)}) copy-start(f32[3,6,9,1,131]{2,4,3,1,0:T(8,128)} %pad_add_fusion.1) | copy-start | bytes 254668
  614.5 6.6 %copy-start.42 = (f32[9,9,1]{0,1,2:T(8,128)S(1)}, f32[9,9,1]{0,1,2:T(8,128)}, u32[]{:S(2)}) copy-start(f32[9,9,1]{0,1,2:T(8,128)} %constant.137) | copy-start | bytes 976
  618.7 3.6 copy-start.43
  618.7 3.7 copy-start.40
  623.5 1.9 copy-start.38
  623.9 3.0 copy-start.1
where the time goes:
time: 638 us; the launch traced here: 627 us
  local copies, waits for them, and re-layouts  513 us (80%)
  other arithmetic  65.4 us (10%)
  starting transfers between devices  39.3 us (6%)
    slice x54, local copies, waits for them, and re-layouts, element_block(): nodes[:, r:r + 2 * za:2, q:q + 2 * yb:2, p:p + 2 * xc:2].reshape(7, elems)  366 us
    another operation x5, local copies, waits for them, and re-layouts, weave(): jnp.stack([lax.slice_in_dim(even, 0, count, axis=axis), middle], axis=axi...  33.1 us
    unnamed x132, local copies, waits for them, and re-layouts  27.7 us
    another operation x12, other arithmetic, weave(): jnp.stack([lax.slice_in_dim(even, 0, count, axis=axis), middle], axis=axi...  26.2 us
    reshape x5, local copies, waits for them, and re-layouts, weave(): woven = woven.reshape(shape)  23.7 us
    another operation x2, other arithmetic  18 us
    another operation x28, local copies, waits for them, and re-layouts, element_block(): gathered = jnp.stack(pieces, axis=0)  15.1 us
  transfers between devices with their start and end apart: 8, of which 0 were waited for; matrix products, arithmetic and copies ran while one was open for 90% of the time, Pallas kernels for 0%

commit v1 on v0

v1 whole, which is shorter than its diff:
```python
import jax
import jax.numpy as jnp
import numpy as np
from jax import lax
from jax.experimental import pallas as pl
from jax.experimental.pallas import tpu as pltpu
from jax.sharding import PartitionSpec as P

F32 = jnp.float32
BF16 = jnp.bfloat16
I32 = jnp.int32

ZN, YN, XN = 16, 8, 128
ZE, YE = ZN + 3, YN + 3
OWNERS, CAP, PAIRS, ROWS = 64, 32, 1024, 2048
CHUNKS = OWNERS * CAP // 128
FACE_ROWS, FACE_COLS, FACE_LANES = 3, 63, 64
FACES = FACE_ROWS * FACE_LANES
SLABS = 28
TILE = 16
YPITCH = TILE
ZPITCH = YE * TILE
NODE_ROWS = ZE * ZPITCH
BLOCK = 9 * TILE
GROUPS = ("gx", "gy")


def shapes_1d():
    points = np.array([-np.sqrt(0.6), 0.0, np.sqrt(0.6)])
    gauss = np.array([5.0, 8.0, 5.0]) / 9.0
    line = np.stack(
        [points * (points - 1.0) / 2.0, 1.0 - points * points, points * (points + 1.0) / 2.0],
        axis=1,
    )
    return line, gauss


def halves(values):
    high = np.asarray(values, np.float32).astype(jnp.bfloat16)
    low = (np.asarray(values, np.float64) - high.astype(np.float64)).astype(jnp.bfloat16)
    return high, low


def record_map():
    line, _ = shapes_1d()
    out = np.zeros((32, 27))
    for k in range(3):
        for qy in range(3):
            for qx in range(3):
                q = 3 * qy + qx
                row = k * 8 + q if q < 8 else 24 + k
                for b in range(3):
                    for a in range(3):
                        out[row, 9 * k + 3 * b + a] = line[qy, b] * line[qx, a]
    return halves(out)


def quad_row(part, q):
    return part * 8 + q if q < 8 else 48 + part


def face_x_map():
    line, _ = shapes_1d()
    out = np.zeros((128, 6 * 128))
    for qx in range(3):
        for side in range(2):
            for fx in range(FACE_COLS):
                for a in range(3):
                    out[2 * fx + a, (2 * qx + side) * 128 + side * 64 + fx] = line[qx, a]
    return halves(out)


def face_y_map():
    line, _ = shapes_1d()
    first = np.zeros((56, 6 * 48))
    second = np.zeros((56, 6 * 48))
    for part in range(6):
        for qy in range(3):
            for qx in range(3):
                row = quad_row(part, 3 * qy + qx)
                for b in range(3):
                    first[row, (2 * qx) * 48 + part * 8 + b] = line[qy, b]
                    first[row, (2 * qx + 1) * 48 + part * 8 + 2 + b] = line[qy, b]
                    second[row, (2 * qx) * 48 + part * 8 + 4 + b] = line[qy, b]
    return halves(first), halves(second)


def node_x_map():
    line, _ = shapes_1d()
    out = np.zeros((FACE_LANES, 3 * 128))
    for qx in range(3):
        for fx in range(FACE_COLS):
            for a in range(3):
                out[fx, qx * 128 + 2 * fx + a] = line[qx, a]
    return halves(out)


def node_y_map():
    line, gauss = shapes_1d()
    out = np.zeros((48, 3 * FACE_ROWS * 64))
    for part in range(6):
        for qx in range(3):
            for qy in range(3):
                weight = 0.25 * gauss[qx] * gauss[qy] * (-1.0 if part < 3 else 1.0)
                for fy in range(FACE_ROWS):
                    for b in range(3):
                        column = qx * FACE_ROWS * 64 + fy * 64 + quad_row(part, 3 * qy + qx)
                        out[part * 8 + 2 * fy + b, column] = weight * line[qy, b]
    return halves(out)


def stiffness_places():
    place = np.zeros((BLOCK, 81))
    for block in range(9):
        for p in range(3):
            for c in range(3):
                place[block * TILE + 3 * p + c, block * 9 + 3 * p + c] = 1.0
    fixed = np.zeros((BLOCK, BLOCK))
    for block in range(9):
        fixed[block * TILE + 9, block * TILE + 12] = 1.0
        for p in range(3):
            fixed[10, block * TILE + 9 + p] = 1.0 / 27.0
    fixed[[b * TILE + 9 for b in range(1, 9)], :] = 0.0
    for block in range(1, 9):
        fixed[block * TILE + 9, block * TILE + 12] = 1.0
    return place.astype(np.float32), halves(fixed)


def split(values):
    high = values.astype(BF16)
    return high, (values - high.astype(F32)).astype(BF16)


def mm(a, b):
    return jnp.dot(a, b, preferred_element_type=F32)


def mm_nt(a, b):
    return lax.dot_general(a, b, (((1,), (1,)), ((), ())), preferred_element_type=F32)


def mm3(a, b):
    return mm(a[0], b[0]) + (mm(a[0], b[1]) + mm(a[1], b[0]))


def lane_ids(rows):
    return lax.broadcasted_iota(I32, (rows, 128), 1)


def pick_lanes(values, index):
    return jnp.take_along_axis(values, index, axis=1, mode="promise_in_bounds")


def compact(values):
    return (
        values[0:16]
        + pltpu.roll(values[16:32], 32, 1)
        + pltpu.roll(values[32:48], 64, 1)
        + pltpu.roll(values[48:64], 96, 1)
    )


def swap_groups(parts):
    group = lane_ids(8) // 32
    out = []
    for f in range(4):
        total = None
        for g in range(4):
            moved = parts[g] if f == g else pltpu.roll(parts[g], (32 * (g - f)) % 128, 1)
            total = moved if total is None else jnp.where(group == g, moved, total)
        out.append(total)
    return out


def request_kernel(owner, row, face, count, u, v, m, request, faces, z_up, z_down):
    for first, field, comps in ((0, u, 3), (3, v, 3), (6, m, 1)):
        for c in range(comps):
            z_up[first + c] = field[pl.ds((c * ZN + ZN - 2) * YN, 2 * YN), :]
            z_down[first + c] = field[pl.ds(c * ZN * YN, YN), :]
    live_count = count[0]
    who = lax.broadcasted_iota(I32, (OWNERS, 128), 0)
    lane = lane_ids(1)
    hits = []
    for t in range(PAIRS // 128):
        live = lane + t * 128 < live_count
        target = jnp.where(live, owner[pl.ds(t, 1), :], -1)
        hits.append(jnp.where(who == target, 1.0, 0.0).astype(F32))
    before = jnp.where(
        lax.broadcasted_iota(I32, (128, 128), 0) < lax.broadcasted_iota(I32, (128, 128), 1), 1.0, 0.0
    ).astype(BF16)
    ranks = mm(jnp.concatenate([h.astype(BF16) for h in hits], axis=0), before)
    base = jnp.zeros((OWNERS, 1), F32)
    places = lax.broadcasted_iota(I32, (128, 128), 0)
    highs, lows, sides = [], [], []
    for t in range(PAIRS // 128):
        rank = jnp.sum(hits[t] * (ranks[t * OWNERS : (t + 1) * OWNERS] + base), axis=0, keepdims=True)
        base = base + jnp.sum(hits[t], axis=1, keepdims=True)
        here = places == rank.astype(I32)
        number = row[pl.ds(t, 1), :] + 1
        f = face[pl.ds(t, 1), :]
        f = f + jnp.where(f >= FACE_COLS, 1, 0) + jnp.where(f >= 2 * FACE_COLS, 1, 0) + 1
        highs.append(jnp.where(here, lax.shift_right_logical(number, 6).astype(F32), 0.0).astype(BF16))
        lows.append(jnp.where(here, (number & 63).astype(F32), 0.0).astype(BF16))
        sides.append(jnp.where(here, f.astype(F32), 0.0).astype(BF16))
    hit = jnp.concatenate([h.astype(BF16) for h in hits], axis=1)
    high = mm_nt(hit, jnp.concatenate(highs, axis=1))
    low = mm_nt(hit, jnp.concatenate(lows, axis=1))
    request[...] = (high * 64.0 + low).astype(I32)
    faces[...] = compact(mm_nt(hit, jnp.concatenate(sides, axis=1))).astype(I32)


def prepare_kernel(
    u, v, m, z_low, z_high, stiffness, master, place, fixed_h, fixed_l, record_h, record_l,
    face_x_h, face_x_l, first_h, first_l, second_h, second_l,
    y_up, y_down, big_h, big_l, table, quads,
):
    for first, field, comps in ((0, u, 3), (3, v, 3), (6, m, 1)):
        for c in range(comps):
            n = first + c
            for out, h, y in ((y_up, 0, YN - 2), (y_up, 1, YN - 1), (y_down, 0, 0)):
                at = (n * (2 if out is y_up else 1) + h) * 24
                out[pl.ds(at, ZN), :] = field[pl.ds(c * ZN * YN + y, ZN, stride=YN), :]
                out[pl.ds(at + 16, 8), :] = jnp.zeros((8, 128), F32)
                out[pl.ds(at + 16, 1), :] = z_low[pl.ds((n * 2) * YN + y, 1), :]
                out[pl.ds(at + 17, 1), :] = z_low[pl.ds((n * 2 + 1) * YN + y, 1), :]
                out[pl.ds(at + 18, 1), :] = z_high[pl.ds(n * YN + y, 1), :]
    places = place[...]
    spread = jnp.dot(places, stiffness[...], precision=lax.Precision.HIGHEST, preferred_element_type=F32)
    spread = lax.dot_general(
        spread, places, (((1,), (1,)), ((), ())), precision=lax.Precision.HIGHEST, preferred_element_type=F32
    )
    high, low = split(spread)
    big_h[...] = high + fixed_h[...]
    big_l[...] = low + fixed_l[...]
    table[...] = mm3((record_h[...], record_l[...]), split(master[...]))
    plane = jnp.concatenate(
        [field[pl.ds(c * ZN * YN, YN), :] for field in (u, v) for c in range(3)], axis=0
    )
    wide = mm3(split(plane), (face_x_h[...], face_x_l[...]))
    tall = split(jnp.concatenate([wide[:, i * 128 : (i + 1) * 128] for i in range(6)], axis=0))
    quads[:, 0:128] = mm3((first_h[...], first_l[...]), tall)
    quads[:, 128:256] = mm3((second_h[...], second_l[...]), tall)


def gather_kernel(ids, table, reply):
    numbers = jnp.maximum(compact(ids[...]) - 1, 0)
    for c in range(CHUNKS):
        number = jnp.broadcast_to(numbers[c : c + 1], (8, 128))
        inside = number & 127
        outside = lax.shift_right_logical(number, 7)
        found = []
        for f in range(4):
            total = pick_lanes(table[pl.ds(f * 8, 8), 0:128], inside)
            for k in range(1, ROWS // 128):
                piece = pick_lanes(table[pl.ds(f * 8, 8), k * 128 : (k + 1) * 128], inside)
                total = jnp.where(outside == k, piece, total)
            found.append(total)
        for g, tile in enumerate(swap_groups(found)):
            reply[g * CHUNKS + c] = tile


def slabs_of(u, v, m, z_low, z_high, y_low, y_high):
    for first, field, comps in ((0, u, 3), (3, v, 3), (6, m, 1)):
        for c in range(comps):
            n = first + c
            for s in range(SLABS):
                if s < 16:
                    tile = field[pl.ds((c * ZN + s) * YN, YN), :]
                elif s < 18:
                    tile = z_low[pl.ds((n * 2 + s - 16) * YN, YN), :]
                elif s < 19:
                    tile = z_high[pl.ds(n * YN, YN), :]
                else:
                    h, zb = divmod(s - 19, 3)
                    if h < 2:
                        tile = y_low[pl.ds((n * 2 + h) * 24 + zb * 8, 8), :]
                    else:
                        tile = y_high[pl.ds(n * 24 + zb * 8, 8), :]
                yield n, s, tile


def edge_kernel(u, v, m, z_low, z_high, y_low, y_high, x_up, x_down):
    lane = lane_ids(8)
    up = [jnp.zeros((8, 128), F32) for _ in range(4)]
    down = [jnp.zeros((8, 128), F32) for _ in range(2)]
    for n, s, tile in slabs_of(u, v, m, z_low, z_high, y_low, y_high):
        i = n * SLABS + s
        k, spot = i // 64, i % 64
        moved = pltpu.roll(tile, (2 * spot - 126) % 128, 1)
        up[k] = jnp.where(lax.shift_right_logical(lane, 1) == spot, moved, up[k])
        k, spot = i // 128, i % 128
        moved = tile if spot == 0 else pltpu.roll(tile, spot, 1)
        down[k] = jnp.where(lane == spot, moved, down[k])
    for k in range(4):
        x_up[pl.ds(k * 8, 8), :] = up[k]
    for k in range(2):
        x_down[pl.ds(k * 8, 8), :] = down[k]


def element_kernel(
    edges, u, v, m, external, z_low, z_high, y_low, y_high, x_low, x_high, big_h, big_l,
    residual, tangent, nodes_u, nodes_v, tiles_h, tiles_l, total_u, total_v,
):
    lane = lane_ids(8)
    even = jnp.maximum(2 * (lane - 1), 0) & 127
    odd = jnp.maximum(2 * (lane - 1) + 1, 0) & 127
    after = (2 * lane) & 127
    for n, s, tile in slabs_of(u, v, m, z_low, z_high, y_low, y_high):
        i = n * SLABS + s
        k, spot = i // 64, i % 64
        left = x_low[pl.ds(k * 8, 8), :]
        k2, spot2 = i // 128, i % 128
        right = x_high[pl.ds(k2 * 8, 8), :]
        first = left if spot == 0 else pltpu.roll(left, (-2 * spot) % 128, 1)
        second = pltpu.roll(left, (-2 * spot - 1) % 128, 1)
        third = right if spot2 == 64 else pltpu.roll(right, (64 - spot2) % 128, 1)
        values = (
            jnp.where(lane == 0, first, pick_lanes(tile, even)),
            jnp.where(lane == 0, second, pick_lanes(tile, odd)),
            jnp.where(lane == 64, third, pick_lanes(tile, after)),
        )
        to = nodes_v if 3 <= n < 6 else nodes_u
        for p, value in enumerate(values):
            at = 9 + p if n == 6 else 3 * p + n % 3
            if s < 19:
                z = s + 2 if s < 16 else (0, 1, 18)[s - 16]
                to[pl.ds(z * ZPITCH + 2 * YPITCH + at, 8, stride=YPITCH), :] = value
            else:
                h, zb = divmod(s - 19, 3)
                base = (0, 1, 10)[h] * YPITCH + at
                if zb < 2:
                    to[pl.ds((2 + zb * 8) * ZPITCH + base, 8, stride=ZPITCH), :] = value
                else:
                    to[pl.ds(base, 1), :] = value[0:1]
                    to[pl.ds(ZPITCH + base, 1), :] = value[1:2]
                    to[pl.ds(18 * ZPITCH + base, 1), :] = value[2:3]

    sub = lax.broadcasted_iota(I32, (TILE, 128), 0)
    one = jnp.where(sub == 12, 1.0, 0.0)

    def halve(z, carry):
        for y in range(YE):
            at = pl.multiple_of(z * ZPITCH + y * YPITCH, TILE)
            for first, source, last, total in ((0, nodes_u, 12, total_u), (128, nodes_v, 9, total_v)):
                value = jnp.where(sub < last, source[pl.ds(at, TILE), :], one)
                high, low = split(value)
                tiles_h[pl.ds(at, TILE), first : first + 128] = high
                tiles_l[pl.ds(at, TILE), first : first + 128] = low
                total[pl.ds(at, TILE), :] = jnp.zeros((TILE, 128), F32)
        return carry

    lax.fori_loop(0, ZE, halve, 0)

    lane_1 = lane_ids(1)
    x_first = jnp.where((edges[2] == 0), 1, 0)
    x_last = jnp.where((edges[2] == lax.axis_size("gx") - 1), 63, 64)
    inside_x = jnp.where((lane_1 >= x_first) & (lane_1 <= x_last), 1.0, 0.0)
    y_first = jnp.where(edges[1] == 0, 1, 0)
    y_last = jnp.where(edges[1] == lax.axis_size("gy") - 1, 3, 4)
    z_first = jnp.where(edges[0] == 0, 1, 0)
    z_last = jnp.where(edges[0] == lax.axis_size("gz") - 1, 7, 8)
    left_high, left_low = big_h[...], big_l[...]

    def layer(k, carry):
        inside_z = (k >= z_first) & (k <= z_last)
        for j in range(5):
            starts = [pl.multiple_of((2 * k + r) * ZPITCH + 2 * j * YPITCH, TILE) for r in range(3)]
            high = jnp.concatenate([tiles_h[pl.ds(s, 3 * TILE), :] for s in starts], axis=0)
            low = jnp.concatenate([tiles_l[pl.ds(s, 3 * TILE), :] for s in starts], axis=0)
            both = mm3((left_high, left_low), (high, low))
            inside = inside_z & (j >= y_first) & (j <= y_last)
            coeff = jnp.where(inside, both[10:11, 0:128] * inside_x, 0.0)
            for r in range(3):
                part = slice(r * 3 * TILE, (r + 1) * 3 * TILE)
                total_u[pl.ds(starts[r], 3 * TILE), :] += both[part, 0:128] * coeff
                total_v[pl.ds(starts[r], 3 * TILE), :] += both[part, 128:256] * coeff
        return carry

    lax.fori_loop(0, 9, layer, 0)

    weave = jnp.where((lane & 1) == 0, 0, 64) + lax.shift_right_logical(lane, 1)
    low_half = lane < 64

    def finish(z, carry):
        at = (z + 2) * ZPITCH + 2 * YPITCH

        def rows(total, row):
            return total[pl.ds(at + row, 8, stride=YPITCH), :]

        def woven(e, o):
            return pick_lanes(jnp.where(low_half, e, pltpu.roll(o, 63, 1)), weave)

        held = rows(total_u, 9)
        mass = woven(pltpu.roll(held, 127, 1) + held, held)
        for c in range(3):
            where = pl.ds(pl.multiple_of((c * ZN + z) * YN, YN), YN)
            uu, vv = u[where, :], v[where, :]
            inner, image = (
                woven(pltpu.roll(rows(t, c), 127, 1) + rows(t, 6 + c), rows(t, 3 + c))
                for t in (total_u, total_v)
            )
            square = uu * uu * mass
            residual[where, :] = inner + 0.1 * square * uu - external[where, :]
            tangent[where, :] = image + 0.3 * square * vv
        return carry

    lax.fori_loop(0, ZN, finish, 0)


def contact_kernel(
    replies, quads, faces, node_x_h, node_x_l, node_y_h, node_y_l, res_in, tan_in, residual, tangent
):
    slot_faces = faces[...]
    face_ids = lax.broadcasted_iota(I32, (FACES, 128), 0) + 1
    values_h, values_l, selectors = [], [], []
    for c in range(CHUNKS):
        m = swap_groups([replies[g * CHUNKS + c] for g in range(4)])
        slot_face = slot_faces[c : c + 1]
        index = jnp.maximum(jnp.broadcast_to(slot_face, (8, 128)) - 1, 0)
        inside, outside = index & 127, index >= 128
        kin = [
            jnp.where(
                outside,
                pick_lanes(quads[pl.ds(i * 8, 8), 128:256], inside),
                pick_lanes(quads[pl.ds(i * 8, 8), 0:128], inside),
            )
            for i in range(7)
        ]

        def point(m0, m1, m2, k):
            gap = m0 + m1 * k[0] + m2 * k[1] + k[2]
            scaled = -2.0 * gap
            small = jnp.exp(-jnp.abs(scaled))
            pressure = 2.0 * (jnp.maximum(scaled, 0.0) + jnp.log1p(small))
            slope = 4.0 * jnp.where(scaled >= 0.0, 1.0, small) / (1.0 + small)
            push = slope * (m1 * k[3] + m2 * k[4] + k[5])
            return pressure * m1, pressure * m2, pressure, push * m1, push * m2, push

        main = point(m[0], m[1], m[2], kin[:6])
        last = point(m[3][0:1], m[3][1:2], m[3][2:3], [kin[6][i : i + 1] for i in range(6)])
        stack = jnp.concatenate(list(main) + list(last) + [jnp.zeros((10, 128), F32)], axis=0)
        high, low = split(stack)
        values_h.append(high)
        values_l.append(low)
        selectors.append(jnp.where(face_ids == slot_face, 1.0, 0.0).astype(BF16))
    values = jnp.concatenate(
        [jnp.concatenate(values_h, axis=1), jnp.concatenate(values_l, axis=1)], axis=0
    )
    sums = mm_nt(values, jnp.concatenate(selectors, axis=1))
    sums = sums[0:64] + sums[64:128]
    sums = jnp.concatenate([sums[:, 0:64], sums[:, 64:128], sums[:, 128:192]], axis=0)
    along = mm3(split(sums), (node_x_h[...], node_x_l[...]))
    tall = split(jnp.concatenate([along[:, i * 128 : (i + 1) * 128] for i in range(3)], axis=0))
    plane = mm3((node_y_h[...], node_y_l[...]), tall)
    for c in range(3):
        residual[c, 0] = res_in[c, 0] + plane[c * 8 : c * 8 + 8]
        tangent[c, 0] = tan_in[c, 0] + plane[24 + c * 8 : 32 + c * 8]


def call(body, outs, scratch=(), smem=(), flops=0, n=0, **more):
    specs = [
        pl.BlockSpec(memory_space=pltpu.SMEM if i in smem else pltpu.VMEM) for i in range(n)
    ]
    return pl.pallas_call(
        body,
        out_shape=tuple(jax.ShapeDtypeStruct(s, t) for s, t in outs),
        in_specs=specs,
        out_specs=tuple(pl.BlockSpec(memory_space=pltpu.VMEM) for _ in outs),
        scratch_shapes=list(scratch),
        cost_estimate=pl.CostEstimate(flops=flops, bytes_accessed=1 << 20, transcendentals=0),
        compiler_params=pltpu.CompilerParams(vmem_limit_bytes=44 << 20),
        **more,
    )


def ring(values, axis, up):
    count = lax.axis_size(axis)
    pairs = [(i, (i + 1) % count) if up else ((i + 1) % count, i) for i in range(count)]
    return lax.ppermute(values, axis, pairs)


def local(
    displacement,
    direction,
    modulus,
    external,
    stiffness,
    master_record,
    pair_face,
    pair_owner,
    pair_row,
    pair_count,
):
    u = displacement.reshape(3 * ZN * YN, XN)
    v = direction.reshape(3 * ZN * YN, XN)
    m = modulus.reshape(ZN * YN, XN)
    request, faces, z_up, z_down = call(
        request_kernel,
        [((OWNERS, 128), I32), ((CHUNKS, 128), I32), ((7, 2 * YN, XN), F32), ((7, YN, XN), F32)],
        smem=(3,), n=7, flops=1 << 20,
    )(pair_owner.reshape(8, 128), pair_row.reshape(8, 128), pair_face.reshape(8, 128), pair_count, u, v, m)
    z_low = ring(z_up, "gz", True).reshape(7 * 2 * YN, XN)
    z_high = ring(z_down, "gz", False).reshape(7 * YN, XN)
    ids = lax.all_to_all(request, GROUPS, split_axis=0, concat_axis=0, tiled=True)

    place, fixed = stiffness_places()
    first, second = face_y_map()
    constants = [jnp.asarray(x) for x in (place, *fixed, *record_map(), *face_x_map(), *first, *second)]
    y_up, y_down, big_h, big_l, table, quads = call(
        prepare_kernel,
        [
            ((7 * 2 * 24, XN), F32), ((7 * 24, XN), F32), ((BLOCK, BLOCK), BF16), ((BLOCK, BLOCK), BF16),
            ((32, ROWS), F32), ((56, 256), F32),
        ],
        n=18, flops=1 << 30,
    )(u, v, m, z_low, z_high, stiffness, master_record, *constants)
    y_low = ring(y_up, "gy", True)
    y_high = ring(y_down, "gy", False)

    (reply,) = call(gather_kernel, [((OWNERS, 8, 128), F32)], n=2, flops=1 << 20)(ids, table)
    x_up, x_down = call(edge_kernel, [((32, 128), F32), ((16, 128), F32)], n=7, flops=1 << 28)(
        u, v, m, z_low, z_high, y_low, y_high
    )
    x_low = ring(x_up, "gx", True)
    x_high = ring(x_down, "gx", False)
    replies = lax.all_to_all(reply, GROUPS, split_axis=0, concat_axis=0, tiled=True)

    edges = jnp.stack([lax.axis_index(a).astype(I32) for a in ("gz", "gy", "gx")])
    residual, tangent = call(
        element_kernel,
        [((3 * ZN * YN, XN), F32)] * 2,
        scratch=[
            pltpu.VMEM((NODE_ROWS, 128), F32),
            pltpu.VMEM((NODE_ROWS, 128), F32),
            pltpu.VMEM((NODE_ROWS, 256), BF16),
            pltpu.VMEM((NODE_ROWS, 256), BF16),
            pltpu.VMEM((NODE_ROWS, 128), F32),
            pltpu.VMEM((NODE_ROWS, 128), F32),
        ],
        smem=(0,), n=13, flops=1 << 33,
    )(
        edges, u, v, m, external.reshape(3 * ZN * YN, XN), z_low, z_high, y_low, y_high, x_low, x_high,
        big_h, big_l,
    )
    residual = residual.reshape(3, ZN, YN, XN)
    tangent = tangent.reshape(3, ZN, YN, XN)

    maps = [jnp.asarray(x) for x in (*node_x_map(), *node_y_map())]
    whole = pl.BlockSpec(memory_space=pltpu.VMEM)
    plane = pl.BlockSpec((3, 1, YN, XN), lambda i: (0, 0, 0, 0))
    out = jax.ShapeDtypeStruct((3, ZN, YN, XN), F32)
    return pl.pallas_call(
        contact_kernel,
        out_shape=(out, out),
        grid=(1,),
        in_specs=[whole] * 7 + [plane, plane],
        out_specs=(plane, plane),
        input_output_aliases={7: 0, 8: 1},
        cost_estimate=pl.CostEstimate(flops=1 << 20, bytes_accessed=1 << 20, transcendentals=0),
        compiler_params=pltpu.CompilerParams(vmem_limit_bytes=44 << 20),
    )(replies, quads, faces, *maps, residual, tangent)


def solution(mesh):
    placed = (
        P(None, "gz", "gy", "gx"),
        P(None, "gz", "gy", "gx"),
        P("gz", "gy", "gx"),
        P(None, "gz", "gy", "gx"),
        P(),
        P(None, ("gx", "gy", "gz")),
        P(("gx", "gy", "gz")),
        P(("gx", "gy", "gz"), None),
        P(("gx", "gy", "gz")),
        P(("gx", "gy", "gz")),
    )
    return jax.shard_map(
        local,
        mesh=mesh,
        in_specs=placed,
        out_specs=(P(None, "gz", "gy", "gx"), P(None, "gz", "gy", "gx")),
        check_vma=False,
    )
```

time: 638 us -> 71 us (0.11); the launches traced: 627 us -> 70.1 us
  local copies, waits for them, and re-layouts: 513 us -> 12.8 us
  other arithmetic: 65.4 us -> 0.08 us
  Pallas kernels: 0 us -> 19.7 us
  starting transfers between devices: 39.3 us -> 23.8 us
  waiting for transfers between devices: 0.02 us -> 12.2 us
    slice x76 -> x0, local copies, waits for them, and re-layouts: 379 us -> none  [the longest x54 366 us: element_block(): nodes[:, r:r + 2 * za:2, q:q + 2 * yb:2, p:p + 2 * xc:2].reshape(7, elems)]
    another operation x46 -> x0, local copies, waits for them, and re-layouts: 49 us -> none  [the longest x5 33.1 us: weave(): jnp.stack([lax.slice_in_dim(even, 0, count, axis=axis), middle], axis=axi...]
    another operation x14 -> x1, other arithmetic: 44.3 us -> 0.08 us  [local(): jnp.stack([lax.axis_index(a).astype(I32) for a in ('gz', 'gy', 'gx')])]
    reshape x16 -> x0, local copies, waits for them, and re-layouts: 27.3 us -> none  [the longest x5 23.7 us: weave(): woven = woven.reshape(shape)]
    pallas_call x0 -> x6, Pallas kernels: none -> 19.7 us  [the longest x1 11.1 us: local(): call(element_kernel, [((3 * ZN * YN, XN), F32)] * 2, scratch=[pltpu.VMEM(...]
    unnamed x132 -> x54, local copies, waits for them, and re-layouts: 27.7 us -> 12.8 us
    gather x3 -> x0, local copies, waits for them, and re-layouts: 9.44 us -> none  [the longest x1 6.44 us: local(): found = jnp.take(master_record, jnp.maximum(flat_ids, 0), axis=1)]
    all_to_all x2, waiting for transfers between devices: 0.01 us -> 8.92 us  [the longest x1 6.17 us: local(): lax.all_to_all(request, GROUPS, split_axis=0, concat_axis=0, tiled=True)]
  transfers between devices with their start and end apart: 8 -> 8, of which waited for: 0 -> 3; matrix products, arithmetic and copies ran while one was open for 90% -> 0% of each run, Pallas kernels for 0% -> 21%
where the time goes in v1:
time: 71 us; the launch traced here: 70.1 us
  starting transfers between devices  23.8 us (34%)
  Pallas kernels  19.7 us (28%)
  local copies, waits for them, and re-layouts  12.8 us (18%)
  waiting for transfers between devices  12.2 us (17%)
  between operations  1.5 us (2%)
    unnamed x54, local copies, waits for them, and re-layouts  12.8 us
    pallas_call x1, Pallas kernels, local(): call(element_kernel, [((3 * ZN * YN, XN), F32)] * 2, scratch=[pltpu.VMEM(...  11.1 us
    all_to_all x1, starting transfers between devices, local(): lax.all_to_all(request, GROUPS, split_axis=0, concat_axis=0, tiled=True)  10.7 us
    ppermute x6, starting transfers between devices, ring(): return lax.ppermute(values, axis, pairs)  8.31 us
    all_to_all x1, waiting for transfers between devices, local(): lax.all_to_all(request, GROUPS, split_axis=0, concat_axis=0, tiled=True)  6.17 us
    all_to_all x1, starting transfers between devices, local(): lax.all_to_all(reply, GROUPS, split_axis=0, concat_axis=0, tiled=True)  4.75 us
    ppermute x6, waiting for transfers between devices, ring(): return lax.ppermute(values, axis, pairs)  3.27 us
    pallas_call x1, Pallas kernels, local(): call(gather_kernel, [((OWNERS, 8, 128), F32)], n=2, flops=1 << 20)  3.09 us
  transfers between devices with their start and end apart: 8, of which 3 were waited for; matrix products, arithmetic and copies ran while one was open for 0% of the time, Pallas kernels for 21%

profile of v1, /device:TPU:8, one launch (start us, length us, event | category | flops | bytes accessed | tf_op | source)
XLA Modules:
  0.0 70.1 jit_solution(1300465957980398659)
XLA Ops:
  0.6 0.0 copy-start.12
  1.3 0.0 copy-start.11
  1.3 0.0 copy-start.10
  1.3 0.0 copy-done.12
  1.3 0.7 copy-done.11
  2.0 0.0 copy-done.10
  2.0 0.0 copy-start
  2.0 0.9 %copy-done = f32[3,16,8,128]{3,2,1,0:T(8,128)S(1)} copy-done((f32[3,16,8,128]{3,2,1,0:T(8,128)S(1)}, f32[3,16,8,128]{3,2,1,0:T(8,128)}, u32[]{:S(2)}) %copy-start) | copy-done | bytes 196632
  2.9 0.0 copy-start.2
  2.9 0.9 %copy-done.2 = f32[3,16,8,128]{3,2,1,0:T(8,128)S(1)} copy-done((f32[3,16,8,128]{3,2,1,0:T(8,128)S(1)}, f32[3,16,8,128]{3,2,1,0:T(8,128)}, u32[]{:S(2)}) %copy-start.2) | copy-done | bytes 196632
  3.9 0.0 copy-start.4
  3.9 0.8 %copy-done.4 = f32[16,8,128]{2,1,0:T(8,128)S(1)} copy-done((f32[16,8,128]{2,1,0:T(8,128)S(1)}, f32[16,8,128]{2,1,0:T(8,128)}, u32[]{:S(2)}) %copy-start.4) | copy-done | bytes 65560
  4.7 0.0 copy-start.1
  4.7 0.0 copy-start.3
  4.7 0.0 copy-start.26
  4.7 1.1 %shard_map.248 = (s32[64,128]{1,0:T(8,128)}, s32[16,128]{1,0:T(8,128)S(1)}, f32[7,16,128]{2,1,0:T(8,128)S(1)}, f32[7,8,128]{2,1,0:T(8,128)S(1)}) custom-call(s32[8,128]{1,0:T(8,128)S(1)} %bitcast.31, s32[8,128]{1,0:T(8,128)S(1)} %bitcast.32, s32[8,128]{1,0:T(8,128)S(1)} %bitcast.33, s32[1]{0:T(128)S(6)} %copy.32.count, f32[384,128]{1,0:T(8,128)S(1)} %bitcast.18, ...), custom_call_target="tpu_custom_call" | custom-call | flops 1048576 | bytes 1048576 | tf_op jit(solution)/shard_map/pallas_call | solution.py:497
  5.9 1.6 %collective-permute-start = (f32[7,16,128]{2,1,0:T(8,128)S(1)}, f32[7,16,128]{2,1,0:T(8,128)S(1)}, u32[]{:S(2)}, u32[]{:S(2)}) collective-permute-start(f32[7,16,128]{2,1,0:T(8,128)S(1)} %get-tuple-element.17), channel_id=1, source_target_pairs={{0,1},{1,2},{2,3},{3,0},{4,5},{5,6},{6,7},{7,4},{8,9},{9,10},{10,1... | collective-permute-start | bytes 172040 | tf_op jit(solution)/shard_map/ppermute | solution.py:479
  7.4 0.6 collective-permute-start.1
  8.1 3.3 %collective-permute-done.1 = f32[7,8,128]{2,1,0:T(8,128)S(1)} collective-permute-done((f32[7,8,128]{2,1,0:T(8,128)S(1)}, f32[7,8,128]{2,1,0:T(8,128)S(1)}, u32[]{:S(2)}, u32[]{:S(2)}) %collective-permute-start.1) | collective-permute-done | bytes 28704 | tf_op jit(solution)/shard_map/ppermute | solution.py:479
  11.3 0.0 collective-permute-done
  11.3 0.0 copy-done.1
  11.3 0.0 copy-done.3
  11.3 0.0 copy-done.5
  11.3 0.0 copy-done.25
  11.3 0.0 copy-done.26
  11.4 0.0 copy-start.13
  11.4 0.9 %copy-done.13 = f32[27,2048]{1,0:T(8,128)S(1)} copy-done((f32[27,2048]{1,0:T(8,128)S(1)}, f32[27,2048]{1,0:T(8,128)}, u32[]{:S(2)}) %copy-start.13) | copy-done | bytes 221208
  12.3 0.8 %copy-done.15 = f32[81,81]{1,0:T(8,128)S(1)} copy-done((f32[81,81]{1,0:T(8,128)S(1)}, f32[81,81]{1,0:T(8,128)}, u32[]{:S(2)}) %copy-start.15) | copy-done | bytes 26268
  13.1 0.9 %copy-done.16 = bf16[128,768]{1,0:T(8,128)(2,1)S(1)} copy-done((bf16[128,768]{1,0:T(8,128)(2,1)S(1)}, bf16[128,768]{1,0:T(8,128)(2,1)}, u32[]{:S(2)}) %copy-start.16) | copy-done | bytes 196632
  14.0 0.9 %copy-done.17 = bf16[128,768]{1,0:T(8,128)(2,1)S(1)} copy-done((bf16[128,768]{1,0:T(8,128)(2,1)S(1)}, bf16[128,768]{1,0:T(8,128)(2,1)}, u32[]{:S(2)}) %copy-start.17) | copy-done | bytes 196632
  15.0 0.9 %copy-done.18 = bf16[144,144]{1,0:T(8,128)(2,1)S(1)} copy-done((bf16[144,144]{1,0:T(8,128)(2,1)S(1)}, bf16[144,144]{1,0:T(8,128)(2,1)}, u32[]{:S(2)}) %copy-start.18) | copy-done | bytes 41496
  15.8 0.9 %copy-done.19 = bf16[144,144]{1,0:T(8,128)(2,1)S(1)} copy-done((bf16[144,144]{1,0:T(8,128)(2,1)S(1)}, bf16[144,144]{1,0:T(8,128)(2,1)}, u32[]{:S(2)}) %copy-start.19) | copy-done | bytes 41496
  16.7 0.9 %copy-done.20 = f32[144,81]{1,0:T(8,128)S(1)} copy-done((f32[144,81]{1,0:T(8,128)S(1)}, f32[144,81]{1,0:T(8,128)}, u32[]{:S(2)}) %copy-start.20) | copy-done | bytes 46680
  17.6 0.8 %copy-done.21 = bf16[56,288]{1,0:T(8,128)(2,1)S(1)} copy-done((bf16[56,288]{1,0:T(8,128)(2,1)S(1)}, bf16[56,288]{1,0:T(8,128)(2,1)}, u32[]{:S(2)}) %copy-start.21) | copy-done | bytes 32280
  18.4 0.8 %copy-done.22 = bf16[56,288]{1,0:T(8,128)(2,1)S(1)} copy-done((bf16[56,288]{1,0:T(8,128)(2,1)S(1)}, bf16[56,288]{1,0:T(8,128)(2,1)}, u32[]{:S(2)}) %copy-start.22) | copy-done | bytes 32280
  19.2 0.8 %copy-done.23 = bf16[56,288]{1,0:T(8,128)(2,1)S(1)} copy-done((bf16[56,288]{1,0:T(8,128)(2,1)S(1)}, bf16[56,288]{1,0:T(8,128)(2,1)}, u32[]{:S(2)}) %copy-start.23) | copy-done | bytes 32280
  20.0 0.8 %copy-done.24 = bf16[56,288]{1,0:T(8,128)(2,1)S(1)} copy-done((bf16[56,288]{1,0:T(8,128)(2,1)S(1)}, bf16[56,288]{1,0:T(8,128)(2,1)}, u32[]{:S(2)}) %copy-start.24) | copy-done | bytes 32280
  20.7 1.0 %shard_map.249 = (f32[336,128]{1,0:T(8,128)S(1)}, f32[168,128]{1,0:T(8,128)S(1)}, bf16[144,144]{1,0:T(8,128)(2,1)S(1)}, bf16[144,144]{1,0:T(8,128)(2,1)S(1)}, f3...) custom-call(f32[384,128]{1,0:T(8,128)S(1)} %bitcast.19, f32[384,128]{1,0:T(8,128)S(1)} %bitcast.23, f32[128,128]{1,0:T(8,128)S(1)} %bitcast.28, ...), custom_call_target="tpu_custom_call" | custom-call | flops 1073741824 | bytes 1048576 | tf_op jit(solution)/shard_map/pallas_call | solution.py:509
  21.7 1.6 %collective-permute-start.2 = (f32[336,128]{1,0:T(8,128)S(1)}, f32[336,128]{1,0:T(8,128)S(1)}, u32[]{:S(2)}, u32[]{:S(2)}) collective-permute-start(f32[336,128]{1,0:T(8,128)S(1)} %get-tuple-element.22), channel_id=1, source_target_pairs={{0,4},{4,8},{8,12},{12,0},{1,5},{5,9},{9,13},{13,1},{2,6},{6,10},{... | collective-permute-start | bytes 516104 | tf_op jit(solution)/shard_map/ppermute | solution.py:479
  23.3 1.7 %collective-permute-start.3 = (f32[168,128]{1,0:T(8,128)S(1)}, f32[168,128]{1,0:T(8,128)S(1)}, u32[]{:S(2)}, u32[]{:S(2)}) collective-permute-start(f32[168,128]{1,0:T(8,128)S(1)} %get-tuple-element.23), channel_id=1, source_target_pairs={{4,0},{8,4},{12,8},{0,12},{5,1},{9,5},{13,9},{1,13},{6,2},{10,6},{... | collective-permute-start | bytes 258056 | tf_op jit(solution)/shard_map/ppermute | solution.py:479
  25.0 10.7 %all-to-all-start = ((s32[64,1,128]{2,1,0:T(1,128)}), s32[64,1,128]{2,1,0:T(1,128)S(1)}, u32[]{:S(2)}, u32[]{:S(2)}) async-start(s32[64,1,128]{2,1,0:T(1,128)} %bitcast.7), calls=%async_computation | async-start | bytes 65536 | tf_op jit(solution)/shard_map/all_to_all | solution.py:504
  35.8 0.0 collective-permute-done.3.y_high
  35.8 0.0 collective-permute-done.2.y_low
  35.8 0.5 shard_map.251
  36.3 2.8 %collective-permute-start.5 = (f32[16,128]{1,0:T(8,128)S(1)}, f32[16,128]{1,0:T(8,128)S(1)}, u32[]{:S(2)}, u32[]{:S(2)}) collective-permute-start(f32[16,128]{1,0:T(8,128)S(1)} %get-tuple-element.25), channel_id=1, source_target_pairs={{16,0},{32,16},{48,32},{64,48},{80,64},{96,80},{112,96},{128,112},... | collective-permute-start | bytes 24584 | tf_op jit(solution)/shard_map/ppermute | solution.py:479
  39.1 0.0 collective-permute-start.4
  39.1 0.1 pad_add_fusion.edges
  39.2 6.2 %all-to-all-done = s32[64,1,128]{2,1,0:T(1,128)S(1)} async-done(((s32[64,1,128]{2,1,0:T(1,128)}), s32[64,1,128]{2,1,0:T(1,128)S(1)}, u32[]{:S(2)}, u32[]{:S(2)}) %all-to-all-start) | async-done | bytes 32800 | tf_op jit(solution)/shard_map/all_to_all | solution.py:504
  45.3 3.1 %shard_map.250 = f32[64,8,128]{2,1,0:T(8,128)} custom-call(s32[64,128]{1,0:T(8,128)S(1)} %bitcast.26, f32[32,2048]{1,0:T(8,128)S(1)} %get-tuple-element.19.table), custom_call_target="tpu_custom_call" | custom-call | flops 1048576 | bytes 1048576 | tf_op jit(solution)/shard_map/pallas_call | solution.py:520
  48.4 4.7 %all-to-all-start.1 = ((f32[64,8,128]{2,1,0:T(8,128)}), f32[64,8,128]{2,1,0:T(8,128)S(1)}, u32[]{:S(2)}, u32[]{:S(2)}) async-start(f32[64,8,128]{2,1,0:T(8,128)} %shard_map.250), calls=%async_computation.1 | async-start | bytes 524288 | tf_op jit(solution)/shard_map/all_to_all | solution.py:526
  53.2 0.0 collective-permute-done.5.x_high
  53.2 0.0 collective-permute-done.4.x_low
  53.2 0.0 copy-done.14
  53.2 0.0 copy-start.6
  53.2 0.0 copy-start.7
  53.2 0.0 copy-start.8
  53.3 0.0 copy-start.9
  53.3 11.1 %shard_map.252 = (f32[384,128]{1,0:T(8,128)}, f32[384,128]{1,0:T(8,128)}) custom-call(s32[3]{0:T(128)S(1)} %pad_add_fusion.edges, f32[384,128]{1,0:T(8,128)S(1)} %bitcast.21, f32[384,128]{1,0:T(8,128)S(1)} %bitcast.25, f32[128,128]{1,0:T(8,128)S(1)} %bitcast.30, f32[384,128]{1,0:T(8,128)S(1)} %bitcast.34, f32[112,128]{1,0:T(8,128)S(1)} %bitcast.37, ...), custom_call_target="tpu_custom_call" | custom-call | flops 8589934592 | bytes 1048576 | tf_op jit(solution)/shard_map/pallas_call | solution.py:529
  64.4 2.7 %all-to-all-done.1.replies = f32[64,8,128]{2,1,0:T(8,128)S(1)} async-done(((f32[64,8,128]{2,1,0:T(8,128)}), f32[64,8,128]{2,1,0:T(8,128)S(1)}, u32[]{:S(2)}, u32[]{:S(2)}) %all-to-all-start.1) | async-done | bytes 262176 | tf_op jit(solution)/shard_map/all_to_all | solution.py:526
  67.1 0.0 copy-done.6
  67.1 0.0 copy-done.7
  67.1 0.0 copy-done.8
  67.2 0.0 copy-done.9
  67.2 2.9 %shard_map.253 = (f32[3,16,8,128]{3,2,1,0:T(8,128)}, f32[3,16,8,128]{3,2,1,0:T(8,128)}) custom-call(f32[64,8,128]{2,1,0:T(8,128)S(1)} %all-to-all-done.1.replies, f32[56,256]{1,0:T(8,128)S(1)} %get-tuple-element.20.quads, s32[16,128]{1,0:T(8,128)S(1)} %get-tuple-element.21.faces, ...), custom_call_target="tpu_custom_call", output_to_operand_aliasing={{0}: (7, {}), {1}: (8, {})} | custom-call | flops 1048576 | bytes 1048576 | tf_op jit(solution)/shard_map/pallas_call | solution.py:552
  (13 shorter events, 0.0 us)
Async XLA Ops:
  0.6 0.7 copy-start.12
  1.3 0.7 copy-start.11
  1.3 0.7 copy-start.10
  2.0 0.9 %copy-start = (f32[3,16,8,128]{3,2,1,0:T(8,128)S(1)}, f32[3,16,8,128]{3,2,1,0:T(8,128)}, u32[]{:S(2)}) copy-start(f32[3,16,8,128]{3,2,1,0:T(8,128)} %param.25) | copy-start | bytes 589828
  2.9 0.9 %copy-start.2 = (f32[3,16,8,128]{3,2,1,0:T(8,128)S(1)}, f32[3,16,8,128]{3,2,1,0:T(8,128)}, u32[]{:S(2)}) copy-start(f32[3,16,8,128]{3,2,1,0:T(8,128)} %param.26) | copy-start | bytes 589828
  3.9 0.8 %copy-start.4 = (f32[16,8,128]{2,1,0:T(8,128)S(1)}, f32[16,8,128]{2,1,0:T(8,128)}, u32[]{:S(2)}) copy-start(f32[16,8,128]{2,1,0:T(8,128)} %param.27) | copy-start | bytes 196612
  4.7 6.6 %copy-start.1 = (f32[3,16,8,128]{3,2,1,0:T(8,128)S(1)}, f32[3,16,8,128]{3,2,1,0:T(8,128)}, u32[]{:S(2)}) copy-start(f32[3,16,8,128]{3,2,1,0:T(8,128)} %param.25) | copy-start | bytes 589828
  4.7 6.6 %copy-start.3 = (f32[3,16,8,128]{3,2,1,0:T(8,128)S(1)}, f32[3,16,8,128]{3,2,1,0:T(8,128)}, u32[]{:S(2)}) copy-start(f32[3,16,8,128]{3,2,1,0:T(8,128)} %param.26) | copy-start | bytes 589828
  4.7 6.6 %copy-start.5 = (f32[16,8,128]{2,1,0:T(8,128)S(1)}, f32[16,8,128]{2,1,0:T(8,128)}, u32[]{:S(2)}) copy-start(f32[16,8,128]{2,1,0:T(8,128)} %param.27) | copy-start | bytes 196612
  4.7 6.6 %copy-start.25 = (bf16[32,27]{1,0:T(8,128)(2,1)S(1)}, bf16[32,27]{1,0:T(8,128)(2,1)}, u32[]{:S(2)}) copy-start(bf16[32,27]{1,0:T(8,128)(2,1)} %constant.46.clone.record_l) | copy-start | bytes 5188
  4.7 6.6 %copy-start.26 = (bf16[32,27]{1,0:T(8,128)(2,1)S(1)}, bf16[32,27]{1,0:T(8,128)(2,1)}, u32[]{:S(2)}) copy-start(bf16[32,27]{1,0:T(8,128)(2,1)} %constant.45.clone.record_h) | copy-start | bytes 5188
  5.9 5.4 %collective-permute-start = (f32[7,16,128]{2,1,0:T(8,128)S(1)}, f32[7,16,128]{2,1,0:T(8,128)S(1)}, u32[]{:S(2)}, u32[]{:S(2)}) collective-permute-start(f32[7,16,128]{2,1,0:T(8,128)S(1)} %get-tuple-element.17), channel_id=1, source_target_pairs={{0,1},{1,2},{2,3},{3,0},{4,5},{5,6},{6,7},{7,4},{8,9},{9,10},{10,1... | collective-permute-start | bytes 172040 | tf_op jit(solution)/shard_map/ppermute | solution.py:479
  7.4 3.9 %collective-permute-start.1 = (f32[7,8,128]{2,1,0:T(8,128)S(1)}, f32[7,8,128]{2,1,0:T(8,128)S(1)}, u32[]{:S(2)}, u32[]{:S(2)}) collective-permute-start(f32[7,8,128]{2,1,0:T(8,128)S(1)} %get-tuple-element.18), channel_id=1, source_target_pairs={{1,0},{2,1},{3,2},{0,3},{5,4},{6,5},{7,6},{4,7},{9,8},{10,9},{11,1... | collective-permute-start | bytes 86024 | tf_op jit(solution)/shard_map/ppermute | solution.py:479
  11.4 1.0 %copy-start.13 = (f32[27,2048]{1,0:T(8,128)S(1)}, f32[27,2048]{1,0:T(8,128)}, u32[]{:S(2)}) copy-start(f32[27,2048]{1,0:T(8,128)} %master.1) | copy-start | bytes 663556
  12.3 0.8 %copy-start.15 = (f32[81,81]{1,0:T(8,128)S(1)}, f32[81,81]{1,0:T(8,128)}, u32[]{:S(2)}) copy-start(f32[81,81]{1,0:T(8,128)} %stiffness.1) | copy-start | bytes 78736
  13.1 0.9 %copy-start.16 = (bf16[128,768]{1,0:T(8,128)(2,1)S(1)}, bf16[128,768]{1,0:T(8,128)(2,1)}, u32[]{:S(2)}) copy-start(bf16[128,768]{1,0:T(8,128)(2,1)} %constant.48.clone.face_x_l) | copy-start | bytes 589828
  14.0 0.9 %copy-start.17 = (bf16[128,768]{1,0:T(8,128)(2,1)S(1)}, bf16[128,768]{1,0:T(8,128)(2,1)}, u32[]{:S(2)}) copy-start(bf16[128,768]{1,0:T(8,128)(2,1)} %constant.47.clone.face_x_h) | copy-start | bytes 589828
  15.0 0.9 %copy-start.18 = (bf16[144,144]{1,0:T(8,128)(2,1)S(1)}, bf16[144,144]{1,0:T(8,128)(2,1)}, u32[]{:S(2)}) copy-start(bf16[144,144]{1,0:T(8,128)(2,1)} %constant.44.clone.fixed_l) | copy-start | bytes 124420
  15.8 0.9 %copy-start.19 = (bf16[144,144]{1,0:T(8,128)(2,1)S(1)}, bf16[144,144]{1,0:T(8,128)(2,1)}, u32[]{:S(2)}) copy-start(bf16[144,144]{1,0:T(8,128)(2,1)} %constant.43.clone.fixed_h) | copy-start | bytes 124420
  16.7 0.9 %copy-start.20 = (f32[144,81]{1,0:T(8,128)S(1)}, f32[144,81]{1,0:T(8,128)}, u32[]{:S(2)}) copy-start(f32[144,81]{1,0:T(8,128)} %constant.42.clone.place) | copy-start | bytes 139972
  17.6 0.8 %copy-start.21 = (bf16[56,288]{1,0:T(8,128)(2,1)S(1)}, bf16[56,288]{1,0:T(8,128)(2,1)}, u32[]{:S(2)}) copy-start(bf16[56,288]{1,0:T(8,128)(2,1)} %constant.52.clone.second_l) | copy-start | bytes 96772
  18.4 0.8 %copy-start.22 = (bf16[56,288]{1,0:T(8,128)(2,1)S(1)}, bf16[56,288]{1,0:T(8,128)(2,1)}, u32[]{:S(2)}) copy-start(bf16[56,288]{1,0:T(8,128)(2,1)} %constant.51.clone.second_h) | copy-start | bytes 96772
  19.2 0.8 %copy-start.23 = (bf16[56,288]{1,0:T(8,128)(2,1)S(1)}, bf16[56,288]{1,0:T(8,128)(2,1)}, u32[]{:S(2)}) copy-start(bf16[56,288]{1,0:T(8,128)(2,1)} %constant.50.clone.first_l) | copy-start | bytes 96772
  20.0 0.8 %copy-start.24 = (bf16[56,288]{1,0:T(8,128)(2,1)S(1)}, bf16[56,288]{1,0:T(8,128)(2,1)}, u32[]{:S(2)}) copy-start(bf16[56,288]{1,0:T(8,128)(2,1)} %constant.49.clone.first_h) | copy-start | bytes 96772
  21.7 14.1 %collective-permute-start.2 = (f32[336,128]{1,0:T(8,128)S(1)}, f32[336,128]{1,0:T(8,128)S(1)}, u32[]{:S(2)}, u32[]{:S(2)}) collective-permute-start(f32[336,128]{1,0:T(8,128)S(1)} %get-tuple-element.22), channel_id=1, source_target_pairs={{0,4},{4,8},{8,12},{12,0},{1,5},{5,9},{9,13},{13,1},{2,6},{6,10},{... | collective-permute-start | bytes 516104 | tf_op jit(solution)/shard_map/ppermute | solution.py:479
  23.3 12.5 %collective-permute-start.3 = (f32[168,128]{1,0:T(8,128)S(1)}, f32[168,128]{1,0:T(8,128)S(1)}, u32[]{:S(2)}, u32[]{:S(2)}) collective-permute-start(f32[168,128]{1,0:T(8,128)S(1)} %get-tuple-element.23), channel_id=1, source_target_pairs={{4,0},{8,4},{12,8},{0,12},{5,1},{9,5},{13,9},{1,13},{6,2},{10,6},{... | collective-permute-start | bytes 258056 | tf_op jit(solution)/shard_map/ppermute | solution.py:479
  25.0 20.3 %all-to-all-start = ((s32[64,1,128]{2,1,0:T(1,128)}), s32[64,1,128]{2,1,0:T(1,128)S(1)}, u32[]{:S(2)}, u32[]{:S(2)}) async-start(s32[64,1,128]{2,1,0:T(1,128)} %bitcast.7), calls=%async_computation | async-start | bytes 65536 | tf_op jit(solution)/shard_map/all_to_all | solution.py:504
  36.3 16.9 %collective-permute-start.5 = (f32[16,128]{1,0:T(8,128)S(1)}, f32[16,128]{1,0:T(8,128)S(1)}, u32[]{:S(2)}, u32[]{:S(2)}) collective-permute-start(f32[16,128]{1,0:T(8,128)S(1)} %get-tuple-element.25), channel_id=1, source_target_pairs={{16,0},{32,16},{48,32},{64,48},{80,64},{96,80},{112,96},{128,112},... | collective-permute-start | bytes 24584 | tf_op jit(solution)/shard_map/ppermute | solution.py:479
  39.1 14.1 %collective-permute-start.4 = (f32[32,128]{1,0:T(8,128)S(1)}, f32[32,128]{1,0:T(8,128)S(1)}, u32[]{:S(2)}, u32[]{:S(2)}) collective-permute-start(f32[32,128]{1,0:T(8,128)S(1)} %get-tuple-element.24), channel_id=1, source_target_pairs={{0,16},{16,32},{32,48},{48,64},{64,80},{80,96},{96,112},{112,128},... | collective-permute-start | bytes 49160 | tf_op jit(solution)/shard_map/ppermute | solution.py:479
  48.4 4.8 %copy-start.14 = (f32[3,16,8,128]{3,2,1,0:T(8,128)S(1)}, f32[3,16,8,128]{3,2,1,0:T(8,128)}, u32[]{:S(2)}) copy-start(f32[3,16,8,128]{3,2,1,0:T(8,128)} %param.28) | copy-start | bytes 589828
  48.4 18.7 %all-to-all-start.1 = ((f32[64,8,128]{2,1,0:T(8,128)}), f32[64,8,128]{2,1,0:T(8,128)S(1)}, u32[]{:S(2)}, u32[]{:S(2)}) async-start(f32[64,8,128]{2,1,0:T(8,128)} %shard_map.250), calls=%async_computation.1 | async-start | bytes 524288 | tf_op jit(solution)/shard_map/all_to_all | solution.py:526
  53.2 13.9 %copy-start.6 = (bf16[48,576]{1,0:T(8,128)(2,1)S(1)}, bf16[48,576]{1,0:T(8,128)(2,1)}, u32[]{:S(2)}) copy-start(bf16[48,576]{1,0:T(8,128)(2,1)} %constant.56.clone.node_y_l) | copy-start | bytes 165892
  53.2 13.9 %copy-start.7 = (bf16[48,576]{1,0:T(8,128)(2,1)S(1)}, bf16[48,576]{1,0:T(8,128)(2,1)}, u32[]{:S(2)}) copy-start(bf16[48,576]{1,0:T(8,128)(2,1)} %constant.55.clone.node_y_h) | copy-start | bytes 165892
  53.2 13.9 %copy-start.8 = (bf16[64,384]{1,0:T(8,128)(2,1)S(1)}, bf16[64,384]{1,0:T(8,128)(2,1)}, u32[]{:S(2)}) copy-start(bf16[64,384]{1,0:T(8,128)(2,1)} %constant.54.clone.node_x_l) | copy-start | bytes 147460
  53.3 13.9 %copy-start.9 = (bf16[64,384]{1,0:T(8,128)(2,1)S(1)}, bf16[64,384]{1,0:T(8,128)(2,1)}, u32[]{:S(2)}) copy-start(bf16[64,384]{1,0:T(8,128)(2,1)} %constant.53.clone.node_x_h) | copy-start | bytes 147460

commit v2 on v1

v2 whole, which is shorter than its diff:
```python
import jax
import jax.numpy as jnp
import numpy as np
from jax import lax
from jax.experimental import pallas as pl
from jax.experimental.pallas import tpu as pltpu
from jax.sharding import PartitionSpec as P

F32 = jnp.float32
BF16 = jnp.bfloat16
I32 = jnp.int32

ZN, YN, XN = 16, 8, 128
ZE, YE = ZN + 3, YN + 3
OWNERS, CAP, PAIRS, ROWS = 64, 32, 1024, 2048
CHUNKS = OWNERS * CAP // 128
FACE_ROWS, FACE_COLS, FACE_LANES = 3, 63, 64
FACES = FACE_ROWS * FACE_LANES
SLABS = 28
TILE = 16
YPITCH = TILE
ZPITCH = YE * TILE
NODE_ROWS = ZE * ZPITCH
BLOCK = 9 * TILE
GROUPS = ("gx", "gy")
GROUP = 14
GATHERED = 16


def shapes_1d():
    points = np.array([-np.sqrt(0.6), 0.0, np.sqrt(0.6)])
    gauss = np.array([5.0, 8.0, 5.0]) / 9.0
    line = np.stack(
        [points * (points - 1.0) / 2.0, 1.0 - points * points, points * (points + 1.0) / 2.0],
        axis=1,
    )
    return line, gauss


def halves(values):
    high = np.asarray(values, np.float32).astype(jnp.bfloat16)
    low = (np.asarray(values, np.float64) - high.astype(np.float64)).astype(jnp.bfloat16)
    return high, low


def record_map():
    line, _ = shapes_1d()
    out = np.zeros((32, 27))
    for k in range(3):
        for qy in range(3):
            for qx in range(3):
                q = 3 * qy + qx
                row = k * 8 + q if q < 8 else 24 + k
                for b in range(3):
                    for a in range(3):
                        out[row, 9 * k + 3 * b + a] = line[qy, b] * line[qx, a]
    return halves(out)


def quad_row(part, q):
    return part * 8 + q if q < 8 else 48 + part


def face_x_map():
    line, _ = shapes_1d()
    out = np.zeros((128, 6 * 128))
    for qx in range(3):
        for side in range(2):
            for fx in range(FACE_COLS):
                for a in range(3):
                    out[2 * fx + a, (2 * qx + side) * 128 + side * 64 + fx] = line[qx, a]
    return halves(out)


def face_y_map():
    line, _ = shapes_1d()
    first = np.zeros((56, 6 * 48))
    second = np.zeros((56, 6 * 48))
    for part in range(6):
        for qy in range(3):
            for qx in range(3):
                row = quad_row(part, 3 * qy + qx)
                for b in range(3):
                    first[row, (2 * qx) * 48 + part * 8 + b] = line[qy, b]
                    first[row, (2 * qx + 1) * 48 + part * 8 + 2 + b] = line[qy, b]
                    second[row, (2 * qx) * 48 + part * 8 + 4 + b] = line[qy, b]
    return halves(first), halves(second)


def node_x_map():
    line, _ = shapes_1d()
    out = np.zeros((FACE_LANES, 3 * 128))
    for qx in range(3):
        for fx in range(FACE_COLS):
            for a in range(3):
                out[fx, qx * 128 + 2 * fx + a] = line[qx, a]
    return halves(out)


def node_y_map():
    line, gauss = shapes_1d()
    out = np.zeros((48, 3 * FACE_ROWS * 64))
    for part in range(6):
        for qx in range(3):
            for qy in range(3):
                weight = 0.25 * gauss[qx] * gauss[qy] * (-1.0 if part < 3 else 1.0)
                for fy in range(FACE_ROWS):
                    for b in range(3):
                        column = qx * FACE_ROWS * 64 + fy * 64 + quad_row(part, 3 * qy + qx)
                        out[part * 8 + 2 * fy + b, column] = weight * line[qy, b]
    return halves(out)


def stiffness_places():
    place = np.zeros((BLOCK, 81))
    for block in range(9):
        for p in range(3):
            for c in range(3):
                place[block * TILE + 3 * p + c, block * 9 + 3 * p + c] = 1.0
    fixed = np.zeros((BLOCK, BLOCK))
    for block in range(9):
        fixed[block * TILE + 9, block * TILE + 12] = 1.0
        for p in range(3):
            fixed[10, block * TILE + 9 + p] = 1.0 / 27.0
    fixed[[b * TILE + 9 for b in range(1, 9)], :] = 0.0
    for block in range(1, 9):
        fixed[block * TILE + 9, block * TILE + 12] = 1.0
    return place.astype(np.float32), halves(fixed)


def packed(pieces, rows, columns):
    out = np.zeros((rows, columns), jnp.bfloat16)
    for row, column, piece in pieces:
        out[row : row + piece.shape[0], column : column + piece.shape[1]] = piece
    return out


def prepare_constants():
    place, fixed = stiffness_places()
    record, along = record_map(), face_x_map()
    first, second = face_y_map()
    pieces = [
        (0, 0, along[0]), (128, 0, along[1]),
        (256, 0, first[0]), (256, 384, second[0]), (320, 0, first[1]), (320, 384, second[1]),
        (384, 0, fixed[0]), (384, 256, fixed[1]), (384, 512, place.astype(jnp.bfloat16)),
        (528, 0, record[0]), (528, 128, record[1]),
    ]
    return packed(pieces, 560, 768)


def contact_constants():
    along, across = node_x_map(), node_y_map()
    pieces = [(0, 0, along[0]), (64, 0, along[1]), (128, 0, across[0]), (176, 0, across[1])]
    return packed(pieces, 224, 576)


def split(values):
    high = values.astype(BF16)
    return high, (values - high.astype(F32)).astype(BF16)


def mm(a, b):
    return jnp.dot(a, b, preferred_element_type=F32)


def mm_nt(a, b):
    return lax.dot_general(a, b, (((1,), (1,)), ((), ())), preferred_element_type=F32)


def mm3(a, b):
    return mm(a[0], b[0]) + (mm(a[0], b[1]) + mm(a[1], b[0]))


def lane_ids(rows):
    return lax.broadcasted_iota(I32, (rows, 128), 1)


def pick_lanes(values, index):
    return jnp.take_along_axis(values, index, axis=1, mode="promise_in_bounds")


def compact(values):
    return (
        values[0:16]
        + pltpu.roll(values[16:32], 32, 1)
        + pltpu.roll(values[32:48], 64, 1)
        + pltpu.roll(values[48:64], 96, 1)
    )


def by_group(lane, parts):
    odd = (lane & 32) != 0
    return jnp.where(lane < 64, jnp.where(odd, parts[1], parts[0]), jnp.where(odd, parts[3], parts[2]))


def swap_groups(quads):
    lane = lane_ids(8)
    moved = [[by_group(lane, [q[(g + r) % 4] for g in range(4)]) for q in quads] for r in range(4)]
    for r in range(1, 4):
        moved[r] = [pltpu.roll(x, 32 * r, 1) for x in moved[r]]
    return [
        [by_group(lane, [moved[(f - g) % 4][i] for f in range(4)]) for g in range(4)]
        for i in range(len(quads))
    ]


def request_kernel(owner, row, face, count, u, v, m, request, faces, z_up, z_down, arrived):
    layers = []
    for i, (to, start, size) in enumerate(((z_up, ZN - 2, 2), (z_down, 0, 1))):
        part = pl.ds(start, size)
        layers += [
            pltpu.make_async_copy(u.at[:, part], to.at[pl.ds(0, 3)], arrived.at[3 * i]),
            pltpu.make_async_copy(v.at[:, part], to.at[pl.ds(3, 3)], arrived.at[3 * i + 1]),
            pltpu.make_async_copy(m.at[part], to.at[6], arrived.at[3 * i + 2]),
        ]
    for copy in layers:
        copy.start()
    live_count = count[0]
    who = lax.broadcasted_iota(I32, (OWNERS, 128), 0)
    lane = lane_ids(1)
    hits = []
    for t in range(PAIRS // 128):
        live = lane + t * 128 < live_count
        target = jnp.where(live, owner[pl.ds(t, 1), :], -1)
        hits.append(jnp.where(who == target, 1.0, 0.0).astype(F32))
    before = jnp.where(
        lax.broadcasted_iota(I32, (128, 128), 0) < lax.broadcasted_iota(I32, (128, 128), 1), 1.0, 0.0
    ).astype(BF16)
    ranks = mm(jnp.concatenate([h.astype(BF16) for h in hits], axis=0), before)
    base = jnp.zeros((OWNERS, 1), F32)
    places = lax.broadcasted_iota(I32, (128, 128), 0)
    highs, lows, sides = [], [], []
    for t in range(PAIRS // 128):
        rank = jnp.sum(hits[t] * (ranks[t * OWNERS : (t + 1) * OWNERS] + base), axis=0, keepdims=True)
        base = base + jnp.sum(hits[t], axis=1, keepdims=True)
        here = places == rank.astype(I32)
        number = row[pl.ds(t, 1), :] + 1
        f = face[pl.ds(t, 1), :]
        f = f + jnp.where(f >= FACE_COLS, 1, 0) + jnp.where(f >= 2 * FACE_COLS, 1, 0) + 1
        highs.append(jnp.where(here, lax.shift_right_logical(number, 6).astype(F32), 0.0).astype(BF16))
        lows.append(jnp.where(here, (number & 63).astype(F32), 0.0).astype(BF16))
        sides.append(jnp.where(here, f.astype(F32), 0.0).astype(BF16))
    hit = jnp.concatenate([h.astype(BF16) for h in hits], axis=1)
    high = mm_nt(hit, jnp.concatenate(highs, axis=1))
    low = mm_nt(hit, jnp.concatenate(lows, axis=1))
    request[...] = (high * 64.0 + low).astype(I32)
    faces[...] = compact(mm_nt(hit, jnp.concatenate(sides, axis=1))).astype(I32)
    for copy in layers:
        copy.wait()


def side_kernel(u, v, m, z_low, z_high, y_up, y_down):
    for first, field, comps in ((0, u, 3), (3, v, 3), (6, m, 1)):
        for c in range(comps):
            n = first + c
            for out, h, y in ((y_up, 0, YN - 2), (y_up, 1, YN - 1), (y_down, 0, 0)):
                at = (n * (2 if out is y_up else 1) + h) * 24
                out[pl.ds(at, ZN), :] = field[pl.ds(c * ZN * YN + y, ZN, stride=YN), :]
                out[pl.ds(at + 16, 8), :] = jnp.zeros((8, 128), F32)
                out[pl.ds(at + 16, 1), :] = z_low[pl.ds((n * 2) * YN + y, 1), :]
                out[pl.ds(at + 17, 1), :] = z_low[pl.ds((n * 2 + 1) * YN + y, 1), :]
                out[pl.ds(at + 18, 1), :] = z_high[pl.ds(n * YN + y, 1), :]


def prepare_kernel(u, v, stiffness, master, fixed, big_h, big_l, table, quads):
    places = fixed[384:528, 512:593]
    high, low = split(stiffness[...])
    lower = (stiffness[...] - high.astype(F32) - low.astype(F32)).astype(BF16)
    spread = [mm_nt(mm(places, part).astype(BF16), places) for part in (high, low, lower)]
    high, low = split((spread[0] + spread[1]) + spread[2])
    big_h[...] = high + fixed[384:528, 0:144]
    big_l[...] = low + fixed[384:528, 256:400]
    table[...] = mm3((fixed[528:560, 0:27], fixed[528:560, 128:155]), split(master[...]))
    plane = jnp.concatenate(
        [field[pl.ds(c * ZN * YN, YN), :] for field in (u, v) for c in range(3)], axis=0
    )
    wide = mm3(split(plane), (fixed[0:128, :], fixed[128:256, :]))
    tall = split(jnp.concatenate([wide[:, i * 128 : (i + 1) * 128] for i in range(6)], axis=0))
    for first, to in ((0, 0), (384, 128)):
        pair = fixed[256:312, first : first + 288], fixed[320:376, first : first + 288]
        quads[:, to : to + 128] = mm3(pair, tall)


def gather_kernel(ids, table, reply):
    numbers = jnp.maximum(compact(ids[...]) - 1, 0)
    for base in range(0, CHUNKS, GATHERED):
        found = []
        for c in range(base, base + GATHERED):
            number = jnp.broadcast_to(numbers[c : c + 1], (8, 128))
            inside = number & 127
            outside = lax.shift_right_logical(number, 7)
            parts = []
            for f in range(4):
                total = pick_lanes(table[pl.ds(f * 8, 8), 0:128], inside)
                for k in range(1, ROWS // 128):
                    piece = pick_lanes(table[pl.ds(f * 8, 8), k * 128 : (k + 1) * 128], inside)
                    total = jnp.where(outside == k, piece, total)
                parts.append(total)
            found.append(parts)
        tiles = swap_groups(found)
        for i in range(GATHERED):
            for g in range(4):
                reply[g * CHUNKS + base + i] = tiles[i][g]


def slab(fields, halos, n, s):
    z_low, z_high, y_low, y_high = halos
    if s < 16:
        return fields[n // 3][pl.ds((n % 3 * ZN + s) * YN, YN), :]
    if s < 18:
        return z_low[pl.ds((n * 2 + s - 16) * YN, YN), :]
    if s < 19:
        return z_high[pl.ds(n * YN, YN), :]
    h, zb = divmod(s - 19, 3)
    if h < 2:
        return y_low[pl.ds((n * 2 + h) * 24 + zb * 8, 8), :]
    return y_high[pl.ds(n * 24 + zb * 8, 8), :]


def edge_kernel(u, v, m, z_low, z_high, y_low, y_high, x_down):
    fields, halos = (u, v, m), (z_low, z_high, y_low, y_high)
    lane = lane_ids(8)
    down = [jnp.zeros((8, 128), F32) for _ in range(2)]
    for c in range(4):
        for s in range(SLABS):
            k, spot = divmod(c * SLABS + s, 64)
            one = slab(fields, halos, 6 if c == 3 else c, s)
            two = one if c == 3 else slab(fields, halos, 3 + c, s)
            one = pltpu.roll(one, spot, 1) if spot else one
            two = pltpu.roll(two, 64 + spot, 1)
            down[k] = jnp.where(lane == spot, one, jnp.where(lane == 64 + spot, two, down[k]))
    for k in range(2):
        x_down[pl.ds(k * 8, 8), :] = down[k]


def element_kernel(
    edges, u, v, m, external, z_low, z_high, y_low, y_high, x_high, big_h, big_l,
    residual, tangent, last, nodes, tiles_h, tiles_l, total,
):
    fields, halos = (u, v, m), (z_low, z_high, y_low, y_high)
    lane = lane_ids(8)
    low_half = lane < 64
    spot_of = lane & 63
    at_last = spot_of == 63
    even_even = 2 * spot_of
    odd_odd = 2 * spot_of + 1
    next_next = (2 * spot_of + 2) & 127

    def node_values(group):
        ones = [slab(fields, halos, 6 if c == 3 else c, s) for c, s in group]
        twos = [None if c == 3 else slab(fields, halos, 3 + c, s) for c, s in group]
        found = []
        for index in (even_even, odd_odd, next_next):
            first = [pick_lanes(one, index) for one in ones]
            second = [None if two is None else pick_lanes(two, index) for two in twos]
            found.append([a if b is None else jnp.where(low_half, a, b) for a, b in zip(first, second)])
        for i, (c, s) in enumerate(group):
            k, spot = divmod(c * SLABS + s, 64)
            held = x_high[pl.ds(k * 8, 8), :]
            after = held if spot == 63 else pltpu.roll(held, 63 - spot, 1)
            found[2][i] = jnp.where(at_last, after, found[2][i])
        return list(zip(*found))

    def put(value, s, at):
        if s < 19:
            z = s + 2 if s < 16 else (0, 1, 18)[s - 16]
            nodes[pl.ds(z * ZPITCH + 2 * YPITCH + at, 8, stride=YPITCH), :] = value
            return
        h, zb = divmod(s - 19, 3)
        base = (0, 1, 10)[h] * YPITCH + at
        if zb < 2:
            nodes[pl.ds((2 + zb * 8) * ZPITCH + base, 8, stride=ZPITCH), :] = value
        else:
            nodes[pl.ds(base, 1), :] = value[0:1]
            nodes[pl.ds(ZPITCH + base, 1), :] = value[1:2]
            nodes[pl.ds(18 * ZPITCH + base, 1), :] = value[2:3]

    todo = [(c, s) for c in range(4) for s in range(SLABS)]
    for start in range(0, len(todo), GROUP):
        group = todo[start : start + GROUP]
        values = node_values(group)
        for (c, s), three in zip(group, values):
            first, step = (9, 1) if c == 3 else (c, 3)
            for p in range(3):
                put(three[p], s, first + step * p)

    sub = lax.broadcasted_iota(I32, (TILE, 128), 0)
    one = jnp.where(sub == 12, 1.0, 0.0)

    def halve(z, carry):
        places = [pl.ds(pl.multiple_of(z * ZPITCH + y * YPITCH, TILE), TILE) for y in range(YE)]
        pairs = [split(jnp.where(sub < 12, nodes[at, :], one)) for at in places]
        for at, (high, low) in zip(places, pairs):
            tiles_h[at, :] = high
            tiles_l[at, :] = low
        return carry

    lax.fori_loop(0, ZE, halve, 0)

    x_last = jnp.where(edges[2] == lax.axis_size("gx") - 1, 63, 64)
    inside_x = jnp.where((lane_ids(1) & 63) < x_last, 1.0, 0.0)
    y_first = jnp.where(edges[1] == 0, 1, 0)
    y_last = jnp.where(edges[1] == lax.axis_size("gy") - 1, 3, 4)
    z_first = jnp.where(edges[0] == 0, 1, 0)
    z_last = jnp.where(edges[0] == lax.axis_size("gz") - 1, 7, 8)
    left_high, left_low = big_h[...], big_l[...]

    total[pl.ds(0, ZPITCH), :] = jnp.zeros((ZPITCH, 128), F32)

    def inside_of(k, j):
        return (k >= z_first) & (k <= z_last) & (j >= y_first) & (j <= y_last)

    def products(elements):
        operands = []
        for tiles in (tiles_h, tiles_l):
            columns = []
            for k, j in elements:
                starts = [pl.multiple_of((2 * k + r) * ZPITCH + 2 * j * YPITCH, TILE) for r in range(3)]
                columns.append(jnp.concatenate([tiles[pl.ds(a, 3 * TILE), :] for a in starts], axis=0))
            operands.append(jnp.concatenate(columns, axis=1))
        both = mm3((left_high, left_low), operands)
        forces = []
        for i, (k, j) in enumerate(elements):
            mine = both[:, i * 128 : (i + 1) * 128]
            forces.append(mine * jnp.where(inside_of(k, j), mine[10:11] * inside_x, 0.0))
        return forces

    def part(force, r, q):
        return force[(3 * r + q) * TILE : (3 * r + q + 1) * TILE]

    def place_of(z, y):
        return pl.ds(pl.multiple_of(z * ZPITCH + y * YPITCH, TILE), TILE)

    def layers(i, carry):
        shared = None
        for j in range(5):
            one, two = products([(2 * i, j), (2 * i + 1, j)])
            for q in range(3):
                sums = [part(one, 0, q), part(one, 1, q), part(one, 2, q) + part(two, 0, q), part(two, 1, q), part(two, 2, q)]
                if q == 0 and shared is not None:
                    sums = [a + b for a, b in zip(sums, shared)]
                if q == 2 and j < 4:
                    shared = sums
                    continue
                y = 2 * j + q
                sums[0] = sums[0] + total[place_of(4 * i, y), :]
                for r in range(5):
                    total[place_of(4 * i + r, y), :] = sums[r]
        return carry

    lax.fori_loop(0, 4, layers, 0)
    last_layer = products([(8, 0), (8, 1)]) + products([(8, 2), (8, 3)]) + products([(8, 4)])
    for r in range(3):
        for y in range(YE):
            held = [part(last_layer[j], r, y - 2 * j) for j in range(5) if 0 <= y - 2 * j <= 2]
            held = held + [total[place_of(16, y), :]] if r == 0 else held
            total[place_of(16 + r, y), :] = sum(held[1:], held[0])

    half = lax.shift_right_logical(lane, 1)
    weave_u = half + jnp.where((lane & 1) == 0, 0, 64)
    weave_v = half + jnp.where((lane & 1) == 0, 64, 0)
    at_first = spot_of == 0
    sent = jnp.zeros((8, 128), F32)
    for start in range(0, ZN, 4):
        layer = range(start, start + 4)

        def rows(z, row):
            return total[pl.ds((z + 2) * ZPITCH + 2 * YPITCH + row, 8, stride=YPITCH), :]

        held = [rows(z, 9) for z in layer]
        p0 = [rows(z, c) for z in layer for c in range(3)]
        p1 = [rows(z, 3 + c) for z in layer for c in range(3)]
        p2 = [rows(z, 6 + c) for z in layer for c in range(3)]
        after = [pltpu.roll(x, 1, 1) for x in held + p2]
        odd = [pltpu.roll(x, 64, 1) for x in p1]
        for i, z in enumerate(layer):
            sent = jnp.where(spot_of == 48 + z, pltpu.roll(held[i], (z - 15) % 128, 1), sent)
            for c in range(3):
                moved = pltpu.roll(p2[3 * i + c], (c * 16 + z - 63) % 128, 1)
                sent = jnp.where(spot_of == c * 16 + z, moved, sent)
        after = [jnp.where(at_first, 0.0, x) for x in after]
        even = [a + b for a, b in zip(p0, after[4:])]
        mass = [pick_lanes(jnp.where(low_half, a + b, a), weave_u) for a, b in zip(held, after)]
        inner = [pick_lanes(jnp.where(low_half, a, b), weave_u) for a, b in zip(even, odd)]
        image = [pick_lanes(jnp.where(low_half, b, a), weave_v) for a, b in zip(even, odd)]
        results = []
        for i, z in enumerate(layer):
            for c in range(3):
                where = pl.ds((c * ZN + z) * YN, YN)
                uu, vv = u[where, :], v[where, :]
                square = uu * uu * mass[i]
                results.append(
                    (
                        where,
                        inner[3 * i + c] + 0.1 * square * uu - external[where, :],
                        image[3 * i + c] + 0.3 * square * vv,
                    )
                )
        for where, res, tan in results:
            residual[where, :] = res
            tangent[where, :] = tan
    last[...] = sent


def slot_kernel(quads, faces, kin, selector):
    slot_faces = faces[...]
    face_ids = lax.broadcasted_iota(I32, (FACES, 128), 0) + 1
    for c in range(CHUNKS):
        slot_face = slot_faces[c : c + 1]
        index = jnp.maximum(jnp.broadcast_to(slot_face, (8, 128)) - 1, 0)
        inside, outside = index & 127, index >= 128
        for i in range(7):
            kin[c, pl.ds(i * 8, 8), :] = jnp.where(
                outside,
                pick_lanes(quads[pl.ds(i * 8, 8), 128:256], inside),
                pick_lanes(quads[pl.ds(i * 8, 8), 0:128], inside),
            )
        selector[:, c * 128 : (c + 1) * 128] = jnp.where(face_ids == slot_face, 1.0, 0.0).astype(BF16)


def contact_kernel(replies, kin, selector, fixed, left, u, v, res_in, tan_in, residual, tangent):
    values_h, values_l = [], []
    records = swap_groups([[replies[g * CHUNKS + c] for g in range(4)] for c in range(CHUNKS)])
    for c in range(CHUNKS):
        m = records[c]

        def point(m0, m1, m2, k):
            gap = m0 + m1 * k[0] + m2 * k[1] + k[2]
            scaled = -2.0 * gap
            small = jnp.exp(-jnp.abs(scaled))
            pressure = 2.0 * (jnp.maximum(scaled, 0.0) + jnp.log1p(small))
            slope = 4.0 * jnp.where(scaled >= 0.0, 1.0, small) / (1.0 + small)
            push = slope * (m1 * k[3] + m2 * k[4] + k[5])
            return pressure * m1, pressure * m2, pressure, push * m1, push * m2, push

        main = point(m[0], m[1], m[2], [kin[c, pl.ds(i * 8, 8), :] for i in range(6)])
        ends = kin[c, pl.ds(48, 8), :]
        ninth = point(m[3][0:1], m[3][1:2], m[3][2:3], [ends[i : i + 1] for i in range(6)])
        stack = jnp.concatenate(list(main) + list(ninth) + [jnp.zeros((10, 128), F32)], axis=0)
        high, low = split(stack)
        values_h.append(high)
        values_l.append(low)
    values = jnp.concatenate(
        [jnp.concatenate(values_h, axis=1), jnp.concatenate(values_l, axis=1)], axis=0
    )
    sums = mm_nt(values, selector[...])
    sums = sums[0:64] + sums[64:128]
    sums = jnp.concatenate([sums[:, 0:64], sums[:, 64:128], sums[:, 128:192]], axis=0)
    along = mm3(split(sums), (fixed[0:64, 0:384], fixed[64:128, 0:384]))
    tall = split(jnp.concatenate([along[:, i * 128 : (i + 1) * 128] for i in range(3)], axis=0))
    plane = mm3((fixed[128:176, :], fixed[176:224, :]), tall)
    at_first = lane_ids(8) == 0
    came = left[...]
    for z in range(ZN):
        mass = pltpu.roll(came, 80 - z, 1)
        for c in range(3):
            where = pl.ds((c * ZN + z) * YN, YN)
            uu, vv = u[where, :], v[where, :]
            square = uu * uu * mass
            spot = c * 16 + z
            inner = came if spot == 0 else pltpu.roll(came, 128 - spot, 1)
            image = pltpu.roll(came, 64 - spot, 1)
            res = res_in[where, :] + jnp.where(at_first, inner + 0.1 * square * uu, 0.0)
            tan = tan_in[where, :] + jnp.where(at_first, image + 0.3 * square * vv, 0.0)
            if z == 0:
                res = res + plane[c * 8 : c * 8 + 8]
                tan = tan + plane[24 + c * 8 : 32 + c * 8]
            residual[where, :] = res
            tangent[where, :] = tan


def call(body, outs, scratch=(), smem=(), hbm=(), flops=0, n=0, limit=44, **more):
    places = [pltpu.SMEM if i in smem else pl.ANY if i in hbm else pltpu.VMEM for i in range(n)]
    specs = [pl.BlockSpec(memory_space=place) for place in places]
    return pl.pallas_call(
        body,
        out_shape=tuple(jax.ShapeDtypeStruct(s, t) for s, t in outs),
        in_specs=specs,
        out_specs=tuple(pl.BlockSpec(memory_space=pltpu.VMEM) for _ in outs),
        scratch_shapes=list(scratch),
        cost_estimate=pl.CostEstimate(flops=flops, bytes_accessed=0, transcendentals=0),
        compiler_params=pltpu.CompilerParams(vmem_limit_bytes=limit << 20),
        **more,
    )


def ring(values, axis, up):
    count = lax.axis_size(axis)
    pairs = [(i, (i + 1) % count) if up else ((i + 1) % count, i) for i in range(count)]
    return lax.ppermute(values, axis, pairs)


def local(
    displacement,
    direction,
    modulus,
    external,
    stiffness,
    master_record,
    pair_face,
    pair_owner,
    pair_row,
    pair_count,
):
    u = displacement.reshape(3 * ZN * YN, XN)
    v = direction.reshape(3 * ZN * YN, XN)
    m = modulus.reshape(ZN * YN, XN)
    request, faces, z_up, z_down = call(
        request_kernel,
        [((OWNERS, 128), I32), ((CHUNKS, 128), I32), ((7, 2, YN, XN), F32), ((7, 1, YN, XN), F32)],
        scratch=[pltpu.SemaphoreType.DMA((6,))], smem=(3,), hbm=(4, 5, 6), n=7, limit=63,
    )(
        pair_owner.reshape(8, 128), pair_row.reshape(8, 128), pair_face.reshape(8, 128), pair_count,
        displacement, direction, modulus,
    )
    z_low = ring(z_up, "gz", True).reshape(7 * 2 * YN, XN)
    z_high = ring(z_down, "gz", False).reshape(7 * YN, XN)
    ids = lax.all_to_all(request, GROUPS, split_axis=0, concat_axis=0, tiled=True)

    big_h, big_l, table, quads = call(
        prepare_kernel,
        [((BLOCK, BLOCK), BF16), ((BLOCK, BLOCK), BF16), ((32, ROWS), F32), ((56, 256), F32)],
        n=5,
    )(u, v, stiffness, master_record, jnp.asarray(prepare_constants()))
    kin, selector = call(
        slot_kernel, [((CHUNKS, 56, 128), F32), ((FACES, OWNERS * CAP), BF16)], n=2
    )(quads, faces)
    y_up, y_down = call(side_kernel, [((7 * 2 * 24, XN), F32), ((7 * 24, XN), F32)], n=5)(
        u, v, m, z_low, z_high
    )
    y_low = ring(y_up, "gy", True)
    y_high = ring(y_down, "gy", False)

    (reply,) = call(gather_kernel, [((OWNERS, 8, 128), F32)], n=2, flops=1 << 20)(ids, table)
    (x_down,) = call(edge_kernel, [((16, 128), F32)], n=7)(u, v, m, z_low, z_high, y_low, y_high)
    x_high = ring(x_down, "gx", False)
    replies = lax.all_to_all(reply, GROUPS, split_axis=0, concat_axis=0, tiled=True)

    edges = jnp.stack([lax.axis_index(a).astype(I32) for a in ("gz", "gy", "gx")])
    residual, tangent, last = call(
        element_kernel,
        [((3 * ZN * YN, XN), F32), ((3 * ZN * YN, XN), F32), ((8, 128), F32)],
        scratch=[
            pltpu.VMEM((NODE_ROWS, 128), F32),
            pltpu.VMEM((NODE_ROWS, 128), BF16),
            pltpu.VMEM((NODE_ROWS, 128), BF16),
            pltpu.VMEM((NODE_ROWS, 128), F32),
        ],
        smem=(0,), n=12, flops=1 << 33,
    )(
        edges, u, v, m, external.reshape(3 * ZN * YN, XN), z_low, z_high, y_low, y_high, x_high,
        big_h, big_l,
    )
    left = ring(last, "gx", True)
    residual, tangent = call(
        contact_kernel, [((3 * ZN * YN, XN), F32), ((3 * ZN * YN, XN), F32)], n=9, flops=1 << 20
    )(replies, kin, selector, jnp.asarray(contact_constants()), left, u, v, residual, tangent)
    return residual.reshape(3, ZN, YN, XN), tangent.reshape(3, ZN, YN, XN)


def solution(mesh):
    placed = (
        P(None, "gz", "gy", "gx"),
        P(None, "gz", "gy", "gx"),
        P("gz", "gy", "gx"),
        P(None, "gz", "gy", "gx"),
        P(),
        P(None, ("gx", "gy", "gz")),
        P(("gx", "gy", "gz")),
        P(("gx", "gy", "gz"), None),
        P(("gx", "gy", "gz")),
        P(("gx", "gy", "gz")),
    )
    return jax.shard_map(
        local,
        mesh=mesh,
        in_specs=placed,
        out_specs=(P(None, "gz", "gy", "gx"), P(None, "gz", "gy", "gx")),
        check_vma=False,
    )
```

time: 71 us -> 56.7 us (0.80)
  local copies, waits for them, and re-layouts: 12.8 us -> 0.05 us
  Pallas kernels: 19.7 us -> 12.8 us
  waiting for transfers between devices: 12.2 us -> 18 us
    unnamed x54 -> x18, local copies, waits for them, and re-layouts: 12.8 us -> 0.05 us
    pallas_call x5 -> x7, Pallas kernels: 16.6 us -> 10.7 us  [the longest x1 4.32 us: local(): call(element_kernel, [((3 * ZN * YN, XN), F32), ((3 * ZN * YN, XN), F32),...]
    ppermute x6, waiting for transfers between devices: 3.27 us -> 7.25 us  [ring(): return lax.ppermute(values, axis, pairs)]
    all_to_all x1, waiting for transfers between devices: 2.75 us -> 5.23 us  [local(): lax.all_to_all(reply, GROUPS, split_axis=0, concat_axis=0, tiled=True)]
    pallas_call x1, Pallas kernels: 3.09 us -> 2.1 us  [local(): call(gather_kernel, [((OWNERS, 8, 128), F32)], n=2, flops=1 << 20)]
  transfers between devices with their start and end apart: 8 -> 8, of which waited for: 3 -> 4; matrix products, arithmetic and copies ran while one was open for 0% -> 0% of each run, Pallas kernels for 21% -> 14%
where the time goes in v2:
time: 56.7 us; the launch traced here: 56.4 us
  starting transfers between devices  24 us (42%)
  waiting for transfers between devices  18 us (32%)
  Pallas kernels  12.8 us (23%)
  between operations  1.47 us (3%)
    all_to_all x1, starting transfers between devices, local(): lax.all_to_all(request, GROUPS, split_axis=0, concat_axis=0, tiled=True)  10.7 us
    ppermute x6, starting transfers between devices, ring(): return lax.ppermute(values, axis, pairs)  8.5 us
    ppermute x6, waiting for transfers between devices, ring(): return lax.ppermute(values, axis, pairs)  7.25 us
    all_to_all x1, waiting for transfers between devices, local(): lax.all_to_all(request, GROUPS, split_axis=0, concat_axis=0, tiled=True)  5.56 us
    all_to_all x1, waiting for transfers between devices, local(): lax.all_to_all(reply, GROUPS, split_axis=0, concat_axis=0, tiled=True)  5.23 us
    all_to_all x1, starting transfers between devices, local(): lax.all_to_all(reply, GROUPS, split_axis=0, concat_axis=0, tiled=True)  4.74 us
    pallas_call x1, Pallas kernels, local(): call(element_kernel, [((3 * ZN * YN, XN), F32), ((3 * ZN * YN, XN), F32),...  4.32 us
    pallas_call x1, Pallas kernels, local(): call(request_kernel, [((OWNERS, 128), I32), ((CHUNKS, 128), I32), ((7, 2,...  2.79 us
  transfers between devices with their start and end apart: 8, of which 4 were waited for; matrix products, arithmetic and copies ran while one was open for 0% of the time, Pallas kernels for 14%

profile of v2, /device:TPU:8, one launch (start us, length us, event | category | flops | bytes accessed | tf_op | source)
XLA Modules:
  0.0 56.4 jit_solution(925606705468120169)
XLA Ops:
  1.3 0.0 copy-start
  1.3 0.0 copy-start.1
  1.3 0.0 copy-start.3
  1.3 2.8 %shard_map.131 = (s32[64,128]{1,0:T(8,128)}, s32[16,128]{1,0:T(8,128)}, f32[7,2,8,128]{3,2,1,0:T(8,128)}, f32[7,1,8,128]{3,2,1,0:T(8,128)}) custom-call(s32[8,128]{1,0:T(8,128)} %bitcast.40, s32[8,128]{1,0:T(8,128)} %bitcast.41, s32[8,128]{1,0:T(8,128)} %bitcast.42, s32[1]{0:T(128)S(6)} %copy.15.count, f32[3,16,8,128]{3,2,1,0:T(8,128)} %u.1, ...), custom_call_target="tpu_custom_call" | custom-call | tf_op jit(solution)/shard_map/pallas_call | solution.py:608
  4.1 0.0 copy-start.2
  4.1 1.7 %collective-permute-start = (f32[7,2,8,128]{3,2,1,0:T(8,128)}, f32[7,2,8,128]{3,2,1,0:T(8,128)S(1)}, u32[]{:S(2)}, u32[]{:S(2)}) collective-permute-start(f32[7,2,8,128]{3,2,1,0:T(8,128)} %get-tuple-element.25), channel_id=1, source_target_pairs={{0,1},{1,2},{2,3},{3,0},{4,5},{5,6},{6,7},{7,4},{8,9},{9,10},{10,1... | collective-permute-start | bytes 172040 | tf_op jit(solution)/shard_map/ppermute | solution.py:590
  5.8 0.7 %collective-permute-start.1 = (f32[7,1,8,128]{3,2,1,0:T(8,128)}, f32[7,1,8,128]{3,2,1,0:T(8,128)S(1)}, u32[]{:S(2)}, u32[]{:S(2)}) collective-permute-start(f32[7,1,8,128]{3,2,1,0:T(8,128)} %get-tuple-element.26), channel_id=1, source_target_pairs={{1,0},{2,1},{3,2},{0,3},{5,4},{6,5},{7,6},{4,7},{9,8},{10,9},{11,1... | collective-permute-start | bytes 86024 | tf_op jit(solution)/shard_map/ppermute | solution.py:590
  6.5 3.4 %collective-permute-done.1 = f32[7,1,8,128]{3,2,1,0:T(8,128)S(1)} collective-permute-done((f32[7,1,8,128]{3,2,1,0:T(8,128)}, f32[7,1,8,128]{3,2,1,0:T(8,128)S(1)}, u32[]{:S(2)}, u32[]{:S(2)}) %collective-permute-start.1) | collective-permute-done | bytes 28704 | tf_op jit(solution)/shard_map/ppermute | solution.py:590
  9.9 0.0 collective-permute-done
  9.9 0.0 copy-done
  9.9 0.0 copy-done.1
  9.9 0.0 copy-done.3
  9.9 0.1 shard_map.135
  9.9 1.6 %collective-permute-start.2 = (f32[336,128]{1,0:T(8,128)S(1)}, f32[336,128]{1,0:T(8,128)S(1)}, u32[]{:S(2)}, u32[]{:S(2)}) collective-permute-start(f32[336,128]{1,0:T(8,128)S(1)} %get-tuple-element.27), channel_id=1, source_target_pairs={{0,4},{4,8},{8,12},{12,0},{1,5},{5,9},{9,13},{13,1},{2,6},{6,10},{... | collective-permute-start | bytes 516104 | tf_op jit(solution)/shard_map/ppermute | solution.py:590
  11.5 1.7 %collective-permute-start.3 = (f32[168,128]{1,0:T(8,128)S(1)}, f32[168,128]{1,0:T(8,128)S(1)}, u32[]{:S(2)}, u32[]{:S(2)}) collective-permute-start(f32[168,128]{1,0:T(8,128)S(1)} %get-tuple-element.28), channel_id=1, source_target_pairs={{4,0},{8,4},{12,8},{0,12},{5,1},{9,5},{13,9},{1,13},{6,2},{10,6},{... | collective-permute-start | bytes 258056 | tf_op jit(solution)/shard_map/ppermute | solution.py:590
  13.3 10.7 %all-to-all-start = ((s32[64,1,128]{2,1,0:T(1,128)}), s32[64,1,128]{2,1,0:T(1,128)S(1)}, u32[]{:S(2)}, u32[]{:S(2)}) async-start(s32[64,1,128]{2,1,0:T(1,128)} %bitcast.39), calls=%async_computation | async-start | bytes 65536 | tf_op jit(solution)/shard_map/all_to_all | solution.py:618
  24.0 0.0 copy-start.5
  24.0 0.0 copy-start.6
  24.0 0.0 collective-permute-done.3.y_high
  24.0 0.0 collective-permute-done.2.y_low
  24.0 0.3 shard_map.136
  24.3 2.8 %collective-permute-start.4 = (f32[16,128]{1,0:T(8,128)S(1)}, f32[16,128]{1,0:T(8,128)S(1)}, u32[]{:S(2)}, u32[]{:S(2)}) collective-permute-start(f32[16,128]{1,0:T(8,128)S(1)} %shard_map.136), channel_id=1, source_target_pairs={{16,0},{32,16},{48,32},{64,48},{80,64},{96,80},{112,96},{128,112},... | collective-permute-start | bytes 24584 | tf_op jit(solution)/shard_map/ppermute | solution.py:590
  27.2 0.1 pad_add_fusion.edges
  27.2 0.0 copy-done.2
  27.2 0.0 copy-done.5
  27.2 0.0 copy-done.6
  27.3 0.7 %shard_map.132 = (bf16[144,144]{1,0:T(8,128)(2,1)S(1)}, bf16[144,144]{1,0:T(8,128)(2,1)S(1)}, f32[32,2048]{1,0:T(8,128)S(1)}, f32[56,256]{1,0:T(8,128)S(1)}) custom-call(f32[384,128]{1,0:T(8,128)S(1)} %bitcast.20, f32[384,128]{1,0:T(8,128)S(1)} %bitcast.25, f32[81,81]{1,0:T(8,128)S(1)} %copy-done.6, f32[27,2048]{1,0:T(8,128)S(1)} %copy-done.5, ...), custom_call_target="tpu_custom_call" | custom-call | tf_op jit(solution)/shard_map/pallas_call | solution.py:620
  28.0 5.6 %all-to-all-done = s32[64,1,128]{2,1,0:T(1,128)S(1)} async-done(((s32[64,1,128]{2,1,0:T(1,128)}), s32[64,1,128]{2,1,0:T(1,128)S(1)}, u32[]{:S(2)}, u32[]{:S(2)}) %all-to-all-start) | async-done | bytes 32800 | tf_op jit(solution)/shard_map/all_to_all | solution.py:618
  33.6 2.1 %shard_map.133 = f32[64,8,128]{2,1,0:T(8,128)} custom-call(s32[64,128]{1,0:T(8,128)S(1)} %bitcast.34, f32[32,2048]{1,0:T(8,128)S(1)} %get-tuple-element.20.table), custom_call_target="tpu_custom_call" | custom-call | flops 1048576 | tf_op jit(solution)/shard_map/pallas_call | solution.py:634
  35.7 0.0 copy-start.8
  35.7 4.7 %all-to-all-start.1 = ((f32[64,8,128]{2,1,0:T(8,128)}), f32[64,8,128]{2,1,0:T(8,128)S(1)}, u32[]{:S(2)}, u32[]{:S(2)}) async-start(f32[64,8,128]{2,1,0:T(8,128)} %shard_map.133), calls=%async_computation.1 | async-start | bytes 524288 | tf_op jit(solution)/shard_map/all_to_all | solution.py:637
  40.4 0.0 collective-permute-done.4.x_high
  40.4 0.0 copy-done.8
  40.4 0.0 copy-start.7
  40.4 0.0 copy-start.4
  40.5 4.3 %shard_map.137 = (f32[384,128]{1,0:T(8,128)S(1)}, f32[384,128]{1,0:T(8,128)S(1)}, f32[8,128]{1,0:T(8,128)S(1)}) custom-call(s32[3]{0:T(128)S(1)} %pad_add_fusion.edges, f32[384,128]{1,0:T(8,128)S(1)} %bitcast.21, f32[384,128]{1,0:T(8,128)S(1)} %bitcast.26, f32[128,128]{1,0:T(8,128)S(1)} %bitcast.30, f32[384,128]{1,0:T(8,128)S(1)} %bitcast.38, ...), custom_call_target="tpu_custom_call" | custom-call | flops 8589934592 | tf_op jit(solution)/shard_map/pallas_call | solution.py:640
  44.8 0.0 collective-permute-start.5
  44.8 0.0 copy-done.7
  44.8 0.4 shard_map.134
  45.3 3.9 %collective-permute-done.5.left = f32[8,128]{1,0:T(8,128)S(1)} collective-permute-done((f32[8,128]{1,0:T(8,128)S(1)}, f32[8,128]{1,0:T(8,128)S(1)}, u32[]{:S(2)}, u32[]{:S(2)}) %collective-permute-start.5) | collective-permute-done | bytes 4128 | tf_op jit(solution)/shard_map/ppermute | solution.py:590
  49.1 5.2 %all-to-all-done.1.replies = f32[64,8,128]{2,1,0:T(8,128)S(1)} async-done(((f32[64,8,128]{2,1,0:T(8,128)}), f32[64,8,128]{2,1,0:T(8,128)S(1)}, u32[]{:S(2)}, u32[]{:S(2)}) %all-to-all-start.1) | async-done | bytes 262176 | tf_op jit(solution)/shard_map/all_to_all | solution.py:637
  54.4 0.0 copy-done.4
  54.4 2.0 %shard_map.138 = (f32[384,128]{1,0:T(8,128)}, f32[384,128]{1,0:T(8,128)}) custom-call(f32[64,8,128]{2,1,0:T(8,128)S(1)} %all-to-all-done.1.replies, f32[16,56,128]{2,1,0:T(8,128)S(1)} %get-tuple-element.23.kin, bf16[192,2048]{1,0:T(8,128)(2,1)S(1)} %get-tuple-element.24.selector, bf16[224,576]{1,0:T(8,128)(2,1)S(1)} %copy-done.4, ...), custom_call_target="tpu_custom_call" | custom-call | flops 1048576 | tf_op jit(solution)/shard_map/pallas_call | solution.py:655
Async XLA Ops:
  1.3 8.6 %copy-start = (f32[3,16,8,128]{3,2,1,0:T(8,128)S(1)}, f32[3,16,8,128]{3,2,1,0:T(8,128)}, u32[]{:S(2)}) copy-start(f32[3,16,8,128]{3,2,1,0:T(8,128)} %u.1) | copy-start | bytes 589828
  1.3 8.6 %copy-start.1 = (f32[3,16,8,128]{3,2,1,0:T(8,128)S(1)}, f32[3,16,8,128]{3,2,1,0:T(8,128)}, u32[]{:S(2)}) copy-start(f32[3,16,8,128]{3,2,1,0:T(8,128)} %v.1) | copy-start | bytes 589828
  1.3 8.6 %copy-start.3 = (f32[16,8,128]{2,1,0:T(8,128)S(1)}, f32[16,8,128]{2,1,0:T(8,128)}, u32[]{:S(2)}) copy-start(f32[16,8,128]{2,1,0:T(8,128)} %m.1) | copy-start | bytes 196612
  4.1 23.1 %copy-start.2 = (bf16[560,768]{1,0:T(8,128)(2,1)S(1)}, bf16[560,768]{1,0:T(8,128)(2,1)}, u32[]{:S(2)}) copy-start(bf16[560,768]{1,0:T(8,128)(2,1)} %constant.16.clone.fixed) | copy-start | bytes 2580484
  4.1 5.7 %collective-permute-start = (f32[7,2,8,128]{3,2,1,0:T(8,128)}, f32[7,2,8,128]{3,2,1,0:T(8,128)S(1)}, u32[]{:S(2)}, u32[]{:S(2)}) collective-permute-start(f32[7,2,8,128]{3,2,1,0:T(8,128)} %get-tuple-element.25), channel_id=1, source_target_pairs={{0,1},{1,2},{2,3},{3,0},{4,5},{5,6},{6,7},{7,4},{8,9},{9,10},{10,1... | collective-permute-start | bytes 172040 | tf_op jit(solution)/shard_map/ppermute | solution.py:590
  5.8 4.1 %collective-permute-start.1 = (f32[7,1,8,128]{3,2,1,0:T(8,128)}, f32[7,1,8,128]{3,2,1,0:T(8,128)S(1)}, u32[]{:S(2)}, u32[]{:S(2)}) collective-permute-start(f32[7,1,8,128]{3,2,1,0:T(8,128)} %get-tuple-element.26), channel_id=1, source_target_pairs={{1,0},{2,1},{3,2},{0,3},{5,4},{6,5},{7,6},{4,7},{9,8},{10,9},{11,1... | collective-permute-start | bytes 86024 | tf_op jit(solution)/shard_map/ppermute | solution.py:590
  9.9 14.1 %collective-permute-start.2 = (f32[336,128]{1,0:T(8,128)S(1)}, f32[336,128]{1,0:T(8,128)S(1)}, u32[]{:S(2)}, u32[]{:S(2)}) collective-permute-start(f32[336,128]{1,0:T(8,128)S(1)} %get-tuple-element.27), channel_id=1, source_target_pairs={{0,4},{4,8},{8,12},{12,0},{1,5},{5,9},{9,13},{13,1},{2,6},{6,10},{... | collective-permute-start | bytes 516104 | tf_op jit(solution)/shard_map/ppermute | solution.py:590
  11.5 12.5 %collective-permute-start.3 = (f32[168,128]{1,0:T(8,128)S(1)}, f32[168,128]{1,0:T(8,128)S(1)}, u32[]{:S(2)}, u32[]{:S(2)}) collective-permute-start(f32[168,128]{1,0:T(8,128)S(1)} %get-tuple-element.28), channel_id=1, source_target_pairs={{4,0},{8,4},{12,8},{0,12},{5,1},{9,5},{13,9},{1,13},{6,2},{10,6},{... | collective-permute-start | bytes 258056 | tf_op jit(solution)/shard_map/ppermute | solution.py:590
  13.3 20.3 %all-to-all-start = ((s32[64,1,128]{2,1,0:T(1,128)}), s32[64,1,128]{2,1,0:T(1,128)S(1)}, u32[]{:S(2)}, u32[]{:S(2)}) async-start(s32[64,1,128]{2,1,0:T(1,128)} %bitcast.39), calls=%async_computation | async-start | bytes 65536 | tf_op jit(solution)/shard_map/all_to_all | solution.py:618
  24.0 3.3 %copy-start.5 = (f32[27,2048]{1,0:T(8,128)S(1)}, f32[27,2048]{1,0:T(8,128)}, u32[]{:S(2)}) copy-start(f32[27,2048]{1,0:T(8,128)} %master.1) | copy-start | bytes 663556
  24.0 3.2 %copy-start.6 = (f32[81,81]{1,0:T(8,128)S(1)}, f32[81,81]{1,0:T(8,128)}, u32[]{:S(2)}) copy-start(f32[81,81]{1,0:T(8,128)} %stiffness.1) | copy-start | bytes 78736
  24.3 16.1 %collective-permute-start.4 = (f32[16,128]{1,0:T(8,128)S(1)}, f32[16,128]{1,0:T(8,128)S(1)}, u32[]{:S(2)}, u32[]{:S(2)}) collective-permute-start(f32[16,128]{1,0:T(8,128)S(1)} %shard_map.136), channel_id=1, source_target_pairs={{16,0},{32,16},{48,32},{64,48},{80,64},{96,80},{112,96},{128,112},... | collective-permute-start | bytes 24584 | tf_op jit(solution)/shard_map/ppermute | solution.py:590
  35.7 4.8 %copy-start.8 = (f32[3,16,8,128]{3,2,1,0:T(8,128)S(1)}, f32[3,16,8,128]{3,2,1,0:T(8,128)}, u32[]{:S(2)}) copy-start(f32[3,16,8,128]{3,2,1,0:T(8,128)} %param.15) | copy-start | bytes 589828
  35.7 18.7 %all-to-all-start.1 = ((f32[64,8,128]{2,1,0:T(8,128)}), f32[64,8,128]{2,1,0:T(8,128)S(1)}, u32[]{:S(2)}, u32[]{:S(2)}) async-start(f32[64,8,128]{2,1,0:T(8,128)} %shard_map.133), calls=%async_computation.1 | async-start | bytes 524288 | tf_op jit(solution)/shard_map/all_to_all | solution.py:637
  40.4 4.4 %copy-start.7 = (s32[16,128]{1,0:T(8,128)S(1)}, s32[16,128]{1,0:T(8,128)}, u32[]{:S(2)}) copy-start(s32[16,128]{1,0:T(8,128)} %get-tuple-element.22.faces) | copy-start | bytes 24580
  40.4 13.9 %copy-start.4 = (bf16[224,576]{1,0:T(8,128)(2,1)S(1)}, bf16[224,576]{1,0:T(8,128)(2,1)}, u32[]{:S(2)}) copy-start(bf16[224,576]{1,0:T(8,128)(2,1)} %constant.17.clone.fixed) | copy-start | bytes 774148
  44.8 4.3 %collective-permute-start.5 = (f32[8,128]{1,0:T(8,128)S(1)}, f32[8,128]{1,0:T(8,128)S(1)}, u32[]{:S(2)}, u32[]{:S(2)}) collective-permute-start(f32[8,128]{1,0:T(8,128)S(1)} %get-tuple-element.31), channel_id=1, source_target_pairs={{0,16},{16,32},{32,48},{48,64},{64,80},{80,96},{96,112},{112,128},... | collective-permute-start | bytes 12296 | tf_op jit(solution)/shard_map/ppermute | solution.py:590

commit v3 on v2

--- a/solution.py
+++ b/solution.py
@@ -24,7 +24,6 @@
 BLOCK = 9 * TILE
 GROUPS = ("gx", "gy")
 GROUP = 14
-GATHERED = 16
 
 
 def shapes_1d():
@@ -135,17 +134,24 @@
     return out
 
 
-def prepare_constants():
+def element_constants():
     place, fixed = stiffness_places()
-    record, along = record_map(), face_x_map()
+    return packed([(0, 0, fixed[0]), (0, 256, fixed[1]), (0, 512, place.astype(jnp.bfloat16))], 144, 640)
+
+
+def slot_constants():
+    along = face_x_map()
     first, second = face_y_map()
     pieces = [
         (0, 0, along[0]), (128, 0, along[1]),
         (256, 0, first[0]), (256, 384, second[0]), (320, 0, first[1]), (320, 384, second[1]),
-        (384, 0, fixed[0]), (384, 256, fixed[1]), (384, 512, place.astype(jnp.bfloat16)),
-        (528, 0, record[0]), (528, 128, record[1]),
     ]
-    return packed(pieces, 560, 768)
+    return packed(pieces, 384, 768)
+
+
+def table_constants():
+    high, low = record_map()
+    return packed([(0, 0, high), (0, 128, low)], 32, 256)
 
 
 def contact_constants():
@@ -204,7 +210,16 @@
     ]
 
 
-def request_kernel(owner, row, face, count, u, v, m, request, faces, z_up, z_down, arrived):
+def request_kernel(
+    owners, rows, sides_in, counts, u, v, m, request, faces, z_up, z_down,
+    owner, row, face, arrived,
+):
+    first = [
+        pltpu.make_async_copy(source, to, arrived.at[6 + i])
+        for i, (source, to) in enumerate(((owners, owner), (rows, row), (sides_in, face)))
+    ]
+    for copy in first:
+        copy.start()
     layers = []
     for i, (to, start, size) in enumerate(((z_up, ZN - 2, 2), (z_down, 0, 1))):
         part = pl.ds(start, size)
@@ -215,7 +230,9 @@
         ]
     for copy in layers:
         copy.start()
-    live_count = count[0]
+    for copy in first:
+        copy.wait()
+    live_count = counts[...]
     who = lax.broadcasted_iota(I32, (OWNERS, 128), 0)
     lane = lane_ids(1)
     hits = []
@@ -262,45 +279,37 @@
                 out[pl.ds(at + 18, 1), :] = z_high[pl.ds(n * YN + y, 1), :]
 
 
-def prepare_kernel(u, v, stiffness, master, fixed, big_h, big_l, table, quads):
-    places = fixed[384:528, 512:593]
+def table_kernel(master, fixed, table):
+    table[...] = mm3((fixed[:, 0:27], fixed[:, 128:155]), split(master[...]))
+
+
+def stiffness_pair(stiffness, fixed):
+    places = fixed[:, 512:593]
     high, low = split(stiffness[...])
     lower = (stiffness[...] - high.astype(F32) - low.astype(F32)).astype(BF16)
     spread = [mm_nt(mm(places, part).astype(BF16), places) for part in (high, low, lower)]
     high, low = split((spread[0] + spread[1]) + spread[2])
-    big_h[...] = high + fixed[384:528, 0:144]
-    big_l[...] = low + fixed[384:528, 256:400]
-    table[...] = mm3((fixed[528:560, 0:27], fixed[528:560, 128:155]), split(master[...]))
-    plane = jnp.concatenate(
-        [field[pl.ds(c * ZN * YN, YN), :] for field in (u, v) for c in range(3)], axis=0
-    )
-    wide = mm3(split(plane), (fixed[0:128, :], fixed[128:256, :]))
-    tall = split(jnp.concatenate([wide[:, i * 128 : (i + 1) * 128] for i in range(6)], axis=0))
-    for first, to in ((0, 0), (384, 128)):
-        pair = fixed[256:312, first : first + 288], fixed[320:376, first : first + 288]
-        quads[:, to : to + 128] = mm3(pair, tall)
+    return high + fixed[:, 0:144], low + fixed[:, 256:400]
 
 
 def gather_kernel(ids, table, reply):
     numbers = jnp.maximum(compact(ids[...]) - 1, 0)
-    for base in range(0, CHUNKS, GATHERED):
-        found = []
-        for c in range(base, base + GATHERED):
-            number = jnp.broadcast_to(numbers[c : c + 1], (8, 128))
-            inside = number & 127
-            outside = lax.shift_right_logical(number, 7)
-            parts = []
-            for f in range(4):
-                total = pick_lanes(table[pl.ds(f * 8, 8), 0:128], inside)
-                for k in range(1, ROWS // 128):
-                    piece = pick_lanes(table[pl.ds(f * 8, 8), k * 128 : (k + 1) * 128], inside)
-                    total = jnp.where(outside == k, piece, total)
-                parts.append(total)
-            found.append(parts)
-        tiles = swap_groups(found)
-        for i in range(GATHERED):
-            for g in range(4):
-                reply[g * CHUNKS + base + i] = tiles[i][g]
+    found = []
+    for c in range(CHUNKS):
+        number = jnp.broadcast_to(numbers[c : c + 1], (8, 128))
+        inside = number & 127
+        outside = lax.shift_right_logical(number, 7)
+        parts = []
+        for f in range(4):
+            total = pick_lanes(table[pl.ds(f * 8, 8), 0:128], inside)
+            for k in range(1, ROWS // 128):
+                piece = pick_lanes(table[pl.ds(f * 8, 8), k * 128 : (k + 1) * 128], inside)
+                total = jnp.where(outside == k, piece, total)
+            parts.append(total)
+        found.append(parts)
+    for c, tiles in enumerate(swap_groups(found)):
+        for g in range(4):
+            reply[g * CHUNKS + c] = tiles[g]
 
 
 def slab(fields, halos, n, s):
@@ -317,7 +326,7 @@
     return y_high[pl.ds(n * 24 + zb * 8, 8), :]
 
 
-def edge_kernel(u, v, m, z_low, z_high, y_low, y_high, x_down):
+def edge_kernel(u, v, m, z_low, z_high, y_low, y_high, reply_in, x_down, reply_out):
     fields, halos = (u, v, m), (z_low, z_high, y_low, y_high)
     lane = lane_ids(8)
     down = [jnp.zeros((8, 128), F32) for _ in range(2)]
@@ -334,7 +343,7 @@
 
 
 def element_kernel(
-    edges, u, v, m, external, z_low, z_high, y_low, y_high, x_high, big_h, big_l,
+    edges, u, v, m, external, z_low, z_high, y_low, y_high, x_high, stiffness, fixed,
     residual, tangent, last, nodes, tiles_h, tiles_l, total,
 ):
     fields, halos = (u, v, m), (z_low, z_high, y_low, y_high)
@@ -403,7 +412,7 @@
     y_last = jnp.where(edges[1] == lax.axis_size("gy") - 1, 3, 4)
     z_first = jnp.where(edges[0] == 0, 1, 0)
     z_last = jnp.where(edges[0] == lax.axis_size("gz") - 1, 7, 8)
-    left_high, left_low = big_h[...], big_l[...]
+    left_high, left_low = stiffness_pair(stiffness, fixed)
 
     total[pl.ds(0, ZPITCH), :] = jnp.zeros((ZPITCH, 128), F32)
 
@@ -502,7 +511,15 @@
     last[...] = sent
 
 
-def slot_kernel(quads, faces, kin, selector):
+def slot_kernel(u, v, faces, fixed, kin, selector, quads):
+    plane = jnp.concatenate(
+        [field[pl.ds(c * ZN * YN, YN), :] for field in (u, v) for c in range(3)], axis=0
+    )
+    wide = mm3(split(plane), (fixed[0:128, :], fixed[128:256, :]))
+    tall = split(jnp.concatenate([wide[:, i * 128 : (i + 1) * 128] for i in range(6)], axis=0))
+    for first, to in ((0, 0), (384, 128)):
+        pair = fixed[256:312, first : first + 288], fixed[320:376, first : first + 288]
+        quads[:, to : to + 128] = mm3(pair, tall)
     slot_faces = faces[...]
     face_ids = lax.broadcasted_iota(I32, (FACES, 128), 0) + 1
     for c in range(CHUNKS):
@@ -569,17 +586,22 @@
             tangent[where, :] = tan
 
 
-def call(body, outs, scratch=(), smem=(), hbm=(), flops=0, n=0, limit=44, **more):
-    places = [pltpu.SMEM if i in smem else pl.ANY if i in hbm else pltpu.VMEM for i in range(n)]
+def call(body, outs, scratch=(), smem=(), free=(), hbm=(), free_out=(), flops=0, n=0, limit=45056, **more):
+    places = [
+        pltpu.SMEM if i in smem else pl.ANY if i in free else pltpu.HBM if i in hbm else pltpu.VMEM
+        for i in range(n)
+    ]
     specs = [pl.BlockSpec(memory_space=place) for place in places]
     return pl.pallas_call(
         body,
         out_shape=tuple(jax.ShapeDtypeStruct(s, t) for s, t in outs),
         in_specs=specs,
-        out_specs=tuple(pl.BlockSpec(memory_space=pltpu.VMEM) for _ in outs),
+        out_specs=tuple(
+            pl.BlockSpec(memory_space=pl.ANY if i in free_out else pltpu.VMEM) for i in range(len(outs))
+        ),
         scratch_shapes=list(scratch),
         cost_estimate=pl.CostEstimate(flops=flops, bytes_accessed=0, transcendentals=0),
-        compiler_params=pltpu.CompilerParams(vmem_limit_bytes=limit << 20),
+        compiler_params=pltpu.CompilerParams(vmem_limit_bytes=limit << 10),
         **more,
     )
 
@@ -608,7 +630,11 @@
     request, faces, z_up, z_down = call(
         request_kernel,
         [((OWNERS, 128), I32), ((CHUNKS, 128), I32), ((7, 2, YN, XN), F32), ((7, 1, YN, XN), F32)],
-        scratch=[pltpu.SemaphoreType.DMA((6,))], smem=(3,), hbm=(4, 5, 6), n=7, limit=63,
+        scratch=[
+            pltpu.VMEM((8, 128), I32), pltpu.VMEM((8, 128), I32), pltpu.VMEM((8, 128), I32),
+            pltpu.SemaphoreType.DMA((9,)),
+        ],
+        hbm=(0, 1, 2, 4, 5, 6), n=7, limit=64512,
     )(
         pair_owner.reshape(8, 128), pair_row.reshape(8, 128), pair_face.reshape(8, 128), pair_count,
         displacement, direction, modulus,
@@ -617,22 +643,22 @@
     z_high = ring(z_down, "gz", False).reshape(7 * YN, XN)
     ids = lax.all_to_all(request, GROUPS, split_axis=0, concat_axis=0, tiled=True)
 
-    big_h, big_l, table, quads = call(
-        prepare_kernel,
-        [((BLOCK, BLOCK), BF16), ((BLOCK, BLOCK), BF16), ((32, ROWS), F32), ((56, 256), F32)],
-        n=5,
-    )(u, v, stiffness, master_record, jnp.asarray(prepare_constants()))
+    (table,) = call(table_kernel, [((32, ROWS), F32)], n=2)(master_record, jnp.asarray(table_constants()))
     kin, selector = call(
-        slot_kernel, [((CHUNKS, 56, 128), F32), ((FACES, OWNERS * CAP), BF16)], n=2
-    )(quads, faces)
+        slot_kernel, [((CHUNKS, 56, 128), F32), ((FACES, OWNERS * CAP), BF16)],
+        scratch=[pltpu.VMEM((56, 256), F32)], n=4,
+    )(u, v, faces, jnp.asarray(slot_constants()))
     y_up, y_down = call(side_kernel, [((7 * 2 * 24, XN), F32), ((7 * 24, XN), F32)], n=5)(
         u, v, m, z_low, z_high
     )
     y_low = ring(y_up, "gy", True)
     y_high = ring(y_down, "gy", False)
 
-    (reply,) = call(gather_kernel, [((OWNERS, 8, 128), F32)], n=2, flops=1 << 20)(ids, table)
-    (x_down,) = call(edge_kernel, [((16, 128), F32)], n=7)(u, v, m, z_low, z_high, y_low, y_high)
+    (reply,) = call(gather_kernel, [((OWNERS, 8, 128), F32)], n=2, flops=5 << 28)(ids, table)
+    x_down, reply = call(
+        edge_kernel, [((16, 128), F32), ((OWNERS, 8, 128), F32)], n=8, free=(7,), free_out=(1,),
+        input_output_aliases={7: 1},
+    )(u, v, m, z_low, z_high, y_low, y_high, reply)
     x_high = ring(x_down, "gx", False)
     replies = lax.all_to_all(reply, GROUPS, split_axis=0, concat_axis=0, tiled=True)
 
@@ -649,7 +675,7 @@
         smem=(0,), n=12, flops=1 << 33,
     )(
         edges, u, v, m, external.reshape(3 * ZN * YN, XN), z_low, z_high, y_low, y_high, x_high,
-        big_h, big_l,
+        stiffness, jnp.asarray(element_constants()),
     )
     left = ring(last, "gx", True)
     residual, tangent = call(

time: 56.7 us -> 52.3 us (0.922); the launches traced: 56.4 us -> 51.3 us
  waiting for transfers between devices: 18 us -> 13.2 us
    ppermute x6, waiting for transfers between devices: 7.25 us -> 3.09 us  [ring(): return lax.ppermute(values, axis, pairs)]
    ppermute x6, starting transfers between devices: 8.5 us -> 6.16 us  [ring(): return lax.ppermute(values, axis, pairs)]
    all_to_all x1, starting transfers between devices: 4.74 us -> 5.8 us  [local(): lax.all_to_all(reply, GROUPS, split_axis=0, concat_axis=0, tiled=True)]
    all_to_all x1, starting transfers between devices: 10.7 us -> 11.7 us  [local(): lax.all_to_all(request, GROUPS, split_axis=0, concat_axis=0, tiled=True)]
    pallas_call x1, Pallas kernels: 0.44 us -> 1.16 us  [local(): call(slot_kernel, [((CHUNKS, 56, 128), F32), ((FACES, OWNERS * CAP), BF16...]
    pallas_call x1, Pallas kernels: 2.79 us -> 2.22 us  [local(): call(request_kernel, [((OWNERS, 128), I32), ((CHUNKS, 128), I32), ((7, 2,...]
  transfers between devices with their start and end apart: 8 -> 8, of which waited for: 4 -> 3; matrix products, arithmetic and copies ran while one was open for 0% -> 0% of each run, Pallas kernels for 14% -> 16%
where the time goes in v3:
time: 52.3 us; the launch traced here: 51.3 us
  starting transfers between devices  23.6 us (45%)
  waiting for transfers between devices  13.2 us (25%)
  Pallas kernels  12.9 us (25%)
  between operations  1.47 us (3%)
    all_to_all x1, starting transfers between devices, local(): lax.all_to_all(request, GROUPS, split_axis=0, concat_axis=0, tiled=True)  11.7 us
    ppermute x6, starting transfers between devices, ring(): return lax.ppermute(values, axis, pairs)  6.16 us
    all_to_all x1, starting transfers between devices, local(): lax.all_to_all(reply, GROUPS, split_axis=0, concat_axis=0, tiled=True)  5.8 us
    all_to_all x1, waiting for transfers between devices, local(): lax.all_to_all(request, GROUPS, split_axis=0, concat_axis=0, tiled=True)  5.46 us
    pallas_call x1, Pallas kernels, local(): call(element_kernel, [((3 * ZN * YN, XN), F32), ((3 * ZN * YN, XN), F32),...  4.79 us
    all_to_all x1, waiting for transfers between devices, local(): lax.all_to_all(reply, GROUPS, split_axis=0, concat_axis=0, tiled=True)  4.69 us
    ppermute x6, waiting for transfers between devices, ring(): return lax.ppermute(values, axis, pairs)  3.09 us
    pallas_call x1, Pallas kernels, local(): call(request_kernel, [((OWNERS, 128), I32), ((CHUNKS, 128), I32), ((7, 2,...  2.22 us
  transfers between devices with their start and end apart: 8, of which 3 were waited for; matrix products, arithmetic and copies ran while one was open for 0% of the time, Pallas kernels for 16%

profile of v3, /device:TPU:8, one launch (start us, length us, event | category | flops | bytes accessed | tf_op | source)
XLA Modules:
  0.0 51.3 jit_solution(7648482298657993034)
XLA Ops:
  1.3 0.0 copy-start
  1.3 0.0 copy-start.1
  1.3 2.2 %shard_map.149 = (s32[64,128]{1,0:T(8,128)}, s32[16,128]{1,0:T(8,128)}, f32[7,2,8,128]{3,2,1,0:T(8,128)}, f32[7,1,8,128]{3,2,1,0:T(8,128)}) custom-call(s32[8,128]{1,0:T(8,128)} %bitcast.40, s32[8,128]{1,0:T(8,128)} %bitcast.41, s32[8,128]{1,0:T(8,128)} %bitcast.42, s32[1]{0:T(128)S(6)} %copy.19.counts, f32[3,16,8,128]{3,2,1,0:T(8,128)} %u.1, ...), custom_call_target="tpu_custom_call" | custom-call | tf_op jit(solution)/shard_map/pallas_call | solution.py:630
  3.5 0.0 copy-start.2
  3.5 1.7 %collective-permute-start = (f32[7,2,8,128]{3,2,1,0:T(8,128)}, f32[7,2,8,128]{3,2,1,0:T(8,128)S(1)}, u32[]{:S(2)}, u32[]{:S(2)}) collective-permute-start(f32[7,2,8,128]{3,2,1,0:T(8,128)} %get-tuple-element.17), channel_id=1, source_target_pairs={{0,1},{1,2},{2,3},{3,0},{4,5},{5,6},{6,7},{7,4},{8,9},{9,10},{10,1... | collective-permute-start | bytes 172040 | tf_op jit(solution)/shard_map/ppermute | solution.py:612
  5.2 0.7 %collective-permute-start.1 = (f32[7,1,8,128]{3,2,1,0:T(8,128)}, f32[7,1,8,128]{3,2,1,0:T(8,128)S(1)}, u32[]{:S(2)}, u32[]{:S(2)}) collective-permute-start(f32[7,1,8,128]{3,2,1,0:T(8,128)} %get-tuple-element.18), channel_id=1, source_target_pairs={{1,0},{2,1},{3,2},{0,3},{5,4},{6,5},{7,6},{4,7},{9,8},{10,9},{11,1... | collective-permute-start | bytes 86024 | tf_op jit(solution)/shard_map/ppermute | solution.py:612
  5.9 11.7 %all-to-all-start = ((s32[64,1,128]{2,1,0:T(1,128)}), s32[64,1,128]{2,1,0:T(1,128)S(1)}, u32[]{:S(2)}, u32[]{:S(2)}) async-start(s32[64,1,128]{2,1,0:T(1,128)} %bitcast.39), calls=%async_computation | async-start | bytes 65536 | tf_op jit(solution)/shard_map/all_to_all | solution.py:644
  17.6 0.0 collective-permute-done.1
  17.6 0.0 collective-permute-done
  17.6 0.0 copy-done
  17.6 0.0 copy-done.1
  17.6 0.0 copy-done.2
  17.6 0.0 copy-start.5
  17.6 0.1 shard_map.150
  17.7 0.0 copy-start.6
  17.7 1.6 %collective-permute-start.2 = (f32[336,128]{1,0:T(8,128)S(1)}, f32[336,128]{1,0:T(8,128)S(1)}, u32[]{:S(2)}, u32[]{:S(2)}) collective-permute-start(f32[336,128]{1,0:T(8,128)S(1)} %get-tuple-element.19), channel_id=1, source_target_pairs={{0,4},{4,8},{8,12},{12,0},{1,5},{5,9},{9,13},{13,1},{2,6},{6,10},{... | collective-permute-start | bytes 516104 | tf_op jit(solution)/shard_map/ppermute | solution.py:612
  19.4 0.0 copy-done.5
  19.4 0.0 copy-done.6
  19.4 0.2 shard_map.151.table
  19.6 2.1 %collective-permute-start.3 = (f32[168,128]{1,0:T(8,128)S(1)}, f32[168,128]{1,0:T(8,128)S(1)}, u32[]{:S(2)}, u32[]{:S(2)}) collective-permute-start(f32[168,128]{1,0:T(8,128)S(1)} %get-tuple-element.20), channel_id=1, source_target_pairs={{4,0},{8,4},{12,8},{0,12},{5,1},{9,5},{13,9},{1,13},{6,2},{10,6},{... | collective-permute-start | bytes 258056 | tf_op jit(solution)/shard_map/ppermute | solution.py:612
  21.7 5.5 %all-to-all-done = s32[64,1,128]{2,1,0:T(1,128)S(1)} async-done(((s32[64,1,128]{2,1,0:T(1,128)}), s32[64,1,128]{2,1,0:T(1,128)S(1)}, u32[]{:S(2)}, u32[]{:S(2)}) %all-to-all-start) | async-done | bytes 32800 | tf_op jit(solution)/shard_map/all_to_all | solution.py:644
  27.2 2.1 %shard_map.152.reply_in = f32[64,8,128]{2,1,0:T(8,128)} custom-call(s32[64,128]{1,0:T(8,128)S(1)} %bitcast.37, f32[32,2048]{1,0:T(8,128)S(1)} %shard_map.151.table), custom_call_target="tpu_custom_call" | custom-call | flops 1342177280 | tf_op jit(solution)/shard_map/pallas_call | solution.py:657
  29.2 0.0 collective-permute-done.3.y_high
  29.2 0.0 collective-permute-done.2.y_low
  29.3 0.3 shard_map.153
  29.6 0.0 collective-permute-start.4
  29.6 0.1 pad_add_fusion.edges
  29.7 0.0 copy-start.8
  29.7 0.0 copy-start.9
  29.7 0.0 copy-start.10
  29.7 5.8 %all-to-all-start.1 = ((f32[64,8,128]{2,1,0:T(8,128)}), f32[64,8,128]{2,1,0:T(8,128)S(1)}, u32[]{:S(2)}, u32[]{:S(2)}) async-start(f32[64,8,128]{2,1,0:T(8,128)} %get-tuple-element.22), calls=%async_computation.1 | async-start | bytes 524288 | tf_op jit(solution)/shard_map/all_to_all | solution.py:663
  35.5 0.0 collective-permute-done.4.x_high
  35.5 0.0 copy-done.8
  35.5 0.0 copy-done.9
  35.5 0.0 copy-done.10
  35.5 0.0 copy-start.3
  35.5 0.0 copy-start.7
  35.5 4.8 %shard_map.155 = (f32[384,128]{1,0:T(8,128)S(1)}, f32[384,128]{1,0:T(8,128)S(1)}, f32[8,128]{1,0:T(8,128)S(1)}) custom-call(s32[3]{0:T(128)S(1)} %pad_add_fusion.edges, f32[384,128]{1,0:T(8,128)S(1)} %bitcast.20, f32[384,128]{1,0:T(8,128)S(1)} %bitcast.25, f32[128,128]{1,0:T(8,128)S(1)} %bitcast.30, f32[384,128]{1,0:T(8,128)S(1)} %bitcast.38, ...), custom_call_target="tpu_custom_call" | custom-call | flops 8589934592 | tf_op jit(solution)/shard_map/pallas_call | solution.py:666
  40.3 0.1 collective-permute-start.5
  40.4 0.0 copy-done.3
  40.4 0.0 copy-done.7
  40.4 0.0 copy-start.4
  40.4 1.2 %shard_map.154 = (f32[16,56,128]{2,1,0:T(8,128)S(1)}, bf16[192,2048]{1,0:T(8,128)(2,1)S(1)}) custom-call(f32[384,128]{1,0:T(8,128)S(1)} %bitcast.21, f32[384,128]{1,0:T(8,128)S(1)} %bitcast.26, s32[16,128]{1,0:T(8,128)S(1)} %copy-done.7, bf16[384,768]{1,0:T(8,128)(2,1)S(1)} %copy-done.3), custom_call_target="tpu_custom_call" | custom-call | tf_op jit(solution)/shard_map/pallas_call | solution.py:647
  41.6 3.1 %collective-permute-done.5.left = f32[8,128]{1,0:T(8,128)S(1)} collective-permute-done((f32[8,128]{1,0:T(8,128)S(1)}, f32[8,128]{1,0:T(8,128)S(1)}, u32[]{:S(2)}, u32[]{:S(2)}) %collective-permute-start.5) | collective-permute-done | bytes 4128 | tf_op jit(solution)/shard_map/ppermute | solution.py:612
  44.7 4.7 %all-to-all-done.1.replies = f32[64,8,128]{2,1,0:T(8,128)S(1)} async-done(((f32[64,8,128]{2,1,0:T(8,128)}), f32[64,8,128]{2,1,0:T(8,128)S(1)}, u32[]{:S(2)}, u32[]{:S(2)}) %all-to-all-start.1) | async-done | bytes 262176 | tf_op jit(solution)/shard_map/all_to_all | solution.py:663
  49.3 0.0 copy-done.4
  49.3 2.0 %shard_map.156 = (f32[384,128]{1,0:T(8,128)}, f32[384,128]{1,0:T(8,128)}) custom-call(f32[64,8,128]{2,1,0:T(8,128)S(1)} %all-to-all-done.1.replies, f32[16,56,128]{2,1,0:T(8,128)S(1)} %get-tuple-element.24.kin, bf16[192,2048]{1,0:T(8,128)(2,1)S(1)} %get-tuple-element.25.selector, bf16[224,576]{1,0:T(8,128)(2,1)S(1)} %copy-done.4, ...), custom_call_target="tpu_custom_call" | custom-call | flops 1048576 | tf_op jit(solution)/shard_map/pallas_call | solution.py:681
Async XLA Ops:
  1.3 16.3 %copy-start = (f32[3,16,8,128]{3,2,1,0:T(8,128)S(1)}, f32[3,16,8,128]{3,2,1,0:T(8,128)}, u32[]{:S(2)}) copy-start(f32[3,16,8,128]{3,2,1,0:T(8,128)} %u.1) | copy-start | bytes 589828
  1.3 16.3 %copy-start.1 = (f32[3,16,8,128]{3,2,1,0:T(8,128)S(1)}, f32[3,16,8,128]{3,2,1,0:T(8,128)}, u32[]{:S(2)}) copy-start(f32[3,16,8,128]{3,2,1,0:T(8,128)} %v.1) | copy-start | bytes 589828
  3.5 14.1 %copy-start.2 = (f32[16,8,128]{2,1,0:T(8,128)S(1)}, f32[16,8,128]{2,1,0:T(8,128)}, u32[]{:S(2)}) copy-start(f32[16,8,128]{2,1,0:T(8,128)} %m.1) | copy-start | bytes 196612
  3.5 14.1 %collective-permute-start = (f32[7,2,8,128]{3,2,1,0:T(8,128)}, f32[7,2,8,128]{3,2,1,0:T(8,128)S(1)}, u32[]{:S(2)}, u32[]{:S(2)}) collective-permute-start(f32[7,2,8,128]{3,2,1,0:T(8,128)} %get-tuple-element.17), channel_id=1, source_target_pairs={{0,1},{1,2},{2,3},{3,0},{4,5},{5,6},{6,7},{7,4},{8,9},{9,10},{10,1... | collective-permute-start | bytes 172040 | tf_op jit(solution)/shard_map/ppermute | solution.py:612
  5.2 12.4 %collective-permute-start.1 = (f32[7,1,8,128]{3,2,1,0:T(8,128)}, f32[7,1,8,128]{3,2,1,0:T(8,128)S(1)}, u32[]{:S(2)}, u32[]{:S(2)}) collective-permute-start(f32[7,1,8,128]{3,2,1,0:T(8,128)} %get-tuple-element.18), channel_id=1, source_target_pairs={{1,0},{2,1},{3,2},{0,3},{5,4},{6,5},{7,6},{4,7},{9,8},{10,9},{11,1... | collective-permute-start | bytes 86024 | tf_op jit(solution)/shard_map/ppermute | solution.py:612
  5.9 21.3 %all-to-all-start = ((s32[64,1,128]{2,1,0:T(1,128)}), s32[64,1,128]{2,1,0:T(1,128)S(1)}, u32[]{:S(2)}, u32[]{:S(2)}) async-start(s32[64,1,128]{2,1,0:T(1,128)} %bitcast.39), calls=%async_computation | async-start | bytes 65536 | tf_op jit(solution)/shard_map/all_to_all | solution.py:644
  17.6 1.7 %copy-start.5 = (f32[27,2048]{1,0:T(8,128)S(1)}, f32[27,2048]{1,0:T(8,128)}, u32[]{:S(2)}) copy-start(f32[27,2048]{1,0:T(8,128)} %master.1) | copy-start | bytes 663556
  17.7 1.7 %copy-start.6 = (bf16[32,256]{1,0:T(8,128)(2,1)S(1)}, bf16[32,256]{1,0:T(8,128)(2,1)}, u32[]{:S(2)}) copy-start(bf16[32,256]{1,0:T(8,128)(2,1)} %constant.20.clone.fixed) | copy-start | bytes 49156
  17.7 11.5 %collective-permute-start.2 = (f32[336,128]{1,0:T(8,128)S(1)}, f32[336,128]{1,0:T(8,128)S(1)}, u32[]{:S(2)}, u32[]{:S(2)}) collective-permute-start(f32[336,128]{1,0:T(8,128)S(1)} %get-tuple-element.19), channel_id=1, source_target_pairs={{0,4},{4,8},{8,12},{12,0},{1,5},{5,9},{9,13},{13,1},{2,6},{6,10},{... | collective-permute-start | bytes 516104 | tf_op jit(solution)/shard_map/ppermute | solution.py:612
  19.6 9.6 %collective-permute-start.3 = (f32[168,128]{1,0:T(8,128)S(1)}, f32[168,128]{1,0:T(8,128)S(1)}, u32[]{:S(2)}, u32[]{:S(2)}) collective-permute-start(f32[168,128]{1,0:T(8,128)S(1)} %get-tuple-element.20), channel_id=1, source_target_pairs={{4,0},{8,4},{12,8},{0,12},{5,1},{9,5},{13,9},{1,13},{6,2},{10,6},{... | collective-permute-start | bytes 258056 | tf_op jit(solution)/shard_map/ppermute | solution.py:612
  29.6 5.9 %collective-permute-start.4 = (f32[16,128]{1,0:T(8,128)S(1)}, f32[16,128]{1,0:T(8,128)S(1)}, u32[]{:S(2)}, u32[]{:S(2)}) collective-permute-start(f32[16,128]{1,0:T(8,128)S(1)} %get-tuple-element.26), channel_id=1, source_target_pairs={{16,0},{32,16},{48,32},{64,48},{80,64},{96,80},{112,96},{128,112},... | collective-permute-start | bytes 24584 | tf_op jit(solution)/shard_map/ppermute | solution.py:612
  29.7 5.8 %copy-start.8 = (f32[3,16,8,128]{3,2,1,0:T(8,128)S(1)}, f32[3,16,8,128]{3,2,1,0:T(8,128)}, u32[]{:S(2)}) copy-start(f32[3,16,8,128]{3,2,1,0:T(8,128)} %param.17) | copy-start | bytes 589828
  29.7 5.8 %copy-start.9 = (f32[81,81]{1,0:T(8,128)S(1)}, f32[81,81]{1,0:T(8,128)}, u32[]{:S(2)}) copy-start(f32[81,81]{1,0:T(8,128)} %stiffness.1) | copy-start | bytes 78736
  29.7 5.8 %copy-start.10 = (bf16[144,640]{1,0:T(8,128)(2,1)S(1)}, bf16[144,640]{1,0:T(8,128)(2,1)}, u32[]{:S(2)}) copy-start(bf16[144,640]{1,0:T(8,128)(2,1)} %constant.22.clone.fixed) | copy-start | bytes 552964
  29.7 19.7 %all-to-all-start.1 = ((f32[64,8,128]{2,1,0:T(8,128)}), f32[64,8,128]{2,1,0:T(8,128)S(1)}, u32[]{:S(2)}, u32[]{:S(2)}) async-start(f32[64,8,128]{2,1,0:T(8,128)} %get-tuple-element.22), calls=%async_computation.1 | async-start | bytes 524288 | tf_op jit(solution)/shard_map/all_to_all | solution.py:663
  35.5 4.9 %copy-start.3 = (bf16[384,768]{1,0:T(8,128)(2,1)S(1)}, bf16[384,768]{1,0:T(8,128)(2,1)}, u32[]{:S(2)}) copy-start(bf16[384,768]{1,0:T(8,128)(2,1)} %constant.21.clone.fixed) | copy-start | bytes 1769476
  35.5 4.9 %copy-start.7 = (s32[16,128]{1,0:T(8,128)S(1)}, s32[16,128]{1,0:T(8,128)}, u32[]{:S(2)}) copy-start(s32[16,128]{1,0:T(8,128)} %get-tuple-element.23.faces) | copy-start | bytes 24580
  40.3 4.3 %collective-permute-start.5 = (f32[8,128]{1,0:T(8,128)S(1)}, f32[8,128]{1,0:T(8,128)S(1)}, u32[]{:S(2)}, u32[]{:S(2)}) collective-permute-start(f32[8,128]{1,0:T(8,128)S(1)} %get-tuple-element.27), channel_id=1, source_target_pairs={{0,16},{16,32},{32,48},{48,64},{64,80},{80,96},{96,112},{112,128},... | collective-permute-start | bytes 12296 | tf_op jit(solution)/shard_map/ppermute | solution.py:612
  40.4 8.9 %copy-start.4 = (bf16[224,576]{1,0:T(8,128)(2,1)S(1)}, bf16[224,576]{1,0:T(8,128)(2,1)}, u32[]{:S(2)}) copy-start(bf16[224,576]{1,0:T(8,128)(2,1)} %constant.23.clone.fixed) | copy-start | bytes 774148

commit v4 on v3

--- a/solution.py
+++ b/solution.py
@@ -211,8 +211,7 @@
 
 
 def request_kernel(
-    owners, rows, sides_in, counts, u, v, m, request, faces, z_up, z_down,
-    owner, row, face, arrived,
+    owners, rows, sides_in, u, v, m, request, codes, z_up, z_down, owner, row, face, arrived
 ):
     first = [
         pltpu.make_async_copy(source, to, arrived.at[6 + i])
@@ -232,21 +231,18 @@
         copy.start()
     for copy in first:
         copy.wait()
-    live_count = counts[...]
     who = lax.broadcasted_iota(I32, (OWNERS, 128), 0)
     lane = lane_ids(1)
     hits = []
     for t in range(PAIRS // 128):
-        live = lane + t * 128 < live_count
-        target = jnp.where(live, owner[pl.ds(t, 1), :], -1)
-        hits.append(jnp.where(who == target, 1.0, 0.0).astype(F32))
+        hits.append(jnp.where(who == owner[pl.ds(t, 1), :], 1.0, 0.0).astype(F32))
     before = jnp.where(
         lax.broadcasted_iota(I32, (128, 128), 0) < lax.broadcasted_iota(I32, (128, 128), 1), 1.0, 0.0
     ).astype(BF16)
     ranks = mm(jnp.concatenate([h.astype(BF16) for h in hits], axis=0), before)
     base = jnp.zeros((OWNERS, 1), F32)
     places = lax.broadcasted_iota(I32, (128, 128), 0)
-    highs, lows, sides = [], [], []
+    highs, lows, sides, marks = [], [], [], []
     for t in range(PAIRS // 128):
         rank = jnp.sum(hits[t] * (ranks[t * OWNERS : (t + 1) * OWNERS] + base), axis=0, keepdims=True)
         base = base + jnp.sum(hits[t], axis=1, keepdims=True)
@@ -254,14 +250,22 @@
         number = row[pl.ds(t, 1), :] + 1
         f = face[pl.ds(t, 1), :]
         f = f + jnp.where(f >= FACE_COLS, 1, 0) + jnp.where(f >= 2 * FACE_COLS, 1, 0) + 1
-        highs.append(jnp.where(here, lax.shift_right_logical(number, 6).astype(F32), 0.0).astype(BF16))
-        lows.append(jnp.where(here, (number & 63).astype(F32), 0.0).astype(BF16))
-        sides.append(jnp.where(here, f.astype(F32), 0.0).astype(BF16))
+        spot = lane + t * 128
+        numbers = (
+            lax.shift_right_logical(number, 6) + 64 * (t // 2),
+            (number & 63) + 64 * (lax.shift_right_logical(spot, 6) & 3),
+            f,
+            spot & 63,
+        )
+        for to, value in zip((highs, lows, sides, marks), numbers):
+            to.append(jnp.where(here, value.astype(F32), 0.0).astype(BF16))
     hit = jnp.concatenate([h.astype(BF16) for h in hits], axis=1)
-    high = mm_nt(hit, jnp.concatenate(highs, axis=1))
-    low = mm_nt(hit, jnp.concatenate(lows, axis=1))
-    request[...] = (high * 64.0 + low).astype(I32)
-    faces[...] = compact(mm_nt(hit, jnp.concatenate(sides, axis=1))).astype(I32)
+    high, low, side, mark = (
+        mm_nt(hit, jnp.concatenate(to, axis=1)).astype(I32) for to in (highs, lows, sides, marks)
+    )
+    request[...] = (high & 63) * 64 + (low & 63)
+    spots = lax.shift_right_logical(high, 6) * 256 + lax.shift_right_logical(low, 6) * 64 + mark
+    codes[...] = compact(spots * 256 + side)
     for copy in layers:
         copy.wait()
 
@@ -511,7 +515,7 @@
     last[...] = sent
 
 
-def slot_kernel(u, v, faces, fixed, kin, selector, quads):
+def slot_kernel(u, v, codes, fixed, count, kin, selector, quads):
     plane = jnp.concatenate(
         [field[pl.ds(c * ZN * YN, YN), :] for field in (u, v) for c in range(3)], axis=0
     )
@@ -520,8 +524,10 @@
     for first, to in ((0, 0), (384, 128)):
         pair = fixed[256:312, first : first + 288], fixed[320:376, first : first + 288]
         quads[:, to : to + 128] = mm3(pair, tall)
-    slot_faces = faces[...]
-    face_ids = lax.broadcasted_iota(I32, (FACES, 128), 0) + 1
+    spots = lax.shift_right_logical(codes[...], 8)
+    slot_faces = jnp.where(spots < count[0], codes[...] & 255, 0)
+    columns = jnp.concatenate([slot_faces.astype(F32), jnp.zeros((112, 128), F32)], axis=0).T
+    face_ids = (lax.broadcasted_iota(I32, (128, FACES), 1) + 1).astype(F32)
     for c in range(CHUNKS):
         slot_face = slot_faces[c : c + 1]
         index = jnp.maximum(jnp.broadcast_to(slot_face, (8, 128)) - 1, 0)
@@ -532,7 +538,7 @@
                 pick_lanes(quads[pl.ds(i * 8, 8), 128:256], inside),
                 pick_lanes(quads[pl.ds(i * 8, 8), 0:128], inside),
             )
-        selector[:, c * 128 : (c + 1) * 128] = jnp.where(face_ids == slot_face, 1.0, 0.0).astype(BF16)
+        selector[pl.ds(c * 128, 128), :] = jnp.where(face_ids == columns[:, c : c + 1], 1.0, 0.0).astype(BF16)
 
 
 def contact_kernel(replies, kin, selector, fixed, left, u, v, res_in, tan_in, residual, tangent):
@@ -560,7 +566,7 @@
     values = jnp.concatenate(
         [jnp.concatenate(values_h, axis=1), jnp.concatenate(values_l, axis=1)], axis=0
     )
-    sums = mm_nt(values, selector[...])
+    sums = mm(values, selector[...])
     sums = sums[0:64] + sums[64:128]
     sums = jnp.concatenate([sums[:, 0:64], sums[:, 64:128], sums[:, 128:192]], axis=0)
     along = mm3(split(sums), (fixed[0:64, 0:384], fixed[64:128, 0:384]))
@@ -627,16 +633,16 @@
     u = displacement.reshape(3 * ZN * YN, XN)
     v = direction.reshape(3 * ZN * YN, XN)
     m = modulus.reshape(ZN * YN, XN)
-    request, faces, z_up, z_down = call(
+    request, codes, z_up, z_down = call(
         request_kernel,
         [((OWNERS, 128), I32), ((CHUNKS, 128), I32), ((7, 2, YN, XN), F32), ((7, 1, YN, XN), F32)],
         scratch=[
             pltpu.VMEM((8, 128), I32), pltpu.VMEM((8, 128), I32), pltpu.VMEM((8, 128), I32),
             pltpu.SemaphoreType.DMA((9,)),
         ],
-        hbm=(0, 1, 2, 4, 5, 6), n=7, limit=64512,
+        hbm=tuple(range(6)), n=6, limit=64512,
     )(
-        pair_owner.reshape(8, 128), pair_row.reshape(8, 128), pair_face.reshape(8, 128), pair_count,
+        pair_owner.reshape(8, 128), pair_row.reshape(8, 128), pair_face.reshape(8, 128),
         displacement, direction, modulus,
     )
     z_low = ring(z_up, "gz", True).reshape(7 * 2 * YN, XN)
@@ -645,9 +651,9 @@
 
     (table,) = call(table_kernel, [((32, ROWS), F32)], n=2)(master_record, jnp.asarray(table_constants()))
     kin, selector = call(
-        slot_kernel, [((CHUNKS, 56, 128), F32), ((FACES, OWNERS * CAP), BF16)],
-        scratch=[pltpu.VMEM((56, 256), F32)], n=4,
-    )(u, v, faces, jnp.asarray(slot_constants()))
+        slot_kernel, [((CHUNKS, 56, 128), F32), ((OWNERS * CAP, FACES), BF16)],
+        scratch=[pltpu.VMEM((56, 256), F32)], smem=(4,), n=5,
+    )(u, v, codes, jnp.asarray(slot_constants()), pair_count)
     y_up, y_down = call(side_kernel, [((7 * 2 * 24, XN), F32), ((7 * 24, XN), F32)], n=5)(
         u, v, m, z_low, z_high
     )

time: 52.3 us -> 51.5 us (0.985)
  waiting for transfers between devices: 13.2 us -> 12.6 us
    ppermute x6, waiting for transfers between devices: 3.09 us -> 2.45 us  [ring(): return lax.ppermute(values, axis, pairs)]
where the time goes in v4:
time: 51.5 us; the launch traced here: 50.5 us
  starting transfers between devices  23.6 us (46%)
  Pallas kernels  12.7 us (25%)
  waiting for transfers between devices  12.6 us (24%)
  between operations  1.5 us (3%)
    all_to_all x1, starting transfers between devices, local(): lax.all_to_all(request, GROUPS, split_axis=0, concat_axis=0, tiled=True)  11.7 us
    ppermute x6, starting transfers between devices, ring(): return lax.ppermute(values, axis, pairs)  6.17 us
    all_to_all x1, starting transfers between devices, local(): lax.all_to_all(reply, GROUPS, split_axis=0, concat_axis=0, tiled=True)  5.8 us
    all_to_all x1, waiting for transfers between devices, local(): lax.all_to_all(request, GROUPS, split_axis=0, concat_axis=0, tiled=True)  5.46 us
    pallas_call x1, Pallas kernels, local(): call(element_kernel, [((3 * ZN * YN, XN), F32), ((3 * ZN * YN, XN), F32),...  4.79 us
    all_to_all x1, waiting for transfers between devices, local(): lax.all_to_all(reply, GROUPS, split_axis=0, concat_axis=0, tiled=True)  4.69 us
    ppermute x6, waiting for transfers between devices, ring(): return lax.ppermute(values, axis, pairs)  2.45 us
    pallas_call x1, Pallas kernels, local(): call(request_kernel, [((OWNERS, 128), I32), ((CHUNKS, 128), I32), ((7, 2,...  2.24 us
  transfers between devices with their start and end apart: 8, of which 3 were waited for; matrix products, arithmetic and copies ran while one was open for 0% of the time, Pallas kernels for 16%

profile of v4, /device:TPU:8, one launch (start us, length us, event | category | flops | bytes accessed | tf_op | source)
XLA Modules:
  0.0 50.5 jit_solution(6238711623896630775)
XLA Ops:
  0.6 0.0 copy-start
  0.6 0.0 copy-start.1
  0.7 2.2 %shard_map.149 = (s32[64,128]{1,0:T(8,128)}, s32[16,128]{1,0:T(8,128)}, f32[7,2,8,128]{3,2,1,0:T(8,128)}, f32[7,1,8,128]{3,2,1,0:T(8,128)}) custom-call(s32[8,128]{1,0:T(8,128)} %bitcast.40, s32[8,128]{1,0:T(8,128)} %bitcast.41, s32[8,128]{1,0:T(8,128)} %bitcast.42, f32[3,16,8,128]{3,2,1,0:T(8,128)} %u.1, f32[3,16,8,128]{3,2,1,0:T(8,128)} %v.1, f32[16,8,128]{2,1,0:T(8,128)} %m.1), custom_call_target="tpu_custom_call" | custom-call | tf_op jit(solution)/shard_map/pallas_call | solution.py:636
  2.9 0.0 copy-start.2
  2.9 1.7 %collective-permute-start = (f32[7,2,8,128]{3,2,1,0:T(8,128)}, f32[7,2,8,128]{3,2,1,0:T(8,128)S(1)}, u32[]{:S(2)}, u32[]{:S(2)}) collective-permute-start(f32[7,2,8,128]{3,2,1,0:T(8,128)} %get-tuple-element.17), channel_id=1, source_target_pairs={{0,1},{1,2},{2,3},{3,0},{4,5},{5,6},{6,7},{7,4},{8,9},{9,10},{10,1... | collective-permute-start | bytes 172040 | tf_op jit(solution)/shard_map/ppermute | solution.py:618
  4.6 0.7 %collective-permute-start.1 = (f32[7,1,8,128]{3,2,1,0:T(8,128)}, f32[7,1,8,128]{3,2,1,0:T(8,128)S(1)}, u32[]{:S(2)}, u32[]{:S(2)}) collective-permute-start(f32[7,1,8,128]{3,2,1,0:T(8,128)} %get-tuple-element.18), channel_id=1, source_target_pairs={{1,0},{2,1},{3,2},{0,3},{5,4},{6,5},{7,6},{4,7},{9,8},{10,9},{11,1... | collective-permute-start | bytes 86024 | tf_op jit(solution)/shard_map/ppermute | solution.py:618
  5.3 11.7 %all-to-all-start = ((s32[64,1,128]{2,1,0:T(1,128)}), s32[64,1,128]{2,1,0:T(1,128)S(1)}, u32[]{:S(2)}, u32[]{:S(2)}) async-start(s32[64,1,128]{2,1,0:T(1,128)} %bitcast.39), calls=%async_computation | async-start | bytes 65536 | tf_op jit(solution)/shard_map/all_to_all | solution.py:650
  17.0 0.0 collective-permute-done.1
  17.0 0.0 collective-permute-done
  17.0 0.0 copy-done
  17.0 0.0 copy-done.1
  17.0 0.0 copy-done.2
  17.0 0.0 copy-start.5
  17.0 0.1 shard_map.150
  17.1 0.0 copy-start.6
  17.1 1.6 %collective-permute-start.2 = (f32[336,128]{1,0:T(8,128)S(1)}, f32[336,128]{1,0:T(8,128)S(1)}, u32[]{:S(2)}, u32[]{:S(2)}) collective-permute-start(f32[336,128]{1,0:T(8,128)S(1)} %get-tuple-element.19), channel_id=1, source_target_pairs={{0,4},{4,8},{8,12},{12,0},{1,5},{5,9},{9,13},{13,1},{2,6},{6,10},{... | collective-permute-start | bytes 516104 | tf_op jit(solution)/shard_map/ppermute | solution.py:618
  18.7 0.0 copy-done.5
  18.7 0.0 copy-done.6
  18.7 0.2 shard_map.151.table
  19.0 2.1 %collective-permute-start.3 = (f32[168,128]{1,0:T(8,128)S(1)}, f32[168,128]{1,0:T(8,128)S(1)}, u32[]{:S(2)}, u32[]{:S(2)}) collective-permute-start(f32[168,128]{1,0:T(8,128)S(1)} %get-tuple-element.20), channel_id=1, source_target_pairs={{4,0},{8,4},{12,8},{0,12},{5,1},{9,5},{13,9},{1,13},{6,2},{10,6},{... | collective-permute-start | bytes 258056 | tf_op jit(solution)/shard_map/ppermute | solution.py:618
  21.1 5.5 %all-to-all-done = s32[64,1,128]{2,1,0:T(1,128)S(1)} async-done(((s32[64,1,128]{2,1,0:T(1,128)}), s32[64,1,128]{2,1,0:T(1,128)S(1)}, u32[]{:S(2)}, u32[]{:S(2)}) %all-to-all-start) | async-done | bytes 32800 | tf_op jit(solution)/shard_map/all_to_all | solution.py:650
  26.5 2.1 %shard_map.152.reply_in = f32[64,8,128]{2,1,0:T(8,128)} custom-call(s32[64,128]{1,0:T(8,128)S(1)} %bitcast.37, f32[32,2048]{1,0:T(8,128)S(1)} %shard_map.151.table), custom_call_target="tpu_custom_call" | custom-call | flops 1342177280 | tf_op jit(solution)/shard_map/pallas_call | solution.py:663
  28.6 0.0 collective-permute-done.3.y_high
  28.6 0.0 collective-permute-done.2.y_low
  28.6 0.3 shard_map.153
  28.9 0.0 collective-permute-start.4
  29.0 0.1 pad_add_fusion.edges
  29.0 0.0 copy-start.8
  29.0 0.0 copy-start.9
  29.0 0.0 copy-start.10
  29.0 5.8 %all-to-all-start.1 = ((f32[64,8,128]{2,1,0:T(8,128)}), f32[64,8,128]{2,1,0:T(8,128)S(1)}, u32[]{:S(2)}, u32[]{:S(2)}) async-start(f32[64,8,128]{2,1,0:T(8,128)} %get-tuple-element.22), calls=%async_computation.1 | async-start | bytes 524288 | tf_op jit(solution)/shard_map/all_to_all | solution.py:669
  34.9 0.0 collective-permute-done.4.x_high
  34.9 0.0 copy-done.8
  34.9 0.0 copy-done.9
  34.9 0.0 copy-done.10
  34.9 0.0 copy-start.3
  34.9 0.0 copy-start.7
  34.9 4.8 %shard_map.155 = (f32[384,128]{1,0:T(8,128)S(1)}, f32[384,128]{1,0:T(8,128)S(1)}, f32[8,128]{1,0:T(8,128)S(1)}) custom-call(s32[3]{0:T(128)S(1)} %pad_add_fusion.edges, f32[384,128]{1,0:T(8,128)S(1)} %bitcast.20, f32[384,128]{1,0:T(8,128)S(1)} %bitcast.25, f32[128,128]{1,0:T(8,128)S(1)} %bitcast.30, f32[384,128]{1,0:T(8,128)S(1)} %bitcast.38, ...), custom_call_target="tpu_custom_call" | custom-call | flops 8589934592 | tf_op jit(solution)/shard_map/pallas_call | solution.py:672
  39.7 0.1 collective-permute-start.5
  40.4 0.0 copy-done.3
  40.4 0.0 copy-done.7
  40.4 0.0 copy-start.4
  40.5 1.1 %shard_map.154 = (f32[16,56,128]{2,1,0:T(8,128)S(1)}, bf16[2048,192]{1,0:T(8,128)(2,1)S(1)}) custom-call(f32[384,128]{1,0:T(8,128)S(1)} %bitcast.21, f32[384,128]{1,0:T(8,128)S(1)} %bitcast.26, s32[16,128]{1,0:T(8,128)S(1)} %copy-done.7, bf16[384,768]{1,0:T(8,128)(2,1)S(1)} %copy-done.3, s32[1]{0:T(128)S(6)} %copy.19.count), custom_call_target="tpu_custom_call" | custom-call | tf_op jit(solution)/shard_map/pallas_call | solution.py:653
  41.6 2.4 %collective-permute-done.5.left = f32[8,128]{1,0:T(8,128)S(1)} collective-permute-done((f32[8,128]{1,0:T(8,128)S(1)}, f32[8,128]{1,0:T(8,128)S(1)}, u32[]{:S(2)}, u32[]{:S(2)}) %collective-permute-start.5) | collective-permute-done | bytes 4128 | tf_op jit(solution)/shard_map/ppermute | solution.py:618
  44.0 4.7 %all-to-all-done.1.replies = f32[64,8,128]{2,1,0:T(8,128)S(1)} async-done(((f32[64,8,128]{2,1,0:T(8,128)}), f32[64,8,128]{2,1,0:T(8,128)S(1)}, u32[]{:S(2)}, u32[]{:S(2)}) %all-to-all-start.1) | async-done | bytes 262176 | tf_op jit(solution)/shard_map/all_to_all | solution.py:669
  48.7 0.0 copy-done.4
  48.7 1.8 %shard_map.156 = (f32[384,128]{1,0:T(8,128)}, f32[384,128]{1,0:T(8,128)}) custom-call(f32[64,8,128]{2,1,0:T(8,128)S(1)} %all-to-all-done.1.replies, f32[16,56,128]{2,1,0:T(8,128)S(1)} %get-tuple-element.24.kin, bf16[2048,192]{1,0:T(8,128)(2,1)S(1)} %get-tuple-element.25.selector, bf16[224,576]{1,0:T(8,128)(2,1)S(1)} %copy-done.4, ...), custom_call_target="tpu_custom_call" | custom-call | flops 1048576 | tf_op jit(solution)/shard_map/pallas_call | solution.py:687
Async XLA Ops:
  0.6 16.3 %copy-start = (f32[3,16,8,128]{3,2,1,0:T(8,128)S(1)}, f32[3,16,8,128]{3,2,1,0:T(8,128)}, u32[]{:S(2)}) copy-start(f32[3,16,8,128]{3,2,1,0:T(8,128)} %u.1) | copy-start | bytes 589828
  0.6 16.3 %copy-start.1 = (f32[3,16,8,128]{3,2,1,0:T(8,128)S(1)}, f32[3,16,8,128]{3,2,1,0:T(8,128)}, u32[]{:S(2)}) copy-start(f32[3,16,8,128]{3,2,1,0:T(8,128)} %v.1) | copy-start | bytes 589828
  2.9 14.1 %copy-start.2 = (f32[16,8,128]{2,1,0:T(8,128)S(1)}, f32[16,8,128]{2,1,0:T(8,128)}, u32[]{:S(2)}) copy-start(f32[16,8,128]{2,1,0:T(8,128)} %m.1) | copy-start | bytes 196612
  2.9 14.1 %collective-permute-start = (f32[7,2,8,128]{3,2,1,0:T(8,128)}, f32[7,2,8,128]{3,2,1,0:T(8,128)S(1)}, u32[]{:S(2)}, u32[]{:S(2)}) collective-permute-start(f32[7,2,8,128]{3,2,1,0:T(8,128)} %get-tuple-element.17), channel_id=1, source_target_pairs={{0,1},{1,2},{2,3},{3,0},{4,5},{5,6},{6,7},{7,4},{8,9},{9,10},{10,1... | collective-permute-start | bytes 172040 | tf_op jit(solution)/shard_map/ppermute | solution.py:618
  4.6 12.4 %collective-permute-start.1 = (f32[7,1,8,128]{3,2,1,0:T(8,128)}, f32[7,1,8,128]{3,2,1,0:T(8,128)S(1)}, u32[]{:S(2)}, u32[]{:S(2)}) collective-permute-start(f32[7,1,8,128]{3,2,1,0:T(8,128)} %get-tuple-element.18), channel_id=1, source_target_pairs={{1,0},{2,1},{3,2},{0,3},{5,4},{6,5},{7,6},{4,7},{9,8},{10,9},{11,1... | collective-permute-start | bytes 86024 | tf_op jit(solution)/shard_map/ppermute | solution.py:618
  5.3 21.3 %all-to-all-start = ((s32[64,1,128]{2,1,0:T(1,128)}), s32[64,1,128]{2,1,0:T(1,128)S(1)}, u32[]{:S(2)}, u32[]{:S(2)}) async-start(s32[64,1,128]{2,1,0:T(1,128)} %bitcast.39), calls=%async_computation | async-start | bytes 65536 | tf_op jit(solution)/shard_map/all_to_all | solution.py:650
  17.0 1.7 %copy-start.5 = (f32[27,2048]{1,0:T(8,128)S(1)}, f32[27,2048]{1,0:T(8,128)}, u32[]{:S(2)}) copy-start(f32[27,2048]{1,0:T(8,128)} %master.1) | copy-start | bytes 663556
  17.1 1.7 %copy-start.6 = (bf16[32,256]{1,0:T(8,128)(2,1)S(1)}, bf16[32,256]{1,0:T(8,128)(2,1)}, u32[]{:S(2)}) copy-start(bf16[32,256]{1,0:T(8,128)(2,1)} %constant.20.clone.fixed) | copy-start | bytes 49156
  17.1 11.5 %collective-permute-start.2 = (f32[336,128]{1,0:T(8,128)S(1)}, f32[336,128]{1,0:T(8,128)S(1)}, u32[]{:S(2)}, u32[]{:S(2)}) collective-permute-start(f32[336,128]{1,0:T(8,128)S(1)} %get-tuple-element.19), channel_id=1, source_target_pairs={{0,4},{4,8},{8,12},{12,0},{1,5},{5,9},{9,13},{13,1},{2,6},{6,10},{... | collective-permute-start | bytes 516104 | tf_op jit(solution)/shard_map/ppermute | solution.py:618
  19.0 9.6 %collective-permute-start.3 = (f32[168,128]{1,0:T(8,128)S(1)}, f32[168,128]{1,0:T(8,128)S(1)}, u32[]{:S(2)}, u32[]{:S(2)}) collective-permute-start(f32[168,128]{1,0:T(8,128)S(1)} %get-tuple-element.20), channel_id=1, source_target_pairs={{4,0},{8,4},{12,8},{0,12},{5,1},{9,5},{13,9},{1,13},{6,2},{10,6},{... | collective-permute-start | bytes 258056 | tf_op jit(solution)/shard_map/ppermute | solution.py:618
  28.9 5.9 %collective-permute-start.4 = (f32[16,128]{1,0:T(8,128)S(1)}, f32[16,128]{1,0:T(8,128)S(1)}, u32[]{:S(2)}, u32[]{:S(2)}) collective-permute-start(f32[16,128]{1,0:T(8,128)S(1)} %get-tuple-element.26), channel_id=1, source_target_pairs={{16,0},{32,16},{48,32},{64,48},{80,64},{96,80},{112,96},{128,112},... | collective-permute-start | bytes 24584 | tf_op jit(solution)/shard_map/ppermute | solution.py:618
  29.0 5.8 %copy-start.8 = (f32[3,16,8,128]{3,2,1,0:T(8,128)S(1)}, f32[3,16,8,128]{3,2,1,0:T(8,128)}, u32[]{:S(2)}) copy-start(f32[3,16,8,128]{3,2,1,0:T(8,128)} %param.17) | copy-start | bytes 589828
  29.0 5.8 %copy-start.9 = (f32[81,81]{1,0:T(8,128)S(1)}, f32[81,81]{1,0:T(8,128)}, u32[]{:S(2)}) copy-start(f32[81,81]{1,0:T(8,128)} %stiffness.1) | copy-start | bytes 78736
  29.0 5.8 %copy-start.10 = (bf16[144,640]{1,0:T(8,128)(2,1)S(1)}, bf16[144,640]{1,0:T(8,128)(2,1)}, u32[]{:S(2)}) copy-start(bf16[144,640]{1,0:T(8,128)(2,1)} %constant.22.clone.fixed) | copy-start | bytes 552964
  29.0 19.7 %all-to-all-start.1 = ((f32[64,8,128]{2,1,0:T(8,128)}), f32[64,8,128]{2,1,0:T(8,128)S(1)}, u32[]{:S(2)}, u32[]{:S(2)}) async-start(f32[64,8,128]{2,1,0:T(8,128)} %get-tuple-element.22), calls=%async_computation.1 | async-start | bytes 524288 | tf_op jit(solution)/shard_map/all_to_all | solution.py:669
  34.9 5.5 %copy-start.3 = (bf16[384,768]{1,0:T(8,128)(2,1)S(1)}, bf16[384,768]{1,0:T(8,128)(2,1)}, u32[]{:S(2)}) copy-start(bf16[384,768]{1,0:T(8,128)(2,1)} %constant.21.clone.fixed) | copy-start | bytes 1769476
  34.9 5.5 %copy-start.7 = (s32[16,128]{1,0:T(8,128)S(1)}, s32[16,128]{1,0:T(8,128)}, u32[]{:S(2)}) copy-start(s32[16,128]{1,0:T(8,128)} %get-tuple-element.23.codes) | copy-start | bytes 24580
  39.7 4.3 %collective-permute-start.5 = (f32[8,128]{1,0:T(8,128)S(1)}, f32[8,128]{1,0:T(8,128)S(1)}, u32[]{:S(2)}, u32[]{:S(2)}) collective-permute-start(f32[8,128]{1,0:T(8,128)S(1)} %get-tuple-element.27), channel_id=1, source_target_pairs={{0,16},{16,32},{32,48},{48,64},{64,80},{80,96},{96,112},{112,128},... | collective-permute-start | bytes 12296 | tf_op jit(solution)/shard_map/ppermute | solution.py:618
  40.4 8.3 %copy-start.4 = (bf16[224,576]{1,0:T(8,128)(2,1)S(1)}, bf16[224,576]{1,0:T(8,128)(2,1)}, u32[]{:S(2)}) copy-start(bf16[224,576]{1,0:T(8,128)(2,1)} %constant.23.clone.fixed) | copy-start | bytes 774148

commit v5 on v4

--- a/solution.py
+++ b/solution.py
@@ -21,6 +21,7 @@
 YPITCH = TILE
 ZPITCH = YE * TILE
 NODE_ROWS = ZE * ZPITCH
+Y_UP, Y_DOWN = 272, 144
 BLOCK = 9 * TILE
 GROUPS = ("gx", "gy")
 GROUP = 14
@@ -275,7 +276,7 @@
         for c in range(comps):
             n = first + c
             for out, h, y in ((y_up, 0, YN - 2), (y_up, 1, YN - 1), (y_down, 0, 0)):
-                at = (n * (2 if out is y_up else 1) + h) * 24
+                at = (n * (2 if out is y_up else 1) + h) * ZE
                 out[pl.ds(at, ZN), :] = field[pl.ds(c * ZN * YN + y, ZN, stride=YN), :]
                 out[pl.ds(at + 16, 8), :] = jnp.zeros((8, 128), F32)
                 out[pl.ds(at + 16, 1), :] = z_low[pl.ds((n * 2) * YN + y, 1), :]
@@ -283,8 +284,10 @@
                 out[pl.ds(at + 18, 1), :] = z_high[pl.ds(n * YN + y, 1), :]
 
 
-def table_kernel(master, fixed, table):
-    table[...] = mm3((fixed[:, 0:27], fixed[:, 128:155]), split(master[...]))
+def table_kernel(master, fixed, table, ninth):
+    full = mm3((fixed[:, 0:27], fixed[:, 128:155]), split(master[...]))
+    table[...] = full[0:24]
+    ninth[...] = jnp.concatenate([full[24:28, 0 : ROWS // 2], full[24:28, ROWS // 2 :]], axis=0)
 
 
 def stiffness_pair(stiffness, fixed):
@@ -296,7 +299,7 @@
     return high + fixed[:, 0:144], low + fixed[:, 256:400]
 
 
-def gather_kernel(ids, table, reply):
+def gather_kernel(ids, table, ninth, reply):
     numbers = jnp.maximum(compact(ids[...]) - 1, 0)
     found = []
     for c in range(CHUNKS):
@@ -304,12 +307,17 @@
         inside = number & 127
         outside = lax.shift_right_logical(number, 7)
         parts = []
-        for f in range(4):
+        for f in range(3):
             total = pick_lanes(table[pl.ds(f * 8, 8), 0:128], inside)
             for k in range(1, ROWS // 128):
                 piece = pick_lanes(table[pl.ds(f * 8, 8), k * 128 : (k + 1) * 128], inside)
                 total = jnp.where(outside == k, piece, total)
             parts.append(total)
+        total = pick_lanes(ninth[:, 0:128], inside)
+        for k in range(1, ROWS // 256):
+            piece = pick_lanes(ninth[:, k * 128 : (k + 1) * 128], inside)
+            total = jnp.where((outside & 7) == k, piece, total)
+        parts.append(jnp.where(outside < 8, total, pltpu.roll(total, 4, 0)))
         found.append(parts)
     for c, tiles in enumerate(swap_groups(found)):
         for g in range(4):
@@ -326,8 +334,8 @@
         return z_high[pl.ds(n * YN, YN), :]
     h, zb = divmod(s - 19, 3)
     if h < 2:
-        return y_low[pl.ds((n * 2 + h) * 24 + zb * 8, 8), :]
-    return y_high[pl.ds(n * 24 + zb * 8, 8), :]
+        return y_low[pl.ds((n * 2 + h) * ZE + zb * 8, 8), :]
+    return y_high[pl.ds(n * ZE + zb * 8, 8), :]
 
 
 def edge_kernel(u, v, m, z_low, z_high, y_low, y_high, reply_in, x_down, reply_out):
@@ -649,18 +657,20 @@
     z_high = ring(z_down, "gz", False).reshape(7 * YN, XN)
     ids = lax.all_to_all(request, GROUPS, split_axis=0, concat_axis=0, tiled=True)
 
-    (table,) = call(table_kernel, [((32, ROWS), F32)], n=2)(master_record, jnp.asarray(table_constants()))
+    table, ninth = call(table_kernel, [((24, ROWS), F32), ((8, ROWS // 2), F32)], n=2)(
+        master_record, jnp.asarray(table_constants())
+    )
     kin, selector = call(
         slot_kernel, [((CHUNKS, 56, 128), F32), ((OWNERS * CAP, FACES), BF16)],
         scratch=[pltpu.VMEM((56, 256), F32)], smem=(4,), n=5,
     )(u, v, codes, jnp.asarray(slot_constants()), pair_count)
-    y_up, y_down = call(side_kernel, [((7 * 2 * 24, XN), F32), ((7 * 24, XN), F32)], n=5)(
+    y_up, y_down = call(side_kernel, [((Y_UP, XN), F32), ((Y_DOWN, XN), F32)], n=5)(
         u, v, m, z_low, z_high
     )
     y_low = ring(y_up, "gy", True)
     y_high = ring(y_down, "gy", False)
 
-    (reply,) = call(gather_kernel, [((OWNERS, 8, 128), F32)], n=2, flops=5 << 28)(ids, table)
+    (reply,) = call(gather_kernel, [((OWNERS, 8, 128), F32)], n=3, flops=1 << 30)(ids, table, ninth)
     x_down, reply = call(
         edge_kernel, [((16, 128), F32), ((OWNERS, 8, 128), F32)], n=8, free=(7,), free_out=(1,),
         input_output_aliases={7: 1},

time: 51.5 us -> 51.3 us (level)
  no operation moved by 1% of the time
where the time goes in v5:
time: 51.3 us; the launch traced here: 50.4 us
  starting transfers between devices  23.6 us (46%)
  waiting for transfers between devices  12.6 us (25%)
  Pallas kernels  12.5 us (24%)
  between operations  1.5 us (3%)
    all_to_all x1, starting transfers between devices, local(): lax.all_to_all(request, GROUPS, split_axis=0, concat_axis=0, tiled=True)  11.7 us
    ppermute x6, starting transfers between devices, ring(): return lax.ppermute(values, axis, pairs)  6.17 us
    all_to_all x1, starting transfers between devices, local(): lax.all_to_all(reply, GROUPS, split_axis=0, concat_axis=0, tiled=True)  5.8 us
    all_to_all x1, waiting for transfers between devices, local(): lax.all_to_all(request, GROUPS, split_axis=0, concat_axis=0, tiled=True)  5.46 us
    pallas_call x1, Pallas kernels, local(): call(element_kernel, [((3 * ZN * YN, XN), F32), ((3 * ZN * YN, XN), F32),...  4.79 us
    all_to_all x1, waiting for transfers between devices, local(): lax.all_to_all(reply, GROUPS, split_axis=0, concat_axis=0, tiled=True)  4.7 us
    ppermute x6, waiting for transfers between devices, ring(): return lax.ppermute(values, axis, pairs)  2.45 us
    pallas_call x1, Pallas kernels, local(): call(request_kernel, [((OWNERS, 128), I32), ((CHUNKS, 128), I32), ((7, 2,...  2.23 us
  transfers between devices with their start and end apart: 8, of which 3 were waited for; matrix products, arithmetic and copies ran while one was open for 0% of the time, Pallas kernels for 16%

profile of v5, /device:TPU:8, one launch (start us, length us, event | category | flops | bytes accessed | tf_op | source)
XLA Modules:
  0.0 50.4 jit_solution(3885730452529912363)
XLA Ops:
  0.6 0.0 copy-start
  0.6 0.0 copy-start.1
  0.7 2.2 %shard_map.149 = (s32[64,128]{1,0:T(8,128)}, s32[16,128]{1,0:T(8,128)}, f32[7,2,8,128]{3,2,1,0:T(8,128)}, f32[7,1,8,128]{3,2,1,0:T(8,128)}) custom-call(s32[8,128]{1,0:T(8,128)} %bitcast.40, s32[8,128]{1,0:T(8,128)} %bitcast.41, s32[8,128]{1,0:T(8,128)} %bitcast.42, f32[3,16,8,128]{3,2,1,0:T(8,128)} %u.1, f32[3,16,8,128]{3,2,1,0:T(8,128)} %v.1, f32[16,8,128]{2,1,0:T(8,128)} %m.1), custom_call_target="tpu_custom_call" | custom-call | tf_op jit(solution)/shard_map/pallas_call | solution.py:644
  2.9 0.0 copy-start.2
  2.9 1.7 %collective-permute-start = (f32[7,2,8,128]{3,2,1,0:T(8,128)}, f32[7,2,8,128]{3,2,1,0:T(8,128)S(1)}, u32[]{:S(2)}, u32[]{:S(2)}) collective-permute-start(f32[7,2,8,128]{3,2,1,0:T(8,128)} %get-tuple-element.19), channel_id=1, source_target_pairs={{0,1},{1,2},{2,3},{3,0},{4,5},{5,6},{6,7},{7,4},{8,9},{9,10},{10,1... | collective-permute-start | bytes 172040 | tf_op jit(solution)/shard_map/ppermute | solution.py:626
  4.6 0.7 %collective-permute-start.1 = (f32[7,1,8,128]{3,2,1,0:T(8,128)}, f32[7,1,8,128]{3,2,1,0:T(8,128)S(1)}, u32[]{:S(2)}, u32[]{:S(2)}) collective-permute-start(f32[7,1,8,128]{3,2,1,0:T(8,128)} %get-tuple-element.20), channel_id=1, source_target_pairs={{1,0},{2,1},{3,2},{0,3},{5,4},{6,5},{7,6},{4,7},{9,8},{10,9},{11,1... | collective-permute-start | bytes 86024 | tf_op jit(solution)/shard_map/ppermute | solution.py:626
  5.3 11.7 %all-to-all-start = ((s32[64,1,128]{2,1,0:T(1,128)}), s32[64,1,128]{2,1,0:T(1,128)S(1)}, u32[]{:S(2)}, u32[]{:S(2)}) async-start(s32[64,1,128]{2,1,0:T(1,128)} %bitcast.39), calls=%async_computation | async-start | bytes 65536 | tf_op jit(solution)/shard_map/all_to_all | solution.py:658
  16.9 0.0 collective-permute-done.1
  17.0 0.0 collective-permute-done
  17.0 0.0 copy-done
  17.0 0.0 copy-done.1
  17.0 0.0 copy-done.2
  17.0 0.0 copy-start.5
  17.0 0.1 shard_map.150
  17.1 0.0 copy-start.6
  17.1 1.6 %collective-permute-start.2 = (f32[272,128]{1,0:T(8,128)S(1)}, f32[272,128]{1,0:T(8,128)S(1)}, u32[]{:S(2)}, u32[]{:S(2)}) collective-permute-start(f32[272,128]{1,0:T(8,128)S(1)} %get-tuple-element.21), channel_id=1, source_target_pairs={{0,4},{4,8},{8,12},{12,0},{1,5},{5,9},{9,13},{13,1},{2,6},{6,10},{... | collective-permute-start | bytes 417800 | tf_op jit(solution)/shard_map/ppermute | solution.py:626
  18.7 0.0 copy-done.5
  18.7 0.0 copy-done.6
  18.7 0.2 shard_map.151
  19.0 2.1 %collective-permute-start.3 = (f32[144,128]{1,0:T(8,128)S(1)}, f32[144,128]{1,0:T(8,128)S(1)}, u32[]{:S(2)}, u32[]{:S(2)}) collective-permute-start(f32[144,128]{1,0:T(8,128)S(1)} %get-tuple-element.22), channel_id=1, source_target_pairs={{4,0},{8,4},{12,8},{0,12},{5,1},{9,5},{13,9},{1,13},{6,2},{10,6},{... | collective-permute-start | bytes 221192 | tf_op jit(solution)/shard_map/ppermute | solution.py:626
  21.1 5.5 %all-to-all-done = s32[64,1,128]{2,1,0:T(1,128)S(1)} async-done(((s32[64,1,128]{2,1,0:T(1,128)}), s32[64,1,128]{2,1,0:T(1,128)S(1)}, u32[]{:S(2)}, u32[]{:S(2)}) %all-to-all-start) | async-done | bytes 32800 | tf_op jit(solution)/shard_map/all_to_all | solution.py:658
  26.5 1.9 %shard_map.152.reply_in = f32[64,8,128]{2,1,0:T(8,128)} custom-call(s32[64,128]{1,0:T(8,128)S(1)} %bitcast.37, f32[24,2048]{1,0:T(8,128)S(1)} %get-tuple-element.24.table, f32[8,1024]{1,0:T(8,128)S(1)} %get-tuple-element.25.ninth), custom_call_target="tpu_custom_call" | custom-call | flops 1073741824 | tf_op jit(solution)/shard_map/pallas_call | solution.py:673
  28.5 0.0 collective-permute-done.3.y_high
  28.5 0.0 collective-permute-done.2.y_low
  28.5 0.3 shard_map.153
  28.8 0.0 collective-permute-start.4
  28.8 0.1 pad_add_fusion.edges
  28.9 0.0 copy-start.8
  28.9 0.0 copy-start.9
  28.9 0.0 copy-start.10
  28.9 5.8 %all-to-all-start.1 = ((f32[64,8,128]{2,1,0:T(8,128)}), f32[64,8,128]{2,1,0:T(8,128)S(1)}, u32[]{:S(2)}, u32[]{:S(2)}) async-start(f32[64,8,128]{2,1,0:T(8,128)} %get-tuple-element.26), calls=%async_computation.1 | async-start | bytes 524288 | tf_op jit(solution)/shard_map/all_to_all | solution.py:679
  34.7 0.0 collective-permute-done.4.x_high
  34.7 0.0 copy-done.8
  34.7 0.0 copy-done.9
  34.7 0.0 copy-done.10
  34.7 0.0 copy-start.3
  34.7 0.0 copy-start.7
  34.8 4.8 %shard_map.155 = (f32[384,128]{1,0:T(8,128)S(1)}, f32[384,128]{1,0:T(8,128)S(1)}, f32[8,128]{1,0:T(8,128)S(1)}) custom-call(s32[3]{0:T(128)S(1)} %pad_add_fusion.edges, f32[384,128]{1,0:T(8,128)S(1)} %bitcast.20, f32[384,128]{1,0:T(8,128)S(1)} %bitcast.25, f32[128,128]{1,0:T(8,128)S(1)} %bitcast.30, f32[384,128]{1,0:T(8,128)S(1)} %bitcast.38, ...), custom_call_target="tpu_custom_call" | custom-call | flops 8589934592 | tf_op jit(solution)/shard_map/pallas_call | solution.py:682
  39.5 0.1 collective-permute-start.5
  40.3 0.0 copy-done.3
  40.3 0.0 copy-done.7
  40.3 0.0 copy-start.4
  40.3 1.1 %shard_map.154 = (f32[16,56,128]{2,1,0:T(8,128)S(1)}, bf16[2048,192]{1,0:T(8,128)(2,1)S(1)}) custom-call(f32[384,128]{1,0:T(8,128)S(1)} %bitcast.21, f32[384,128]{1,0:T(8,128)S(1)} %bitcast.26, s32[16,128]{1,0:T(8,128)S(1)} %copy-done.7, bf16[384,768]{1,0:T(8,128)(2,1)S(1)} %copy-done.3, s32[1]{0:T(128)S(6)} %copy.19.count), custom_call_target="tpu_custom_call" | custom-call | tf_op jit(solution)/shard_map/pallas_call | solution.py:663
  41.4 2.4 %collective-permute-done.5.left = f32[8,128]{1,0:T(8,128)S(1)} collective-permute-done((f32[8,128]{1,0:T(8,128)S(1)}, f32[8,128]{1,0:T(8,128)S(1)}, u32[]{:S(2)}, u32[]{:S(2)}) %collective-permute-start.5) | collective-permute-done | bytes 4128 | tf_op jit(solution)/shard_map/ppermute | solution.py:626
  43.9 4.7 %all-to-all-done.1.replies = f32[64,8,128]{2,1,0:T(8,128)S(1)} async-done(((f32[64,8,128]{2,1,0:T(8,128)}), f32[64,8,128]{2,1,0:T(8,128)S(1)}, u32[]{:S(2)}, u32[]{:S(2)}) %all-to-all-start.1) | async-done | bytes 262176 | tf_op jit(solution)/shard_map/all_to_all | solution.py:679
  48.6 0.0 copy-done.4
  48.6 1.8 %shard_map.156 = (f32[384,128]{1,0:T(8,128)}, f32[384,128]{1,0:T(8,128)}) custom-call(f32[64,8,128]{2,1,0:T(8,128)S(1)} %all-to-all-done.1.replies, f32[16,56,128]{2,1,0:T(8,128)S(1)} %get-tuple-element.28.kin, bf16[2048,192]{1,0:T(8,128)(2,1)S(1)} %get-tuple-element.29.selector, bf16[224,576]{1,0:T(8,128)(2,1)S(1)} %copy-done.4, ...), custom_call_target="tpu_custom_call" | custom-call | flops 1048576 | tf_op jit(solution)/shard_map/pallas_call | solution.py:697
Async XLA Ops:
  0.6 16.3 %copy-start = (f32[3,16,8,128]{3,2,1,0:T(8,128)S(1)}, f32[3,16,8,128]{3,2,1,0:T(8,128)}, u32[]{:S(2)}) copy-start(f32[3,16,8,128]{3,2,1,0:T(8,128)} %u.1) | copy-start | bytes 589828
  0.6 16.3 %copy-start.1 = (f32[3,16,8,128]{3,2,1,0:T(8,128)S(1)}, f32[3,16,8,128]{3,2,1,0:T(8,128)}, u32[]{:S(2)}) copy-start(f32[3,16,8,128]{3,2,1,0:T(8,128)} %v.1) | copy-start | bytes 589828
  2.9 14.1 %copy-start.2 = (f32[16,8,128]{2,1,0:T(8,128)S(1)}, f32[16,8,128]{2,1,0:T(8,128)}, u32[]{:S(2)}) copy-start(f32[16,8,128]{2,1,0:T(8,128)} %m.1) | copy-start | bytes 196612
  2.9 14.1 %collective-permute-start = (f32[7,2,8,128]{3,2,1,0:T(8,128)}, f32[7,2,8,128]{3,2,1,0:T(8,128)S(1)}, u32[]{:S(2)}, u32[]{:S(2)}) collective-permute-start(f32[7,2,8,128]{3,2,1,0:T(8,128)} %get-tuple-element.19), channel_id=1, source_target_pairs={{0,1},{1,2},{2,3},{3,0},{4,5},{5,6},{6,7},{7,4},{8,9},{9,10},{10,1... | collective-permute-start | bytes 172040 | tf_op jit(solution)/shard_map/ppermute | solution.py:626
  4.6 12.4 %collective-permute-start.1 = (f32[7,1,8,128]{3,2,1,0:T(8,128)}, f32[7,1,8,128]{3,2,1,0:T(8,128)S(1)}, u32[]{:S(2)}, u32[]{:S(2)}) collective-permute-start(f32[7,1,8,128]{3,2,1,0:T(8,128)} %get-tuple-element.20), channel_id=1, source_target_pairs={{1,0},{2,1},{3,2},{0,3},{5,4},{6,5},{7,6},{4,7},{9,8},{10,9},{11,1... | collective-permute-start | bytes 86024 | tf_op jit(solution)/shard_map/ppermute | solution.py:626
  5.3 21.3 %all-to-all-start = ((s32[64,1,128]{2,1,0:T(1,128)}), s32[64,1,128]{2,1,0:T(1,128)S(1)}, u32[]{:S(2)}, u32[]{:S(2)}) async-start(s32[64,1,128]{2,1,0:T(1,128)} %bitcast.39), calls=%async_computation | async-start | bytes 65536 | tf_op jit(solution)/shard_map/all_to_all | solution.py:658
  17.0 1.7 %copy-start.5 = (f32[27,2048]{1,0:T(8,128)S(1)}, f32[27,2048]{1,0:T(8,128)}, u32[]{:S(2)}) copy-start(f32[27,2048]{1,0:T(8,128)} %master.1) | copy-start | bytes 663556
  17.1 1.7 %copy-start.6 = (bf16[32,256]{1,0:T(8,128)(2,1)S(1)}, bf16[32,256]{1,0:T(8,128)(2,1)}, u32[]{:S(2)}) copy-start(bf16[32,256]{1,0:T(8,128)(2,1)} %constant.20.clone.fixed) | copy-start | bytes 49156
  17.1 11.4 %collective-permute-start.2 = (f32[272,128]{1,0:T(8,128)S(1)}, f32[272,128]{1,0:T(8,128)S(1)}, u32[]{:S(2)}, u32[]{:S(2)}) collective-permute-start(f32[272,128]{1,0:T(8,128)S(1)} %get-tuple-element.21), channel_id=1, source_target_pairs={{0,4},{4,8},{8,12},{12,0},{1,5},{5,9},{9,13},{13,1},{2,6},{6,10},{... | collective-permute-start | bytes 417800 | tf_op jit(solution)/shard_map/ppermute | solution.py:626
  19.0 9.5 %collective-permute-start.3 = (f32[144,128]{1,0:T(8,128)S(1)}, f32[144,128]{1,0:T(8,128)S(1)}, u32[]{:S(2)}, u32[]{:S(2)}) collective-permute-start(f32[144,128]{1,0:T(8,128)S(1)} %get-tuple-element.22), channel_id=1, source_target_pairs={{4,0},{8,4},{12,8},{0,12},{5,1},{9,5},{13,9},{1,13},{6,2},{10,6},{... | collective-permute-start | bytes 221192 | tf_op jit(solution)/shard_map/ppermute | solution.py:626
  28.8 5.9 %collective-permute-start.4 = (f32[16,128]{1,0:T(8,128)S(1)}, f32[16,128]{1,0:T(8,128)S(1)}, u32[]{:S(2)}, u32[]{:S(2)}) collective-permute-start(f32[16,128]{1,0:T(8,128)S(1)} %get-tuple-element.30), channel_id=1, source_target_pairs={{16,0},{32,16},{48,32},{64,48},{80,64},{96,80},{112,96},{128,112},... | collective-permute-start | bytes 24584 | tf_op jit(solution)/shard_map/ppermute | solution.py:626
  28.9 5.8 %copy-start.8 = (f32[3,16,8,128]{3,2,1,0:T(8,128)S(1)}, f32[3,16,8,128]{3,2,1,0:T(8,128)}, u32[]{:S(2)}) copy-start(f32[3,16,8,128]{3,2,1,0:T(8,128)} %param.17) | copy-start | bytes 589828
  28.9 5.8 %copy-start.9 = (f32[81,81]{1,0:T(8,128)S(1)}, f32[81,81]{1,0:T(8,128)}, u32[]{:S(2)}) copy-start(f32[81,81]{1,0:T(8,128)} %stiffness.1) | copy-start | bytes 78736
  28.9 5.8 %copy-start.10 = (bf16[144,640]{1,0:T(8,128)(2,1)S(1)}, bf16[144,640]{1,0:T(8,128)(2,1)}, u32[]{:S(2)}) copy-start(bf16[144,640]{1,0:T(8,128)(2,1)} %constant.22.clone.fixed) | copy-start | bytes 552964
  28.9 19.7 %all-to-all-start.1 = ((f32[64,8,128]{2,1,0:T(8,128)}), f32[64,8,128]{2,1,0:T(8,128)S(1)}, u32[]{:S(2)}, u32[]{:S(2)}) async-start(f32[64,8,128]{2,1,0:T(8,128)} %get-tuple-element.26), calls=%async_computation.1 | async-start | bytes 524288 | tf_op jit(solution)/shard_map/all_to_all | solution.py:679
  34.7 5.5 %copy-start.3 = (bf16[384,768]{1,0:T(8,128)(2,1)S(1)}, bf16[384,768]{1,0:T(8,128)(2,1)}, u32[]{:S(2)}) copy-start(bf16[384,768]{1,0:T(8,128)(2,1)} %constant.21.clone.fixed) | copy-start | bytes 1769476
  34.7 5.5 %copy-start.7 = (s32[16,128]{1,0:T(8,128)S(1)}, s32[16,128]{1,0:T(8,128)}, u32[]{:S(2)}) copy-start(s32[16,128]{1,0:T(8,128)} %get-tuple-element.27.codes) | copy-start | bytes 24580
  39.5 4.3 %collective-permute-start.5 = (f32[8,128]{1,0:T(8,128)S(1)}, f32[8,128]{1,0:T(8,128)S(1)}, u32[]{:S(2)}, u32[]{:S(2)}) collective-permute-start(f32[8,128]{1,0:T(8,128)S(1)} %get-tuple-element.31), channel_id=1, source_target_pairs={{0,16},{16,32},{32,48},{48,64},{64,80},{80,96},{96,112},{112,128},... | collective-permute-start | bytes 12296 | tf_op jit(solution)/shard_map/ppermute | solution.py:626
  40.3 8.3 %copy-start.4 = (bf16[224,576]{1,0:T(8,128)(2,1)S(1)}, bf16[224,576]{1,0:T(8,128)(2,1)}, u32[]{:S(2)}) copy-start(bf16[224,576]{1,0:T(8,128)(2,1)} %constant.23.clone.fixed) | copy-start | bytes 774148
